TPU v7x, 256 devices: a whole 4x4x8 slice. The times are simulated.
256 devices in a mesh: row: 16 (over z_hi, y, core), col: 16 (over z_lo, x).
Axes of the slice: x: 4, y: 4, z: 8 (z_hi: 2, z_lo: 4; z = z_hi * 4 + z_lo), core: 2. Of those that a mesh axis runs over, the one named last changes fastest.
Arguments:
- objects: float32 [2, 2, 4096, 4096], P(None, None, 'row', 'col'), may hold values from -5 to 5
- probe: float32 [2, 256, 256], replicated, may hold values from -6 to 6
- prev_partial: float32 [16, 16, 2, 256, 256], P('row', 'col'), may hold values from -6 to 6
- offsets: int32 [16, 16, 1, 2], P('row', 'col'), may hold values from 0 to 128
- counts: int32 [16, 16], P('row', 'col'), may hold values from 0 to 1
- amplitudes: float32 [16, 16, 1, 256, 256], P('row', 'col'), may hold values from 1 to 2.5
Outputs:
- new_objects: float32 [2, 2, 4096, 4096], P(None, None, 'row', 'col')
- new_probe: float32 [2, 256, 256], replicated
- new_partial: float32 [16, 16, 2, 256, 256], P('row', 'col')
All inputs are finite; a program needn't handle non-finite values.
Results may differ from a plain program's by a relative error of at most 0.0003.
Values sent between devices are 32-bit elements; how exact they have to be, the bound alone decides.
No kernel may reach another device: no remote copies, remote signals or barrier semaphores. Data moves between devices by JAX's collectives and lax.ppermute only.
A program may use at most 64 MiB of HBM per device.

v0:
```python
import math

import jax
import jax.numpy as jnp
import ml_dtypes
import numpy as np
from jax import lax
from jax.experimental import pallas as pl
from jax.experimental.pallas import tpu as pltpu
from jax.sharding import Mesh
from jax.sharding import PartitionSpec as P

WIN = 256
HALO = 64
TILE = 256
SIDE = TILE + 2 * HALO
AXES = ("row_0", "row_1", "row_2", "col_0", "col_1")
ROW = ("row_0", "row_1", "row_2")
COL = ("col_0", "col_1")
PLANE = ("row_1", "col_1", "row_2")
DEPTH = ("row_0", "col_0")

OBJ_RATE = 0.1
PROBE_RATE = 0.3
VMEM = pl.BlockSpec(memory_space=pltpu.VMEM)
SMEM = pl.BlockSpec(memory_space=pltpu.SMEM)
PARAMS = pltpu.CompilerParams(vmem_limit_bytes=48 * 1024 * 1024)


def operator_parts():
    index = np.arange(WIN)
    angle = 2.0 * np.pi * (index[:, None] * index[None, :] % WIN) / WIN
    forward = np.exp(-1j * angle) / math.sqrt(WIN)
    freq = np.where(index < WIN // 2, index, index - WIN)
    shift = np.exp(1j * np.pi * freq.astype(np.float64) ** 2 / (4.0 * WIN))
    propagate = np.conj(forward) @ (shift[:, None] * forward)
    parts = []
    for matrix in (propagate, forward):
        matrix = (matrix + matrix.T) / 2
        halves = []
        for part in (matrix.real, matrix.imag, -matrix.imag):
            high = part.astype(np.float32).astype(ml_dtypes.bfloat16)
            low = (part - high.astype(np.float64)).astype(np.float32)
            halves.append((high, low.astype(ml_dtypes.bfloat16)))
        parts += [high for high, _ in halves] + [low for _, low in halves]
    return np.stack(parts)


def halves_of(value):
    high = value.astype(jnp.bfloat16)
    low = (value - high.astype(jnp.float32)).astype(jnp.bfloat16)
    return high, low


def dot(left, right):
    return jnp.dot(left, right, preferred_element_type=jnp.float32)


def three(left, right):
    (left_high, left_low), (right_high, right_low) = left, right
    return dot(left_high, right_high) + (dot(left_low, right_high) + dot(left_high, right_low))


def sandwich(mats, which, real_part, imag_part):
    def block(rows):
        return jnp.concatenate(
            [jnp.concatenate([mats[6 * which + k] for k in row], axis=1) for row in rows], axis=0
        )

    right = tuple(block(((3 * h, 3 * h + 1), (3 * h + 2, 3 * h))) for h in range(2))
    left = tuple(block(((3 * h, 3 * h + 2), (3 * h + 1, 3 * h))) for h in range(2))
    inner = three(halves_of(jnp.concatenate([real_part, imag_part], axis=1)), right)
    stacked = jnp.concatenate([inner[:, :WIN], inner[:, WIN:]], axis=0)
    outer = three(left, halves_of(stacked))
    return outer[:WIN], outer[WIN:]


def first_half(shape):
    return lax.broadcasted_iota(jnp.int32, shape, len(shape) - 1) < HALO


def pack_columns(objects, north, south, west_send, east_send):
    for s in range(2):
        for src, start, size in ((north, 0, HALO), (objects, HALO, TILE), (south, HALO + TILE, HALO)):
            rows = pl.ds(start, size)
            real, imag = src[s, 0], src[s, 1]
            keep = first_half((size, 2 * HALO))
            west_send[s, rows] = jnp.where(keep, real[:, :128], pltpu.roll(imag[:, :128], HALO, 1))
            east_send[s, rows] = jnp.where(keep, pltpu.roll(real[:, 128:], HALO, 1), imag[:, 128:])


def gradient(
    offset, count, objects, north, south, west, east, probe, amp, mats,
    center, north_out, south_out, west_out, east_out, probe_out, ext, grad,
):
    keep = first_half((SIDE, 2 * HALO))
    for s in range(2):
        for k in range(2):
            ext[2 * s + k, :HALO, :TILE] = north[s, k]
            ext[2 * s + k, HALO : HALO + TILE, :TILE] = objects[s, k]
            ext[2 * s + k, HALO + TILE : SIDE, :TILE] = south[s, k]
        ext[2 * s, :SIDE, TILE:] = jnp.where(keep, east[s], pltpu.roll(west[s], HALO, 1))
        ext[2 * s + 1, :SIDE, TILE:] = jnp.where(keep, pltpu.roll(east[s], HALO, 1), west[s])
    grad[...] = jnp.zeros_like(grad)
    top, left = offset[0], offset[1]
    into = lax.rem(SIDE + HALO - left, SIDE)
    back = lax.rem(SIDE - HALO + left, SIDE)

    low = lax.rem(top, 8)
    rows = pl.ds(pl.multiple_of(top - low, 8), WIN + 8)

    def window(k):
        wide = pltpu.roll(ext[k, rows, :], into, 1)[:, :WIN]
        return pltpu.roll(wide, lax.rem(WIN + 8 - low, WIN + 8), 0)[:WIN]

    def place(k, value):
        tall = jnp.concatenate([value, jnp.zeros((8, WIN), jnp.float32)], axis=0)
        tall = pltpu.roll(tall, low, 0)
        wide = jnp.concatenate([tall, jnp.zeros((WIN + 8, SIDE - WIN), jnp.float32)], axis=1)
        grad[k, rows, :] = pltpu.roll(wide, back, 1)

    a_re, a_im, b_re, b_im = (window(k) for k in range(4))
    p_re, p_im = probe[0], probe[1]
    u_re = p_re * a_re - p_im * a_im
    u_im = p_re * a_im + p_im * a_re
    v_re, v_im = sandwich(mats, 0, u_re, u_im)
    e_re = v_re * b_re - v_im * b_im
    e_im = v_re * b_im + v_im * b_re
    w_re, w_im = sandwich(mats, 1, e_re, e_im)
    size = jnp.sqrt(w_re * w_re + w_im * w_im + 1.0)
    live = jnp.where(count[0] > 0, 2.0, 0.0)
    slope = live * (size - amp[...]) / size
    e_re, e_im = sandwich(mats, 1, slope * w_re, -slope * w_im)
    place(2, -OBJ_RATE * (e_re * v_re - e_im * v_im))
    place(3, OBJ_RATE * (e_re * v_im + e_im * v_re))
    v_re = e_re * b_re - e_im * b_im
    v_im = e_re * b_im + e_im * b_re
    u_re, u_im = sandwich(mats, 0, v_re, v_im)
    place(0, -OBJ_RATE * (u_re * p_re - u_im * p_im))
    place(1, OBJ_RATE * (u_re * p_im + u_im * p_re))
    probe_out[0] = u_re * a_re - u_im * a_im
    probe_out[1] = -(u_re * a_im + u_im * a_re)
    for s in range(2):
        for k in range(2):
            north_out[s, k] = grad[2 * s + k, :HALO, :TILE]
            south_out[s, k] = grad[2 * s + k, HALO + TILE : SIDE, :TILE]
            center[s, k] = objects[s, k] + grad[2 * s + k, HALO : HALO + TILE, :TILE]
        real, imag = grad[2 * s, :SIDE, TILE:], grad[2 * s + 1, :SIDE, TILE:]
        east_out[s] = jnp.where(keep, real, pltpu.roll(imag, HALO, 1))
        west_out[s] = jnp.where(keep, pltpu.roll(real, HALO, 1), imag)


def edge_columns(west, east, s, start, size):
    keep = first_half((size, 2 * HALO))
    w, e = west[s, pl.ds(start, size)], east[s, pl.ds(start, size)]
    zero = jnp.zeros_like(w)
    wr, er = pltpu.roll(w, HALO, 1), pltpu.roll(e, HALO, 1)
    return (
        (jnp.where(keep, w, zero), jnp.where(keep, zero, er)),
        (jnp.where(keep, wr, zero), jnp.where(keep, zero, e)),
    )


def add_margins(north, south, west, east, north_send, south_send):
    for s in range(2):
        for src, dst, start in ((north, north_send, 0), (south, south_send, HALO + TILE)):
            for k, (first, last) in enumerate(edge_columns(west, east, s, start, HALO)):
                dst[s, k, :, :128] = src[s, k, :, :128] + first
                dst[s, k, :, 128:] = src[s, k, :, 128:] + last


def finish(center, west, east, north, south, new_objects):
    for s in range(2):
        for k, (first, last) in enumerate(edge_columns(west, east, s, HALO, TILE)):
            for cols, edge in ((slice(0, 128), first), (slice(128, 256), last)):
                value = center[s, k, :, cols] + edge
                new_objects[s, k, :HALO, cols] = value[:HALO] + north[s, k, :, cols]
                new_objects[s, k, HALO : TILE - HALO, cols] = value[HALO : TILE - HALO]
                new_objects[s, k, TILE - HALO :, cols] = value[TILE - HALO :] + south[s, k, :, cols]


def call(body, outs, *args, specs=None, scratch=(), flops=0, name=None):
    moved = sum(math.prod(o) * 4 for o in outs)
    return pl.pallas_call(
        body,
        out_shape=[jax.ShapeDtypeStruct(o, jnp.float32) for o in outs],
        in_specs=specs or [VMEM] * len(args),
        out_specs=[VMEM] * len(outs),
        scratch_shapes=scratch,
        compiler_params=PARAMS,
        cost_estimate=pl.CostEstimate(flops=flops, bytes_accessed=2 * moved, transcendentals=0),
        name=name,
    )(*args)


def shifted(value, axis, by):
    peers = lax.axis_size(axis)
    return lax.ppermute(value, axis, [(i, i + by) for i in range(peers) if 0 <= i + by < peers])


def swap(value, axes):
    return lax.all_to_all(value, axes, 0, 0, tiled=True)


def probe_sum(partial):
    plane, depth = lax.axis_size(PLANE), lax.axis_size(DEPTH)
    rows = 2 * WIN // plane
    part = jnp.sum(swap(partial.reshape(plane, rows, WIN), PLANE), axis=0)
    part = jnp.sum(swap(jnp.broadcast_to(part, (depth, rows, WIN)), DEPTH), axis=0)
    return swap(jnp.broadcast_to(part, (plane, rows, WIN)), PLANE).reshape(2, WIN, WIN)


def shards(objects, probe, prev_partial, offsets, counts, amplitudes):
    strip, column = (2, 2, HALO, TILE), (2, SIDE, 2 * HALO)
    tile = (2, 2, TILE, TILE)
    north = shifted(objects[:, :, TILE - HALO :, :], ROW, 1)
    south = shifted(objects[:, :, :HALO, :], ROW, -1)
    west_send, east_send = call(pack_columns, [column] * 2, objects, north, south, name="pack")
    west = shifted(east_send, COL, 1)
    east = shifted(west_send, COL, -1)
    center, north_part, south_part, west_part, east_part, partial = call(
        gradient,
        [tile, strip, strip, column, column, (2, WIN, WIN)],
        offsets.reshape(2), counts.reshape(1), objects, north, south, west, east, probe,
        amplitudes.reshape(WIN, WIN), jnp.asarray(operator_parts()),
        specs=[SMEM, SMEM] + [VMEM] * 8,
        scratch=[pltpu.VMEM((4, SIDE + 8, SIDE), jnp.float32)] * 2,
        flops=96 * 2 * WIN**3,
        name="gradient",
    )
    from_west = shifted(east_part, COL, 1)
    from_east = shifted(west_part, COL, -1)
    north_send, south_send = call(
        add_margins, [strip] * 2, north_part, south_part, from_west, from_east, name="margins"
    )
    from_north = shifted(south_send, ROW, 1)
    from_south = shifted(north_send, ROW, -1)
    (new_objects,) = call(
        finish, [tile], center, from_west, from_east, from_north, from_south, name="finish"
    )
    rate = PROBE_RATE / math.sqrt(lax.axis_size(ROW) * lax.axis_size(COL))
    new_probe = probe - rate * probe_sum(prev_partial)
    return (new_objects, new_probe, partial[None, None])


def solution(mesh):
    split = Mesh(mesh.devices.reshape(2, 4, 2, 4, 4), AXES)
    return jax.shard_map(
        shards,
        mesh=split,
        in_specs=(
            P(None, None, ROW, COL),
            P(),
            P(ROW, COL, None, None, None),
            P(ROW, COL, None, None),
            P(ROW, COL),
            P(ROW, COL, None, None, None),
        ),
        out_specs=(P(None, None, ROW, COL), P(), P(ROW, COL, None, None, None)),
        check_vma=False,
    )
```

profile of v0, /device:TPU:31, one launch (start us, length us, event | category | flops | bytes accessed | tf_op | source)
XLA Modules:
  0.0 111.1 jit_solution(3472519803613994789)
XLA Ops:
  0.6 0.0 copy-start
  0.6 7.8 %all-to-all-start = ((f32[32,16,256]{2,1,0:T(8,128)}), f32[32,16,256]{2,1,0:T(8,128)}, u32[]{:S(2)}, u32[]{:S(2)}) async-start(f32[32,16,256]{2,1,0:T(8,128)} %bitcast.12), calls=%async_computation | async-start | bytes 1048576 | tf_op jit(solution)/shard_map/all_to_all | solution.py:202
  8.5 1.1 fusion
  9.6 9.0 %collective-permute-start = (f32[2,2,64,256]{3,2,1,0:T(8,128)S(1)}, f32[2,2,64,256]{3,2,1,0:T(8,128)S(1)}, u32[]{:S(2)}, u32[]{:S(2)}) collective-permute-start(f32[2,2,64,256]{3,2,1,0:T(8,128)S(1)} %get-tuple-element.24), channel_id=1, source_target_pairs={{0,16},{16,32},{32,48},{48,64},{64,80},{80,96},{96,112},{112,128},... | collective-permute-start | bytes 786440 | tf_op jit(solution)/shard_map/ppermute | solution.py:198
  18.5 1.9 %collective-permute-start.1 = (f32[2,2,64,256]{3,2,1,0:T(8,128)S(1)}, f32[2,2,64,256]{3,2,1,0:T(8,128)S(1)}, u32[]{:S(2)}, u32[]{:S(2)}) collective-permute-start(f32[2,2,64,256]{3,2,1,0:T(8,128)S(1)} %get-tuple-element.23), channel_id=1, source_target_pairs={{16,0},{32,16},{48,32},{64,48},{80,64},{96,80},{112,96},{128,112},... | collective-permute-start | bytes 786440 | tf_op jit(solution)/shard_map/ppermute | solution.py:198
  20.5 1.4 %collective-permute-done.north = f32[2,2,64,256]{3,2,1,0:T(8,128)S(1)} collective-permute-done((f32[2,2,64,256]{3,2,1,0:T(8,128)S(1)}, f32[2,2,64,256]{3,2,1,0:T(8,128)S(1)}, u32[]{:S(2)}, u32[]{:S(2)}) %collective-permute-start) | collective-permute-done | bytes 262176 | tf_op jit(solution)/shard_map/ppermute | solution.py:198
  21.8 10.5 %collective-permute-done.1.south = f32[2,2,64,256]{3,2,1,0:T(8,128)S(1)} collective-permute-done((f32[2,2,64,256]{3,2,1,0:T(8,128)S(1)}, f32[2,2,64,256]{3,2,1,0:T(8,128)S(1)}, u32[]{:S(2)}, u32[]{:S(2)}) %collective-permute-start.1) | collective-permute-done | bytes 262176 | tf_op jit(solution)/shard_map/ppermute | solution.py:198
  32.3 0.0 copy-done
  32.4 1.0 pack.1
  33.4 0.0 copy-start.1
  33.4 0.0 copy-start.5
  33.4 5.3 %collective-permute-start.2 = (f32[2,384,128]{2,1,0:T(8,128)}, f32[2,384,128]{2,1,0:T(8,128)S(1)}, u32[]{:S(2)}, u32[]{:S(2)}) collective-permute-start(f32[2,384,128]{2,1,0:T(8,128)} %get-tuple-element.13), channel_id=1, source_target_pairs={{0,1},{1,2},{2,3},{3,4},{4,5},{5,6},{6,7},{7,8},{8,9},{9,10},{10,1... | collective-permute-start | bytes 1179656 | tf_op jit(solution)/shard_map/ppermute | solution.py:198
  38.7 1.9 %collective-permute-start.3 = (f32[2,384,128]{2,1,0:T(8,128)S(1)}, f32[2,384,128]{2,1,0:T(8,128)S(1)}, u32[]{:S(2)}, u32[]{:S(2)}) collective-permute-start(f32[2,384,128]{2,1,0:T(8,128)S(1)} %get-tuple-element.14), channel_id=1, source_target_pairs={{1,0},{2,1},{3,2},{4,3},{5,4},{6,5},{7,6},{8,7},{9,8},{10,9},{11,1... | collective-permute-start | bytes 1179656 | tf_op jit(solution)/shard_map/ppermute | solution.py:198
  40.6 0.0 all-to-all-done
  40.6 1.1 reduce_sum.18
  41.7 0.7 broadcast_in_dim.9
  42.4 5.1 %all-to-all-start.1 = ((f32[8,16,256]{2,1,0:T(8,128)}), f32[8,16,256]{2,1,0:T(8,128)S(1)}, u32[]{:S(2)}, u32[]{:S(2)}) async-start(f32[8,16,256]{2,1,0:T(8,128)} %broadcast_in_dim.9), calls=%async_computation.1 | async-start | bytes 262144 | tf_op jit(solution)/shard_map/all_to_all | solution.py:202
  48.1 7.3 %all-to-all-done.1 = f32[8,16,256]{2,1,0:T(8,128)S(1)} async-done(((f32[8,16,256]{2,1,0:T(8,128)}), f32[8,16,256]{2,1,0:T(8,128)S(1)}, u32[]{:S(2)}, u32[]{:S(2)}) %all-to-all-start.1) | async-done | bytes 131104 | tf_op jit(solution)/shard_map/all_to_all | solution.py:202
  55.4 0.9 broadcast_in_dim.10
  56.3 6.7 %all-to-all-start.2 = ((f32[32,16,256]{2,1,0:T(8,128)}), f32[32,16,256]{2,1,0:T(8,128)}, u32[]{:S(2)}, u32[]{:S(2)}) async-start(f32[32,16,256]{2,1,0:T(8,128)} %broadcast_in_dim.10), calls=%async_computation.2 | async-start | bytes 1048576 | tf_op jit(solution)/shard_map/all_to_all | solution.py:202
  63.0 0.0 collective-permute-done.2.west
  63.0 0.0 collective-permute-done.3.east
  63.0 0.0 copy-start.2
  63.0 0.7 copy-done.2
  63.7 0.0 copy-done.1
  63.7 0.0 copy-done.5
  63.7 0.0 copy-start.3
  63.7 1.0 copy-done.3
  64.7 0.0 copy-start.4
  64.7 0.9 copy-done.4
  65.7 10.1 %gradient.1 = (f32[2,2,256,256]{3,2,1,0:T(8,128)S(1)}, f32[2,2,64,256]{3,2,1,0:T(8,128)S(1)}, f32[2,2,64,256]{3,2,1,0:T(8,128)S(1)}, f32[2,384,128]{2,1,0:T(8,12...) custom-call(s32[2]{0:T(128)S(1)} %bitcast.10, s32[1]{0:T(128)} %bitcast.8.count, ...), custom_call_target="tpu_custom_call" | custom-call | flops 3221225472 | bytes 5767168 | tf_op jit(solution)/shard_map/gradient/pallas_call | solution.py:184
  75.8 2.2 %collective-permute-start.4 = (f32[2,384,128]{2,1,0:T(8,128)S(1)}, f32[2,384,128]{2,1,0:T(8,128)S(1)}, u32[]{:S(2)}, u32[]{:S(2)}) collective-permute-start(f32[2,384,128]{2,1,0:T(8,128)S(1)} %get-tuple-element.16), channel_id=1, source_target_pairs={{0,1},{1,2},{2,3},{3,4},{4,5},{5,6},{6,7},{7,8},{8,9},{9,10},{10,1... | collective-permute-start | bytes 1179656 | tf_op jit(solution)/shard_map/ppermute | solution.py:198
  78.0 3.1 %collective-permute-start.5 = (f32[2,384,128]{2,1,0:T(8,128)S(1)}, f32[2,384,128]{2,1,0:T(8,128)S(1)}, u32[]{:S(2)}, u32[]{:S(2)}) collective-permute-start(f32[2,384,128]{2,1,0:T(8,128)S(1)} %get-tuple-element.17), channel_id=1, source_target_pairs={{1,0},{2,1},{3,2},{4,3},{5,4},{6,5},{7,6},{8,7},{9,8},{10,9},{11,1... | collective-permute-start | bytes 1179656 | tf_op jit(solution)/shard_map/ppermute | solution.py:198
  81.1 6.9 %collective-permute-done.4.west = f32[2,384,128]{2,1,0:T(8,128)S(1)} collective-permute-done((f32[2,384,128]{2,1,0:T(8,128)S(1)}, f32[2,384,128]{2,1,0:T(8,128)S(1)}, u32[]{:S(2)}, u32[]{:S(2)}) %collective-permute-start.4) | collective-permute-done | bytes 393248 | tf_op jit(solution)/shard_map/ppermute | solution.py:198
  88.0 4.0 %collective-permute-done.5.east = f32[2,384,128]{2,1,0:T(8,128)S(1)} collective-permute-done((f32[2,384,128]{2,1,0:T(8,128)S(1)}, f32[2,384,128]{2,1,0:T(8,128)S(1)}, u32[]{:S(2)}, u32[]{:S(2)}) %collective-permute-start.5) | collective-permute-done | bytes 393248 | tf_op jit(solution)/shard_map/ppermute | solution.py:198
  92.0 0.1 margins.1
  92.2 3.9 %collective-permute-start.6 = (f32[2,2,64,256]{3,2,1,0:T(8,128)S(1)}, f32[2,2,64,256]{3,2,1,0:T(8,128)S(1)}, u32[]{:S(2)}, u32[]{:S(2)}) collective-permute-start(f32[2,2,64,256]{3,2,1,0:T(8,128)S(1)} %get-tuple-element.20), channel_id=1, source_target_pairs={{0,16},{16,32},{32,48},{48,64},{64,80},{80,96},{96,112},{112,128},... | collective-permute-start | bytes 786440 | tf_op jit(solution)/shard_map/ppermute | solution.py:198
  96.1 1.9 %collective-permute-start.7 = (f32[2,2,64,256]{3,2,1,0:T(8,128)S(1)}, f32[2,2,64,256]{3,2,1,0:T(8,128)S(1)}, u32[]{:S(2)}, u32[]{:S(2)}) collective-permute-start(f32[2,2,64,256]{3,2,1,0:T(8,128)S(1)} %get-tuple-element.21), channel_id=1, source_target_pairs={{16,0},{32,16},{48,32},{64,48},{80,64},{96,80},{112,96},{128,112},... | collective-permute-start | bytes 786440 | tf_op jit(solution)/shard_map/ppermute | solution.py:198
  98.0 0.0 all-to-all-done.2
  98.0 1.1 broadcast_multiply_fusion
  99.1 0.9 bitcast_subtract_fusion
  100.0 0.0 collective-permute-done.6.north
  100.0 9.9 %collective-permute-done.7.south = f32[2,2,64,256]{3,2,1,0:T(8,128)S(1)} collective-permute-done((f32[2,2,64,256]{3,2,1,0:T(8,128)S(1)}, f32[2,2,64,256]{3,2,1,0:T(8,128)S(1)}, u32[]{:S(2)}, u32[]{:S(2)}) %collective-permute-start.7) | collective-permute-done | bytes 262176 | tf_op jit(solution)/shard_map/ppermute | solution.py:198
  109.9 1.2 %finish.1 = f32[2,2,256,256]{3,2,1,0:T(8,128)} custom-call(f32[2,2,256,256]{3,2,1,0:T(8,128)S(1)} %get-tuple-element.15.center, f32[2,384,128]{2,1,0:T(8,128)S(1)} %collective-permute-done.4.west, f32[2,384,128]{2,1,0:T(8,128)S(1)} %collective-permute-done.5.east, f32[2,2,64,256]{3,2,1,0:T(8,128)S(1)} %collective-permute-done.6.north, ...), custom_call_target="tpu_custom_call" | custom-call | bytes 2097152 | tf_op jit(solution)/shard_map/finish/pallas_call | solution.py:184
  (1 shorter events, 0.0 us)
Async XLA Ops:
  0.6 31.7 %copy-start = (f32[2,2,256,256]{3,2,1,0:T(8,128)S(1)}, f32[2,2,256,256]{3,2,1,0:T(8,128)}, u32[]{:S(2)}) copy-start(f32[2,2,256,256]{3,2,1,0:T(8,128)} %objects.3) | copy-start | bytes 3145732
  0.6 40.0 %all-to-all-start = ((f32[32,16,256]{2,1,0:T(8,128)}), f32[32,16,256]{2,1,0:T(8,128)}, u32[]{:S(2)}, u32[]{:S(2)}) async-start(f32[32,16,256]{2,1,0:T(8,128)} %bitcast.12), calls=%async_computation | async-start | bytes 1048576 | tf_op jit(solution)/shard_map/all_to_all | solution.py:202
  9.6 12.3 %collective-permute-start = (f32[2,2,64,256]{3,2,1,0:T(8,128)S(1)}, f32[2,2,64,256]{3,2,1,0:T(8,128)S(1)}, u32[]{:S(2)}, u32[]{:S(2)}) collective-permute-start(f32[2,2,64,256]{3,2,1,0:T(8,128)S(1)} %get-tuple-element.24), channel_id=1, source_target_pairs={{0,16},{16,32},{32,48},{48,64},{64,80},{80,96},{96,112},{112,128},... | collective-permute-start | bytes 786440 | tf_op jit(solution)/shard_map/ppermute | solution.py:198
  18.5 13.8 %collective-permute-start.1 = (f32[2,2,64,256]{3,2,1,0:T(8,128)S(1)}, f32[2,2,64,256]{3,2,1,0:T(8,128)S(1)}, u32[]{:S(2)}, u32[]{:S(2)}) collective-permute-start(f32[2,2,64,256]{3,2,1,0:T(8,128)S(1)} %get-tuple-element.23), channel_id=1, source_target_pairs={{16,0},{32,16},{48,32},{64,48},{80,64},{96,80},{112,96},{128,112},... | collective-permute-start | bytes 786440 | tf_op jit(solution)/shard_map/ppermute | solution.py:198
  33.4 30.4 %copy-start.1 = (f32[2,256,256]{2,1,0:T(8,128)S(1)}, f32[2,256,256]{2,1,0:T(8,128)}, u32[]{:S(2)}) copy-start(f32[2,256,256]{2,1,0:T(8,128)} %probe.1) | copy-start | bytes 1572868
  33.4 30.4 %copy-start.5 = (s32[1,1,1,2]{3,2,1,0:T(1,128)S(1)}, s32[1,1,1,2]{3,2,1,0:T(1,128)}, u32[]{:S(2)}) copy-start(s32[1,1,1,2]{3,2,1,0:T(1,128)} %param.10) | copy-start | bytes 28
  33.4 29.6 %collective-permute-start.2 = (f32[2,384,128]{2,1,0:T(8,128)}, f32[2,384,128]{2,1,0:T(8,128)S(1)}, u32[]{:S(2)}, u32[]{:S(2)}) collective-permute-start(f32[2,384,128]{2,1,0:T(8,128)} %get-tuple-element.13), channel_id=1, source_target_pairs={{0,1},{1,2},{2,3},{3,4},{4,5},{5,6},{6,7},{7,8},{8,9},{9,10},{10,1... | collective-permute-start | bytes 1179656 | tf_op jit(solution)/shard_map/ppermute | solution.py:198
  38.7 24.3 %collective-permute-start.3 = (f32[2,384,128]{2,1,0:T(8,128)S(1)}, f32[2,384,128]{2,1,0:T(8,128)S(1)}, u32[]{:S(2)}, u32[]{:S(2)}) collective-permute-start(f32[2,384,128]{2,1,0:T(8,128)S(1)} %get-tuple-element.14), channel_id=1, source_target_pairs={{1,0},{2,1},{3,2},{4,3},{5,4},{6,5},{7,6},{8,7},{9,8},{10,9},{11,1... | collective-permute-start | bytes 1179656 | tf_op jit(solution)/shard_map/ppermute | solution.py:198
  42.4 13.0 %all-to-all-start.1 = ((f32[8,16,256]{2,1,0:T(8,128)}), f32[8,16,256]{2,1,0:T(8,128)S(1)}, u32[]{:S(2)}, u32[]{:S(2)}) async-start(f32[8,16,256]{2,1,0:T(8,128)} %broadcast_in_dim.9), calls=%async_computation.1 | async-start | bytes 262144 | tf_op jit(solution)/shard_map/all_to_all | solution.py:202
  56.3 41.7 %all-to-all-start.2 = ((f32[32,16,256]{2,1,0:T(8,128)}), f32[32,16,256]{2,1,0:T(8,128)}, u32[]{:S(2)}, u32[]{:S(2)}) async-start(f32[32,16,256]{2,1,0:T(8,128)} %broadcast_in_dim.10), calls=%async_computation.2 | async-start | bytes 1048576 | tf_op jit(solution)/shard_map/all_to_all | solution.py:202
  63.0 0.7 copy-start.2
  63.7 1.0 copy-start.3
  64.7 0.9 copy-start.4
  75.8 12.2 %collective-permute-start.4 = (f32[2,384,128]{2,1,0:T(8,128)S(1)}, f32[2,384,128]{2,1,0:T(8,128)S(1)}, u32[]{:S(2)}, u32[]{:S(2)}) collective-permute-start(f32[2,384,128]{2,1,0:T(8,128)S(1)} %get-tuple-element.16), channel_id=1, source_target_pairs={{0,1},{1,2},{2,3},{3,4},{4,5},{5,6},{6,7},{7,8},{8,9},{9,10},{10,1... | collective-permute-start | bytes 1179656 | tf_op jit(solution)/shard_map/ppermute | solution.py:198
  78.0 14.0 %collective-permute-start.5 = (f32[2,384,128]{2,1,0:T(8,128)S(1)}, f32[2,384,128]{2,1,0:T(8,128)S(1)}, u32[]{:S(2)}, u32[]{:S(2)}) collective-permute-start(f32[2,384,128]{2,1,0:T(8,128)S(1)} %get-tuple-element.17), channel_id=1, source_target_pairs={{1,0},{2,1},{3,2},{4,3},{5,4},{6,5},{7,6},{8,7},{9,8},{10,9},{11,1... | collective-permute-start | bytes 1179656 | tf_op jit(solution)/shard_map/ppermute | solution.py:198
  92.2 7.8 %collective-permute-start.6 = (f32[2,2,64,256]{3,2,1,0:T(8,128)S(1)}, f32[2,2,64,256]{3,2,1,0:T(8,128)S(1)}, u32[]{:S(2)}, u32[]{:S(2)}) collective-permute-start(f32[2,2,64,256]{3,2,1,0:T(8,128)S(1)} %get-tuple-element.20), channel_id=1, source_target_pairs={{0,16},{16,32},{32,48},{48,64},{64,80},{80,96},{96,112},{112,128},... | collective-permute-start | bytes 786440 | tf_op jit(solution)/shard_map/ppermute | solution.py:198
  96.1 13.8 %collective-permute-start.7 = (f32[2,2,64,256]{3,2,1,0:T(8,128)S(1)}, f32[2,2,64,256]{3,2,1,0:T(8,128)S(1)}, u32[]{:S(2)}, u32[]{:S(2)}) collective-permute-start(f32[2,2,64,256]{3,2,1,0:T(8,128)S(1)} %get-tuple-element.21), channel_id=1, source_target_pairs={{16,0},{32,16},{48,32},{64,48},{80,64},{96,80},{112,96},{128,112},... | collective-permute-start | bytes 786440 | tf_op jit(solution)/shard_map/ppermute | solution.py:198
where the time goes:
time: 113 us; the launch traced here: 111 us
  starting transfers between devices  48.8 us (43%)
  waiting for transfers between devices  40 us (35%)
  Pallas kernels  12.5 us (11%)
  local copies, waits for them, and re-layouts  5.3 us (5%)
  other arithmetic  3.06 us (3%)
  between operations  1.44 us (1%)
    ppermute x8, waiting for transfers between devices, shifted(): lax.ppermute(value, axis, [(i, i + by) for i in range(peers) if 0 <= i +...  32.7 us
    ppermute x8, starting transfers between devices, shifted(): lax.ppermute(value, axis, [(i, i + by) for i in range(peers) if 0 <= i +...  29.2 us
    all_to_all x3, starting transfers between devices, swap(): return lax.all_to_all(value, axes, 0, 0, tiled=True)  19.6 us
    pallas_call x4, Pallas kernels, call(): pl.pallas_call(body, out_shape=[jax.ShapeDtypeStruct(o, jnp.float32) for...  12.5 us
    all_to_all x3, waiting for transfers between devices, swap(): return lax.all_to_all(value, axes, 0, 0, tiled=True)  7.28 us
    unnamed x12, local copies, waits for them, and re-layouts  2.7 us
  transfers between devices with their start and end apart: 11, of which 6 were waited for; matrix products, arithmetic and copies ran while one was open for 5% of the time, Pallas kernels for 10%

commit v1 on v0

v1 whole, which is shorter than its diff:
```python
import math

import jax
import jax.numpy as jnp
import ml_dtypes
import numpy as np
from jax import lax
from jax.experimental import pallas as pl
from jax.experimental.pallas import tpu as pltpu
from jax.sharding import Mesh
from jax.sharding import PartitionSpec as P

WIN = 256
HALO = 64
TILE = 256
SIDE = TILE + 2 * HALO
AXES = ("row_0", "row_1", "row_2", "col_0", "col_1")
ROW = ("row_0", "row_1", "row_2")
COL = ("col_0", "col_1")
PLANE = ("row_1", "col_1")
PAIR = "row_2"
DEPTH = ("row_0", "col_0")

OBJ_RATE = 0.1
PROBE_RATE = 0.3
VMEM = pl.BlockSpec(memory_space=pltpu.VMEM)
HBM = pl.BlockSpec(memory_space=pltpu.HBM)
ANY = pl.BlockSpec(memory_space=pl.ANY)
SMEM = pl.BlockSpec(memory_space=pltpu.SMEM)
MIB = 1024 * 1024


def operator_parts():
    index = np.arange(WIN)
    angle = 2.0 * np.pi * (index[:, None] * index[None, :] % WIN) / WIN
    forward = np.exp(-1j * angle) / math.sqrt(WIN)
    freq = np.where(index < WIN // 2, index, index - WIN)
    shift = np.exp(1j * np.pi * freq.astype(np.float64) ** 2 / (4.0 * WIN))
    propagate = np.conj(forward) @ (shift[:, None] * forward)
    parts = []
    for matrix in (propagate, forward):
        matrix = (matrix + matrix.T) / 2
        halves = []
        for part in (matrix.real, matrix.imag, -matrix.imag):
            high = part.astype(np.float32).astype(ml_dtypes.bfloat16)
            low = (part - high.astype(np.float64)).astype(np.float32)
            halves.append((high, low.astype(ml_dtypes.bfloat16)))
        parts += [high for high, _ in halves] + [low for _, low in halves]
    return np.stack(parts)


def halves_of(value):
    high = value.astype(jnp.bfloat16)
    low = (value - high.astype(jnp.float32)).astype(jnp.bfloat16)
    return high, low


def dot(left, right):
    return jnp.dot(left, right, preferred_element_type=jnp.float32)


def three(left, right):
    (left_high, left_low), (right_high, right_low) = left, right
    return dot(left_high, right_high) + (dot(left_low, right_high) + dot(left_high, right_low))


def sandwich(mats, which, real_part, imag_part):
    def block(rows):
        return jnp.concatenate(
            [jnp.concatenate([mats[6 * which + k] for k in row], axis=1) for row in rows], axis=0
        )

    right = tuple(block(((3 * h, 3 * h + 1), (3 * h + 2, 3 * h))) for h in range(2))
    left = tuple(block(((3 * h, 3 * h + 2), (3 * h + 1, 3 * h))) for h in range(2))
    inner = three(halves_of(jnp.concatenate([real_part, imag_part], axis=1)), right)
    stacked = jnp.concatenate([inner[:, :WIN], inner[:, WIN:]], axis=0)
    outer = three(left, halves_of(stacked))
    return outer[:WIN], outer[WIN:]


def first_half(shape):
    return lax.broadcasted_iota(jnp.int32, shape, len(shape) - 1) < HALO


def side_columns(src, s, size):
    real, imag = src[s, 0], src[s, 1]
    keep = first_half((size, 2 * HALO))
    return (
        jnp.where(keep, real[:, :128], pltpu.roll(imag[:, :128], HALO, 1)),
        jnp.where(keep, pltpu.roll(real[:, 128:], HALO, 1), imag[:, 128:]),
    )


def either(flag, when_even, when_odd):
    return jnp.where(flag == 0, when_even, when_odd)


def pack_sides(facts, objects, row_a, row_b, col_a, col_b):
    row_odd, col_odd = facts[3], facts[4]
    for s in range(2):
        top, bottom = objects[s, :, :HALO], objects[s, :, TILE - HALO :]
        row_a[s] = either(row_odd, bottom, top)
        row_b[s] = either(row_odd, top, bottom)
        first, last = side_columns(objects, s, TILE)
        col_a[s] = either(col_odd, last, first)
        col_b[s] = either(col_odd, first, last)


def pack_corners(facts, row_a, row_b, col_a, col_b):
    row_odd, col_odd = facts[3], facts[4]
    for s in range(2):
        a, b = side_columns(row_a, s, HALO), side_columns(row_b, s, HALO)
        for rows, when_even, when_odd in ((pl.ds(0, HALO), b, a), (pl.ds(HALO, HALO), a, b)):
            first, last = (either(row_odd, *pair) for pair in zip(when_even, when_odd))
            col_a[s, rows] = either(col_odd, last, first)
            col_b[s, rows] = either(col_odd, first, last)


def gradient(
    facts, objects, row_a, row_b, col_a, col_b, corners_a, corners_b, probe, amp, mats,
    center_out, north_out, south_out, col_a_out, col_b_out, corners_a_out, corners_b_out, probe_out,
    ext, grad, sides, sides_out, probe_in, amp_in, mats_in, probe_grad, arrive, leave,
):
    row_odd, col_odd = facts[3], facts[4]
    across = pl.ds(0, TILE)
    middle, upper, lower = pl.ds(HALO, TILE), pl.ds(0, HALO), pl.ds(HALO + TILE, HALO)

    def beyond(odd):
        return pl.ds(pl.multiple_of((1 - odd) * (HALO + TILE), HALO), HALO)

    incoming = [
        (objects, ext.at[:, :, middle, across]),
        (row_a, ext.at[:, :, beyond(row_odd), across]),
        (row_b, ext.at[:, :, beyond(1 - row_odd), across]),
        (probe, probe_in),
        (mats, mats_in),
        (amp, amp_in),
    ]
    outgoing = [(probe_grad, probe_out)]
    for side, col, corner, col_out, corner_out in (
        (1 - col_odd, col_a, corners_a, col_a_out, corners_a_out),
        (col_odd, col_b, corners_b, col_b_out, corners_b_out),
    ):
        for rows, src, dst in (
            (upper, corner.at[:, upper], corner_out.at[:, upper]),
            (middle, col, col_out),
            (lower, corner.at[:, pl.ds(HALO, HALO)], corner_out.at[:, pl.ds(HALO, HALO)]),
        ):
            incoming.insert(3, (src, sides.at[side, :, rows]))
            outgoing.append((sides_out.at[side, :, rows], dst))
    outgoing += [
        (grad.at[:, :, upper, across], north_out),
        (grad.at[:, :, lower, across], south_out),
        (ext.at[:, :, middle, across], center_out),
    ]
    coming = [pltpu.make_async_copy(*pair, arrive.at[i]) for i, pair in enumerate(incoming)]
    going = [pltpu.make_async_copy(*pair, leave.at[i]) for i, pair in enumerate(outgoing)]
    for copy in coming:
        copy.start()
    grad[...] = jnp.zeros_like(grad)
    for copy in coming[:-3]:
        copy.wait()
    keep = first_half((SIDE, 2 * HALO))
    for s in range(2):
        w, e = sides[0, s], sides[1, s]
        ext[s, 0, :SIDE, TILE:] = jnp.where(keep, e, pltpu.roll(w, HALO, 1))
        ext[s, 1, :SIDE, TILE:] = jnp.where(keep, pltpu.roll(e, HALO, 1), w)
    top, left = facts[0], facts[1]
    into = lax.rem(SIDE + HALO - left, SIDE)
    back = lax.rem(SIDE - HALO + left, SIDE)
    low = lax.rem(top, 8)
    rows = pl.ds(pl.multiple_of(top - low, 8), WIN + 8)

    def window(s, k):
        wide = pltpu.roll(ext[s, k, rows, :], into, 1)[:, :WIN]
        return pltpu.roll(wide, lax.rem(WIN + 8 - low, WIN + 8), 0)[:WIN]

    def place(s, k, value):
        tall = jnp.concatenate([value, jnp.zeros((8, WIN), jnp.float32)], axis=0)
        tall = pltpu.roll(tall, low, 0)
        wide = jnp.concatenate([tall, jnp.zeros((WIN + 8, SIDE - WIN), jnp.float32)], axis=1)
        grad[s, k, rows, :] = pltpu.roll(wide, back, 1)

    a_re, a_im, b_re, b_im = window(0, 0), window(0, 1), window(1, 0), window(1, 1)
    coming[-3].wait()
    p_re, p_im = probe_in[0], probe_in[1]
    u_re = p_re * a_re - p_im * a_im
    u_im = p_re * a_im + p_im * a_re
    coming[-2].wait()
    v_re, v_im = sandwich(mats_in, 0, u_re, u_im)
    e_re = v_re * b_re - v_im * b_im
    e_im = v_re * b_im + v_im * b_re
    w_re, w_im = sandwich(mats_in, 1, e_re, e_im)
    coming[-1].wait()
    size = jnp.sqrt(w_re * w_re + w_im * w_im + 1.0)
    live = jnp.where(facts[2] > 0, 2.0, 0.0)
    slope = live * (size - amp_in[...]) / size
    e_re, e_im = sandwich(mats_in, 1, slope * w_re, -slope * w_im)
    place(1, 0, -OBJ_RATE * (e_re * v_re - e_im * v_im))
    place(1, 1, OBJ_RATE * (e_re * v_im + e_im * v_re))
    v_re = e_re * b_re - e_im * b_im
    v_im = e_re * b_im + e_im * b_re
    u_re, u_im = sandwich(mats_in, 0, v_re, v_im)
    place(0, 0, -OBJ_RATE * (u_re * p_re - u_im * p_im))
    place(0, 1, OBJ_RATE * (u_re * p_im + u_im * p_re))
    probe_grad[0] = u_re * a_re - u_im * a_im
    probe_grad[1] = -(u_re * a_im + u_im * a_re)
    for s in range(2):
        real, imag = grad[s, 0, :SIDE, TILE:], grad[s, 1, :SIDE, TILE:]
        sides_out[0, s] = jnp.where(keep, pltpu.roll(real, HALO, 1), imag)
        sides_out[1, s] = jnp.where(keep, real, pltpu.roll(imag, HALO, 1))
    for copy in going[:-1]:
        copy.start()
    for s in range(2):
        for k in range(2):
            ext[s, k, middle, :TILE] = ext[s, k, middle, :TILE] + grad[s, k, middle, :TILE]
    going[-1].start()
    for copy in going:
        copy.wait()


def edge_columns(col_odd, col_a, col_b, s, start, size):
    keep = first_half((size, 2 * HALO))
    a, b = col_a[s, pl.ds(start, size)], col_b[s, pl.ds(start, size)]
    w, e = either(col_odd, b, a), either(col_odd, a, b)
    zero = jnp.zeros_like(w)
    wr, er = pltpu.roll(w, HALO, 1), pltpu.roll(e, HALO, 1)
    return (
        (jnp.where(keep, w, zero), jnp.where(keep, zero, er)),
        (jnp.where(keep, wr, zero), jnp.where(keep, zero, e)),
    )


def add_margins(facts, north, south, corners_a, corners_b, row_a, row_b):
    row_odd, col_odd = facts[3], facts[4]
    for s in range(2):
        upper = edge_columns(col_odd, corners_a, corners_b, s, 0, HALO)
        lower = edge_columns(col_odd, corners_a, corners_b, s, HALO, HALO)
        for k in range(2):
            for half, cols in enumerate((slice(0, 128), slice(128, 256))):
                up = north[s, k, :, cols] + upper[k][half]
                down = south[s, k, :, cols] + lower[k][half]
                row_a[s, k, :, cols] = either(row_odd, down, up)
                row_b[s, k, :, cols] = either(row_odd, up, down)


def finish(facts, center, col_a, col_b, row_a, row_b, new_objects):
    row_odd, col_odd = facts[3], facts[4]
    for s in range(2):
        for k, edges in enumerate(edge_columns(col_odd, col_a, col_b, s, 0, TILE)):
            for cols, edge in zip((slice(0, 128), slice(128, 256)), edges):
                value = center[s, k, :, cols] + edge
                a, b = row_a[s, k, :, cols], row_b[s, k, :, cols]
                new_objects[s, k, :HALO, cols] = value[:HALO] + either(row_odd, b, a)
                new_objects[s, k, HALO : TILE - HALO, cols] = value[HALO : TILE - HALO]
                new_objects[s, k, TILE - HALO :, cols] = value[TILE - HALO :] + either(row_odd, a, b)


def call(body, outs, *args, specs=None, scratch=(), flops=0, limit=2, name=None):
    moved = sum(math.prod(o) * 4 for o in outs)
    return pl.pallas_call(
        body,
        out_shape=[jax.ShapeDtypeStruct(o, jnp.float32) for o in outs],
        in_specs=[SMEM] + (specs or [VMEM] * (len(args) - 1)),
        out_specs=[HBM if specs else VMEM] * len(outs),
        scratch_shapes=scratch,
        compiler_params=pltpu.CompilerParams(vmem_limit_bytes=limit * MIB),
        cost_estimate=pl.CostEstimate(flops=flops, bytes_accessed=2 * moved, transcendentals=0),
        name=name,
    )(*args)


def exchanged(value, axis, first):
    pairs = [(i, i + 1) for i in range(first, lax.axis_size(axis) - 1, 2)]
    return lax.ppermute(value, axis, pairs + [(j, i) for i, j in pairs])


def swap(value, axes):
    return lax.all_to_all(value, axes, 0, 0, tiled=True)


def after(value, *others):
    return lax.optimization_barrier((value, *others))[0]


def probe_sum(partial, *marks):
    plane, depth = lax.axis_size(PLANE), lax.axis_size(DEPTH)
    rows = WIN // plane
    core = lax.axis_index(PAIR)
    own, other = (lax.dynamic_index_in_dim(partial, k, 0, False) for k in (core, 1 - core))
    part = own + exchanged(after(other, marks[0]), PAIR, 0)
    part = swap(after(part, marks[1]).reshape(plane, rows, WIN), PLANE)
    part = jnp.sum(after(part, marks[2]), axis=0)
    part = swap(jnp.broadcast_to(part, (depth, rows, WIN)), DEPTH)
    part = jnp.sum(after(part, marks[3]), axis=0)
    own = swap(jnp.broadcast_to(part, (plane, rows, WIN)), PLANE).reshape(WIN, WIN)
    other = exchanged(own, PAIR, 0)
    return jnp.stack([either(core, own, other), either(core, other, own)])


def shards(objects, probe, prev_partial, offsets, counts, amplitudes):
    strip, column, corners = (2, 2, HALO, TILE), (2, TILE, 2 * HALO), (2, 2 * HALO, 2 * HALO)
    tile = (2, 2, TILE, TILE)
    facts = jnp.concatenate([
        offsets.reshape(2), counts.reshape(1),
        jnp.stack([lax.axis_index("row_2"), lax.axis_index("col_1") % 2]).astype(jnp.int32),
    ])
    row_a, row_b, col_a, col_b = call(pack_sides, [strip] * 2 + [column] * 2, facts, objects, name="pack_sides")
    row_b, row_a = exchanged(row_b, ROW, 1), exchanged(row_a, ROW, 0)
    col_b, col_a = exchanged(col_b, COL, 1), exchanged(col_a, COL, 0)
    side_mark = row_a
    sent_a, sent_b = call(pack_corners, [corners] * 2, facts, row_a, row_b, name="pack_corners")
    corners_b, corners_a = exchanged(sent_b, COL, 1), exchanged(sent_a, COL, 0)
    center, north, south, col_a_part, col_b_part, corners_a_part, corners_b_part, partial = call(
        gradient,
        [tile, strip, strip, column, column, corners, corners, (2, WIN, WIN)],
        facts, objects, row_a, row_b, col_a, col_b, corners_a, corners_b, probe,
        amplitudes.reshape(WIN, WIN), jnp.asarray(operator_parts()),
        specs=[ANY] * 3 + [HBM] * 7,
        scratch=[pltpu.VMEM((2, 2, SIDE + 8, SIDE), jnp.float32)] * 2
        + [pltpu.VMEM((2, 2, SIDE, 2 * HALO), jnp.float32)] * 2
        + [pltpu.VMEM((2, WIN, WIN), jnp.float32), pltpu.VMEM((WIN, WIN), jnp.float32)]
        + [pltpu.VMEM((12, WIN, WIN), jnp.bfloat16), pltpu.VMEM((2, WIN, WIN), jnp.float32)]
        + [pltpu.SemaphoreType.DMA((12,)), pltpu.SemaphoreType.DMA((10,))],
        flops=96 * 2 * WIN**3,
        limit=60,
        name="gradient",
    )
    corners_b, corners_a = exchanged(corners_b_part, COL, 1), exchanged(corners_a_part, COL, 0)
    corners_a, corners_b, col_a_part, col_b_part = lax.optimization_barrier(
        (corners_a, corners_b, col_a_part, col_b_part)
    )
    row_a, row_b = call(add_margins, [strip] * 2, facts, north, south, corners_a, corners_b, name="margins")
    row_b, row_a = exchanged(row_b, ROW, 1), exchanged(row_a, ROW, 0)
    col_b, col_a = exchanged(col_b_part, COL, 1), exchanged(col_a_part, COL, 0)
    (new_objects,) = call(finish, [tile], facts, center, col_a, col_b, row_a, row_b, name="finish")
    rate = PROBE_RATE / math.sqrt(lax.axis_size(ROW) * lax.axis_size(COL))
    total = probe_sum(prev_partial[0, 0], side_mark, side_mark, partial, corners_a)
    new_probe = probe - rate * total
    return (new_objects, new_probe, partial[None, None])


def solution(mesh):
    split = Mesh(mesh.devices.reshape(2, 4, 2, 4, 4), AXES)
    return jax.shard_map(
        shards,
        mesh=split,
        in_specs=(
            P(None, None, ROW, COL),
            P(),
            P(ROW, COL, None, None, None),
            P(ROW, COL, None, None),
            P(ROW, COL),
            P(ROW, COL, None, None, None),
        ),
        out_specs=(P(None, None, ROW, COL), P(), P(ROW, COL, None, None, None)),
        check_vma=False,
    )
```

time: 113 us -> 94.3 us (0.83)
  waiting for transfers between devices: 40 us -> 12.5 us
  starting transfers between devices: 48.8 us -> 55.8 us
  Pallas kernels: 12.5 us -> 15.7 us
    ppermute x8 -> x14, waiting for transfers between devices: 32.7 us -> 12.5 us  [exchanged(): return lax.ppermute(value, axis, pairs + [(j, i) for i, j in pairs])]
    ppermute x8 -> x14, starting transfers between devices: 29.2 us -> 38.2 us  [exchanged(): return lax.ppermute(value, axis, pairs + [(j, i) for i, j in pairs])]
    all_to_all x3, waiting for transfers between devices: 7.28 us -> 0.01 us  [swap(): return lax.all_to_all(value, axes, 0, 0, tiled=True)]
    pallas_call x4 -> x5, Pallas kernels: 12.5 us -> 15.7 us  [call(): pl.pallas_call(body, out_shape=[jax.ShapeDtypeStruct(o, jnp.float32) for...]
    all_to_all x3, starting transfers between devices: 19.6 us -> 17.6 us  [swap(): return lax.all_to_all(value, axes, 0, 0, tiled=True)]
    unnamed x12 -> x30, local copies, waits for them, and re-layouts: 2.7 us -> 2.1 us
  transfers between devices with their start and end apart: 11 -> 17, of which waited for: 6 -> 4; matrix products, arithmetic and copies ran while one was open for 5% -> 2% of each run, Pallas kernels for 10% -> 16%
where the time goes in v1:
time: 94.3 us; the launch traced here: 92.5 us
  starting transfers between devices  55.8 us (59%)
  Pallas kernels  15.7 us (17%)
  waiting for transfers between devices  12.5 us (13%)
  local copies, waits for them, and re-layouts  4.46 us (5%)
  other arithmetic  2.4 us (3%)
  between operations  1.63 us (2%)
    ppermute x14, starting transfers between devices, exchanged(): return lax.ppermute(value, axis, pairs + [(j, i) for i, j in pairs])  38.2 us
    all_to_all x3, starting transfers between devices, swap(): return lax.all_to_all(value, axes, 0, 0, tiled=True)  17.6 us
    pallas_call x5, Pallas kernels, call(): pl.pallas_call(body, out_shape=[jax.ShapeDtypeStruct(o, jnp.float32) for...  15.7 us
    ppermute x14, waiting for transfers between devices, exchanged(): return lax.ppermute(value, axis, pairs + [(j, i) for i, j in pairs])  12.5 us
    unnamed x30, local copies, waits for them, and re-layouts  2.1 us
  transfers between devices with their start and end apart: 17, of which 4 were waited for; matrix products, arithmetic and copies ran while one was open for 2% of the time, Pallas kernels for 16%

profile of v1, /device:TPU:31, one launch (start us, length us, event | category | flops | bytes accessed | tf_op | source)
XLA Modules:
  0.0 92.5 jit_solution(16107685006975470328)
XLA Ops:
  1.3 0.7 pad_add_fusion.facts
  2.0 1.2 %copy-done = f32[2,2,256,256]{3,2,1,0:T(8,128)S(1)} copy-done((f32[2,2,256,256]{3,2,1,0:T(8,128)S(1)}, f32[2,2,256,256]{3,2,1,0:T(8,128)}, u32[]{:S(2)}) %copy-start) | copy-done | bytes 1048600
  3.3 0.8 pack_sides.1
  4.0 0.8 collective-permute-start
  4.8 8.4 %collective-permute-start.1 = (f32[2,2,64,256]{3,2,1,0:T(8,128)S(1)}, f32[2,2,64,256]{3,2,1,0:T(8,128)S(1)}, u32[]{:S(2)}, u32[]{:S(2)}) collective-permute-start(f32[2,2,64,256]{3,2,1,0:T(8,128)S(1)} %get-tuple-element.28), channel_id=1, source_target_pairs={{16,32},{48,64},{80,96},{112,128},{144,160},{176,192},{208,224},{3... | collective-permute-start | bytes 786440 | tf_op jit(solution)/shard_map/ppermute | solution.py:275
  13.2 1.0 %dynamic-slice_bitcast_fusion = f32[256,256]{1,0:T(8,128)S(1)} fusion(f32[1,1,2,256,256]{4,3,2,1,0:T(8,128)} %param.9, s32[]{:T(128)S(6)} %select_n.29), kind=kLoop, calls=%fused_computation.5 | loop fusion | bytes 524292 | tf_op jit(solution)/shard_map/jit(dynamic_index_in_dim)/squeeze | solution.py:290
  14.1 0.0 collective-permute-done.row_a
  14.1 0.0 copy-start.2
  14.2 0.1 collective-permute-start.12
  14.3 0.6 collective-permute-start.2
  14.9 3.2 %collective-permute-start.3 = (f32[2,256,128]{2,1,0:T(8,128)S(1)}, f32[2,256,128]{2,1,0:T(8,128)S(1)}, u32[]{:S(2)}, u32[]{:S(2)}) collective-permute-start(f32[2,256,128]{2,1,0:T(8,128)S(1)} %get-tuple-element.30), channel_id=1, source_target_pairs={{1,2},{3,4},{5,6},{7,8},{9,10},{11,12},{13,14},{2,1},{4,3},{6,5},{... | collective-permute-start | bytes 786440 | tf_op jit(solution)/shard_map/ppermute | solution.py:275
  18.1 0.5 collective-permute-done.1.row_b
  18.6 0.7 pack_corners.1
  19.3 0.6 collective-permute-start.4
  19.9 4.0 %collective-permute-start.5 = (f32[2,128,128]{2,1,0:T(8,128)S(1)}, f32[2,128,128]{2,1,0:T(8,128)S(1)}, u32[]{:S(2)}, u32[]{:S(2)}) collective-permute-start(f32[2,128,128]{2,1,0:T(8,128)S(1)} %get-tuple-element.32), channel_id=1, source_target_pairs={{1,2},{3,4},{5,6},{7,8},{9,10},{11,12},{13,14},{2,1},{4,3},{6,5},{... | collective-permute-start | bytes 393224 | tf_op jit(solution)/shard_map/ppermute | solution.py:275
  23.9 0.0 collective-permute-done.12
  23.9 0.0 copy-done.9
  23.9 0.7 bitcast_add_fusion
  24.7 0.0 copy-done.6
  24.7 6.1 %all-to-all-start = ((f32[16,16,256]{2,1,0:T(8,128)}), f32[16,16,256]{2,1,0:T(8,128)S(1)}, u32[]{:S(2)}, u32[]{:S(2)}) async-start(f32[16,16,256]{2,1,0:T(8,128)} %bitcast.7), calls=%async_computation | async-start | bytes 524288 | tf_op jit(solution)/shard_map/all_to_all | solution.py:279
  30.8 0.0 collective-permute-done.2.col_a
  30.8 0.0 copy-start.11
  30.8 0.0 collective-permute-done.3.col_b
  30.8 0.0 copy-start.12
  30.8 0.0 collective-permute-done.4.corners_a
  30.8 0.0 copy-start.13
  30.8 0.0 collective-permute-done.5.corners_b
  30.8 0.0 copy-start.14
  30.9 0.6 copy-done.11
  31.5 0.1 copy-done.12
  31.5 0.1 copy-done.13
  31.6 0.1 copy-done.14
  31.7 11.9 %gradient.1 = (f32[2,2,256,256]{3,2,1,0:T(8,128)}, f32[2,2,64,256]{3,2,1,0:T(8,128)}, f32[2,2,64,256]{3,2,1,0:T(8,128)}, f32[2,256,128]{2,1,0:T(8,128)}, f32[2,2...) custom-call(s32[5]{0:T(128)} %copy-done.6, ...), custom_call_target="tpu_custom_call" | custom-call | flops 3221225472 | bytes 5767168 | tf_op jit(solution)/shard_map/gradient/pallas_call | solution.py:261
  43.5 0.0 copy-start.4
  43.5 0.0 copy-start.5
  43.6 0.0 copy-start.7
  43.6 0.0 copy-start.10
  43.6 0.0 copy-start.1
  43.6 0.0 all-to-all-done
  43.6 0.7 broadcast_in_dim.9
  44.3 5.1 %all-to-all-start.1 = ((f32[8,16,256]{2,1,0:T(8,128)}), f32[8,16,256]{2,1,0:T(8,128)S(1)}, u32[]{:S(2)}, u32[]{:S(2)}) async-start(f32[8,16,256]{2,1,0:T(8,128)} %broadcast_in_dim.9), calls=%async_computation.1 | async-start | bytes 262144 | tf_op jit(solution)/shard_map/all_to_all | solution.py:279
  49.4 0.6 collective-permute-start.6
  50.0 4.3 %collective-permute-start.7 = (f32[2,128,128]{2,1,0:T(8,128)}, f32[2,128,128]{2,1,0:T(8,128)S(1)}, u32[]{:S(2)}, u32[]{:S(2)}) collective-permute-start(f32[2,128,128]{2,1,0:T(8,128)} %get-tuple-element.35), channel_id=1, source_target_pairs={{1,2},{3,4},{5,6},{7,8},{9,10},{11,12},{13,14},{2,1},{4,3},{6,5},{... | collective-permute-start | bytes 393224 | tf_op jit(solution)/shard_map/ppermute | solution.py:275
  54.3 0.0 collective-permute-done.6.corners_a
  54.4 5.1 %collective-permute-done.7.corners_b = f32[2,128,128]{2,1,0:T(8,128)S(1)} collective-permute-done((f32[2,128,128]{2,1,0:T(8,128)}, f32[2,128,128]{2,1,0:T(8,128)S(1)}, u32[]{:S(2)}, u32[]{:S(2)}) %collective-permute-start.7) | collective-permute-done | bytes 131104 | tf_op jit(solution)/shard_map/ppermute | solution.py:275
  59.5 0.0 all-to-all-done.1
  59.5 0.7 broadcast_in_dim.10
  60.2 6.4 %all-to-all-start.2 = ((f32[16,16,256]{2,1,0:T(8,128)}), f32[16,16,256]{2,1,0:T(8,128)S(1)}, u32[]{:S(2)}, u32[]{:S(2)}) async-start(f32[16,16,256]{2,1,0:T(8,128)} %broadcast_in_dim.10), calls=%async_computation.2 | async-start | bytes 524288 | tf_op jit(solution)/shard_map/all_to_all | solution.py:279
  66.6 0.0 copy-done.4
  66.7 0.7 margins.1
  67.4 4.6 %collective-permute-start.10 = (f32[2,2,64,256]{3,2,1,0:T(8,128)S(1)}, f32[2,2,64,256]{3,2,1,0:T(8,128)S(1)}, u32[]{:S(2)}, u32[]{:S(2)}) collective-permute-start(f32[2,2,64,256]{3,2,1,0:T(8,128)S(1)} %get-tuple-element.44), channel_id=1, source_target_pairs={{0,16},{32,48},{64,80},{96,112},{128,144},{160,176},{192,208},{224... | collective-permute-start | bytes 786440 | tf_op jit(solution)/shard_map/ppermute | solution.py:275
  71.9 7.5 %collective-permute-start.11 = (f32[2,2,64,256]{3,2,1,0:T(8,128)S(1)}, f32[2,2,64,256]{3,2,1,0:T(8,128)S(1)}, u32[]{:S(2)}, u32[]{:S(2)}) collective-permute-start(f32[2,2,64,256]{3,2,1,0:T(8,128)S(1)} %get-tuple-element.45), channel_id=1, source_target_pairs={{16,32},{48,64},{80,96},{112,128},{144,160},{176,192},{208,224},{3... | collective-permute-start | bytes 786440 | tf_op jit(solution)/shard_map/ppermute | solution.py:275
  79.4 0.7 collective-permute-start.8
  80.1 2.8 %collective-permute-start.9 = (f32[2,256,128]{2,1,0:T(8,128)S(1)}, f32[2,256,128]{2,1,0:T(8,128)S(1)}, u32[]{:S(2)}, u32[]{:S(2)}) collective-permute-start(f32[2,256,128]{2,1,0:T(8,128)S(1)} %copy-done.10), channel_id=1, source_target_pairs={{1,2},{3,4},{5,6},{7,8},{9,10},{11,12},{13,14},{2,1},{4,3},{6,5},{... | collective-permute-start | bytes 786440 | tf_op jit(solution)/shard_map/ppermute | solution.py:275
  82.9 0.0 all-to-all-done.2
  82.9 0.1 collective-permute-start.13
  83.0 0.0 collective-permute-done.10.row_a
  83.0 3.3 %collective-permute-done.11.row_b = f32[2,2,64,256]{3,2,1,0:T(8,128)S(1)} collective-permute-done((f32[2,2,64,256]{3,2,1,0:T(8,128)S(1)}, f32[2,2,64,256]{3,2,1,0:T(8,128)S(1)}, u32[]{:S(2)}, u32[]{:S(2)}) %collective-permute-start.11) | collective-permute-done | bytes 262176 | tf_op jit(solution)/shard_map/ppermute | solution.py:275
  86.2 0.0 collective-permute-done.8.col_a
  86.2 3.6 %collective-permute-done.9.col_b = f32[2,256,128]{2,1,0:T(8,128)S(1)} collective-permute-done((f32[2,256,128]{2,1,0:T(8,128)S(1)}, f32[2,256,128]{2,1,0:T(8,128)S(1)}, u32[]{:S(2)}, u32[]{:S(2)}) %collective-permute-start.9) | collective-permute-done | bytes 262176 | tf_op jit(solution)/shard_map/ppermute | solution.py:275
  89.9 1.7 %finish.1 = f32[2,2,256,256]{3,2,1,0:T(8,128)} custom-call(s32[5]{0:T(128)S(1)} %copy-done.7, f32[2,2,256,256]{3,2,1,0:T(8,128)S(1)} %copy-done.1, f32[2,256,128]{2,1,0:T(8,128)S(1)} %collective-permute-done.8.col_a, f32[2,256,128]{2,1,0:T(8,128)S(1)} %collective-permute-done.9.col_b, f32[2,2,64,256]{3,2,1,0:T(8,128)S(1)} %collective-permute-done.10.row_a, ...), custom_call_target="tpu_custom_call" | custom-call | bytes 2097152 | tf_op jit(solution)/shard_map/finish/pallas_call | solution.py:261
  91.6 0.0 collective-permute-done.13
  91.7 0.0 copy-done.8
  91.7 0.9 fusion
  (14 shorter events, 0.1 us)
Async XLA Ops:
  2.0 1.2 %copy-start = (f32[2,2,256,256]{3,2,1,0:T(8,128)S(1)}, f32[2,2,256,256]{3,2,1,0:T(8,128)}, u32[]{:S(2)}) copy-start(f32[2,2,256,256]{3,2,1,0:T(8,128)} %objects.3) | copy-start | bytes 3145732
  3.2 21.4 %copy-start.6 = (s32[5]{0:T(128)}, s32[5]{0:T(128)S(1)}, u32[]{:S(2)}) copy-start(s32[5]{0:T(128)S(1)} %pad_add_fusion.facts) | copy-start | bytes 64
  3.2 20.7 %copy-start.9 = (f32[1,1,2,256,256]{4,3,2,1,0:T(8,128)S(1)}, f32[1,1,2,256,256]{4,3,2,1,0:T(8,128)}, u32[]{:S(2)}) copy-start(f32[1,1,2,256,256]{4,3,2,1,0:T(8,128)} %param.9) | copy-start | bytes 1572868
  4.0 10.1 %collective-permute-start = (f32[2,2,64,256]{3,2,1,0:T(8,128)S(1)}, f32[2,2,64,256]{3,2,1,0:T(8,128)S(1)}, u32[]{:S(2)}, u32[]{:S(2)}) collective-permute-start(f32[2,2,64,256]{3,2,1,0:T(8,128)S(1)} %get-tuple-element.27), channel_id=1, source_target_pairs={{0,16},{32,48},{64,80},{96,112},{128,144},{160,176},{192,208},{224... | collective-permute-start | bytes 786440 | tf_op jit(solution)/shard_map/ppermute | solution.py:275
  4.8 13.8 %collective-permute-start.1 = (f32[2,2,64,256]{3,2,1,0:T(8,128)S(1)}, f32[2,2,64,256]{3,2,1,0:T(8,128)S(1)}, u32[]{:S(2)}, u32[]{:S(2)}) collective-permute-start(f32[2,2,64,256]{3,2,1,0:T(8,128)S(1)} %get-tuple-element.28), channel_id=1, source_target_pairs={{16,32},{48,64},{80,96},{112,128},{144,160},{176,192},{208,224},{3... | collective-permute-start | bytes 786440 | tf_op jit(solution)/shard_map/ppermute | solution.py:275
  14.1 16.7 %copy-start.2 = (f32[2,2,64,256]{3,2,1,0:T(8,128)}, f32[2,2,64,256]{3,2,1,0:T(8,128)S(1)}, u32[]{:S(2)}) copy-start(f32[2,2,64,256]{3,2,1,0:T(8,128)S(1)} %collective-permute-done.row_a) | copy-start | bytes 786436
  14.2 9.8 %collective-permute-start.12 = (f32[256,256]{1,0:T(8,128)S(1)}, f32[256,256]{1,0:T(8,128)S(1)}, u32[]{:S(2)}, u32[]{:S(2)}) collective-permute-start(f32[256,256]{1,0:T(8,128)S(1)} %dynamic-slice_bitcast_fusion), channel_id=1, source_target_pairs={{0,16},{16,0},{1,17},{17,1},{2,18},{18,2},{3,19},{19,3},{4,20},{20... | collective-permute-start | bytes 786440 | tf_op jit(solution)/shard_map/ppermute | solution.py:275
  14.3 16.5 %collective-permute-start.2 = (f32[2,256,128]{2,1,0:T(8,128)S(1)}, f32[2,256,128]{2,1,0:T(8,128)S(1)}, u32[]{:S(2)}, u32[]{:S(2)}) collective-permute-start(f32[2,256,128]{2,1,0:T(8,128)S(1)} %get-tuple-element.29), channel_id=1, source_target_pairs={{0,1},{2,3},{4,5},{6,7},{8,9},{10,11},{12,13},{14,15},{1,0},{3,2},... | collective-permute-start | bytes 786440 | tf_op jit(solution)/shard_map/ppermute | solution.py:275
  14.9 15.9 %collective-permute-start.3 = (f32[2,256,128]{2,1,0:T(8,128)S(1)}, f32[2,256,128]{2,1,0:T(8,128)S(1)}, u32[]{:S(2)}, u32[]{:S(2)}) collective-permute-start(f32[2,256,128]{2,1,0:T(8,128)S(1)} %get-tuple-element.30), channel_id=1, source_target_pairs={{1,2},{3,4},{5,6},{7,8},{9,10},{11,12},{13,14},{2,1},{4,3},{6,5},{... | collective-permute-start | bytes 786440 | tf_op jit(solution)/shard_map/ppermute | solution.py:275
  18.6 12.3 %copy-start.3 = (f32[2,2,64,256]{3,2,1,0:T(8,128)}, f32[2,2,64,256]{3,2,1,0:T(8,128)S(1)}, u32[]{:S(2)}) copy-start(f32[2,2,64,256]{3,2,1,0:T(8,128)S(1)} %collective-permute-done.1.row_b) | copy-start | bytes 786436
  19.3 11.5 %collective-permute-start.4 = (f32[2,128,128]{2,1,0:T(8,128)S(1)}, f32[2,128,128]{2,1,0:T(8,128)S(1)}, u32[]{:S(2)}, u32[]{:S(2)}) collective-permute-start(f32[2,128,128]{2,1,0:T(8,128)S(1)} %get-tuple-element.31), channel_id=1, source_target_pairs={{0,1},{2,3},{4,5},{6,7},{8,9},{10,11},{12,13},{14,15},{1,0},{3,2},... | collective-permute-start | bytes 393224 | tf_op jit(solution)/shard_map/ppermute | solution.py:275
  19.9 10.9 %collective-permute-start.5 = (f32[2,128,128]{2,1,0:T(8,128)S(1)}, f32[2,128,128]{2,1,0:T(8,128)S(1)}, u32[]{:S(2)}, u32[]{:S(2)}) collective-permute-start(f32[2,128,128]{2,1,0:T(8,128)S(1)} %get-tuple-element.32), channel_id=1, source_target_pairs={{1,2},{3,4},{5,6},{7,8},{9,10},{11,12},{13,14},{2,1},{4,3},{6,5},{... | collective-permute-start | bytes 393224 | tf_op jit(solution)/shard_map/ppermute | solution.py:275
  24.7 18.9 %all-to-all-start = ((f32[16,16,256]{2,1,0:T(8,128)}), f32[16,16,256]{2,1,0:T(8,128)S(1)}, u32[]{:S(2)}, u32[]{:S(2)}) async-start(f32[16,16,256]{2,1,0:T(8,128)} %bitcast.7), calls=%async_computation | async-start | bytes 524288 | tf_op jit(solution)/shard_map/all_to_all | solution.py:279
  30.8 0.7 copy-start.11
  30.8 0.8 copy-start.12
  30.8 0.8 copy-start.13
  30.8 0.8 copy-start.14
  43.5 23.1 %copy-start.4 = (f32[2,2,64,256]{3,2,1,0:T(8,128)S(1)}, f32[2,2,64,256]{3,2,1,0:T(8,128)}, u32[]{:S(2)}) copy-start(f32[2,2,64,256]{3,2,1,0:T(8,128)} %get-tuple-element.40.north) | copy-start | bytes 786436
  43.5 23.1 %copy-start.5 = (f32[2,2,64,256]{3,2,1,0:T(8,128)S(1)}, f32[2,2,64,256]{3,2,1,0:T(8,128)}, u32[]{:S(2)}) copy-start(f32[2,2,64,256]{3,2,1,0:T(8,128)} %get-tuple-element.41.south) | copy-start | bytes 786436
  43.6 23.1 %copy-start.7 = (s32[5]{0:T(128)S(1)}, s32[5]{0:T(128)}, u32[]{:S(2)}) copy-start(s32[5]{0:T(128)} %copy-done.6) | copy-start | bytes 64
  43.6 36.5 %copy-start.10 = (f32[2,256,128]{2,1,0:T(8,128)S(1)}, f32[2,256,128]{2,1,0:T(8,128)}, u32[]{:S(2)}) copy-start(f32[2,256,128]{2,1,0:T(8,128)} %get-tuple-element.39) | copy-start | bytes 786436
  43.6 46.3 %copy-start.1 = (f32[2,2,256,256]{3,2,1,0:T(8,128)S(1)}, f32[2,2,256,256]{3,2,1,0:T(8,128)}, u32[]{:S(2)}) copy-start(f32[2,2,256,256]{3,2,1,0:T(8,128)} %get-tuple-element.33.center) | copy-start | bytes 3145732
  44.3 15.2 %all-to-all-start.1 = ((f32[8,16,256]{2,1,0:T(8,128)}), f32[8,16,256]{2,1,0:T(8,128)S(1)}, u32[]{:S(2)}, u32[]{:S(2)}) async-start(f32[8,16,256]{2,1,0:T(8,128)} %broadcast_in_dim.9), calls=%async_computation.1 | async-start | bytes 262144 | tf_op jit(solution)/shard_map/all_to_all | solution.py:279
  49.4 4.9 %collective-permute-start.6 = (f32[2,128,128]{2,1,0:T(8,128)}, f32[2,128,128]{2,1,0:T(8,128)S(1)}, u32[]{:S(2)}, u32[]{:S(2)}) collective-permute-start(f32[2,128,128]{2,1,0:T(8,128)} %get-tuple-element.34), channel_id=1, source_target_pairs={{0,1},{2,3},{4,5},{6,7},{8,9},{10,11},{12,13},{14,15},{1,0},{3,2},... | collective-permute-start | bytes 393224 | tf_op jit(solution)/shard_map/ppermute | solution.py:275
  50.0 9.5 %collective-permute-start.7 = (f32[2,128,128]{2,1,0:T(8,128)}, f32[2,128,128]{2,1,0:T(8,128)S(1)}, u32[]{:S(2)}, u32[]{:S(2)}) collective-permute-start(f32[2,128,128]{2,1,0:T(8,128)} %get-tuple-element.35), channel_id=1, source_target_pairs={{1,2},{3,4},{5,6},{7,8},{9,10},{11,12},{13,14},{2,1},{4,3},{6,5},{... | collective-permute-start | bytes 393224 | tf_op jit(solution)/shard_map/ppermute | solution.py:275
  60.2 22.6 %all-to-all-start.2 = ((f32[16,16,256]{2,1,0:T(8,128)}), f32[16,16,256]{2,1,0:T(8,128)S(1)}, u32[]{:S(2)}, u32[]{:S(2)}) async-start(f32[16,16,256]{2,1,0:T(8,128)} %broadcast_in_dim.10), calls=%async_computation.2 | async-start | bytes 524288 | tf_op jit(solution)/shard_map/all_to_all | solution.py:279
  67.4 15.6 %collective-permute-start.10 = (f32[2,2,64,256]{3,2,1,0:T(8,128)S(1)}, f32[2,2,64,256]{3,2,1,0:T(8,128)S(1)}, u32[]{:S(2)}, u32[]{:S(2)}) collective-permute-start(f32[2,2,64,256]{3,2,1,0:T(8,128)S(1)} %get-tuple-element.44), channel_id=1, source_target_pairs={{0,16},{32,48},{64,80},{96,112},{128,144},{160,176},{192,208},{224... | collective-permute-start | bytes 786440 | tf_op jit(solution)/shard_map/ppermute | solution.py:275
  71.9 14.3 %collective-permute-start.11 = (f32[2,2,64,256]{3,2,1,0:T(8,128)S(1)}, f32[2,2,64,256]{3,2,1,0:T(8,128)S(1)}, u32[]{:S(2)}, u32[]{:S(2)}) collective-permute-start(f32[2,2,64,256]{3,2,1,0:T(8,128)S(1)} %get-tuple-element.45), channel_id=1, source_target_pairs={{16,32},{48,64},{80,96},{112,128},{144,160},{176,192},{208,224},{3... | collective-permute-start | bytes 786440 | tf_op jit(solution)/shard_map/ppermute | solution.py:275
  79.4 6.8 %collective-permute-start.8 = (f32[2,256,128]{2,1,0:T(8,128)}, f32[2,256,128]{2,1,0:T(8,128)S(1)}, u32[]{:S(2)}, u32[]{:S(2)}) collective-permute-start(f32[2,256,128]{2,1,0:T(8,128)} %get-tuple-element.38), channel_id=1, source_target_pairs={{0,1},{2,3},{4,5},{6,7},{8,9},{10,11},{12,13},{14,15},{1,0},{3,2},... | collective-permute-start | bytes 786440 | tf_op jit(solution)/shard_map/ppermute | solution.py:275
  80.1 9.8 %collective-permute-start.9 = (f32[2,256,128]{2,1,0:T(8,128)S(1)}, f32[2,256,128]{2,1,0:T(8,128)S(1)}, u32[]{:S(2)}, u32[]{:S(2)}) collective-permute-start(f32[2,256,128]{2,1,0:T(8,128)S(1)} %copy-done.10), channel_id=1, source_target_pairs={{1,2},{3,4},{5,6},{7,8},{9,10},{11,12},{13,14},{2,1},{4,3},{6,5},{... | collective-permute-start | bytes 786440 | tf_op jit(solution)/shard_map/ppermute | solution.py:275
  82.9 8.7 %collective-permute-start.13 = (f32[256,256]{1,0:T(8,128)S(1)}, f32[256,256]{1,0:T(8,128)S(1)}, u32[]{:S(2)}, u32[]{:S(2)}) collective-permute-start(f32[256,256]{1,0:T(8,128)S(1)} %bitcast.19), channel_id=1, source_target_pairs={{0,16},{16,0},{1,17},{17,1},{2,18},{18,2},{3,19},{19,3},{4,20},{20... | collective-permute-start | bytes 786440 | tf_op jit(solution)/shard_map/ppermute | solution.py:275
  89.9 1.8 %copy-start.8 = (f32[2,256,256]{2,1,0:T(8,128)S(1)}, f32[2,256,256]{2,1,0:T(8,128)}, u32[]{:S(2)}) copy-start(f32[2,256,256]{2,1,0:T(8,128)} %probe.1) | copy-start | bytes 1572868

commit v2 on v1

--- a/solution.py
+++ b/solution.py
@@ -283,17 +283,24 @@
     return lax.optimization_barrier((value, *others))[0]
 
 
-def probe_sum(partial, *marks):
-    plane, depth = lax.axis_size(PLANE), lax.axis_size(DEPTH)
-    rows = WIN // plane
+def scatter_sum(partial, mark):
+    plane = lax.axis_size(PLANE)
     core = lax.axis_index(PAIR)
     own, other = (lax.dynamic_index_in_dim(partial, k, 0, False) for k in (core, 1 - core))
-    part = own + exchanged(after(other, marks[0]), PAIR, 0)
-    part = swap(after(part, marks[1]).reshape(plane, rows, WIN), PLANE)
-    part = jnp.sum(after(part, marks[2]), axis=0)
-    part = swap(jnp.broadcast_to(part, (depth, rows, WIN)), DEPTH)
-    part = jnp.sum(after(part, marks[3]), axis=0)
-    own = swap(jnp.broadcast_to(part, (plane, rows, WIN)), PLANE).reshape(WIN, WIN)
+    part = own + exchanged(after(other, mark), PAIR, 0)
+    return swap(part.reshape(plane, WIN // plane, WIN), PLANE)
+
+
+def depth_sum(parts, mark):
+    part = jnp.sum(after(parts, mark), axis=0)
+    return swap(jnp.broadcast_to(part, (lax.axis_size(DEPTH),) + part.shape), DEPTH)
+
+
+def gather_sum(parts, mark, last):
+    part = jnp.sum(after(parts, mark), axis=0)
+    core = lax.axis_index(PAIR)
+    own = swap(jnp.broadcast_to(part, (lax.axis_size(PLANE),) + part.shape), PLANE).reshape(WIN, WIN)
+    own = after(own, last)
     other = exchanged(own, PAIR, 0)
     return jnp.stack([either(core, own, other), either(core, other, own)])
 
@@ -308,9 +315,10 @@
     row_a, row_b, col_a, col_b = call(pack_sides, [strip] * 2 + [column] * 2, facts, objects, name="pack_sides")
     row_b, row_a = exchanged(row_b, ROW, 1), exchanged(row_a, ROW, 0)
     col_b, col_a = exchanged(col_b, COL, 1), exchanged(col_a, COL, 0)
-    side_mark = row_a
+    scattered = scatter_sum(prev_partial[0, 0], row_a)
     sent_a, sent_b = call(pack_corners, [corners] * 2, facts, row_a, row_b, name="pack_corners")
     corners_b, corners_a = exchanged(sent_b, COL, 1), exchanged(sent_a, COL, 0)
+    corners_a, scattered = lax.optimization_barrier((corners_a, scattered))
     center, north, south, col_a_part, col_b_part, corners_a_part, corners_b_part, partial = call(
         gradient,
         [tile, strip, strip, column, column, corners, corners, (2, WIN, WIN)],
@@ -327,15 +335,16 @@
         name="gradient",
     )
     corners_b, corners_a = exchanged(corners_b_part, COL, 1), exchanged(corners_a_part, COL, 0)
-    corners_a, corners_b, col_a_part, col_b_part = lax.optimization_barrier(
-        (corners_a, corners_b, col_a_part, col_b_part)
+    deep = depth_sum(scattered, partial)
+    corners_a, corners_b, col_a_part, col_b_part, deep = lax.optimization_barrier(
+        (corners_a, corners_b, col_a_part, col_b_part, deep)
     )
     row_a, row_b = call(add_margins, [strip] * 2, facts, north, south, corners_a, corners_b, name="margins")
     row_b, row_a = exchanged(row_b, ROW, 1), exchanged(row_a, ROW, 0)
     col_b, col_a = exchanged(col_b_part, COL, 1), exchanged(col_a_part, COL, 0)
-    (new_objects,) = call(finish, [tile], facts, center, col_a, col_b, row_a, row_b, name="finish")
+    (new_objects,) = call(finish, [tile], facts, center, col_a, col_b, row_a, row_b, flops=10**10, name="finish")
     rate = PROBE_RATE / math.sqrt(lax.axis_size(ROW) * lax.axis_size(COL))
-    total = probe_sum(prev_partial[0, 0], side_mark, side_mark, partial, corners_a)
+    total = gather_sum(deep, row_a, row_b)
     new_probe = probe - rate * total
     return (new_objects, new_probe, partial[None, None])
 

time: 94.3 us -> 96.6 us (1.024)
  the two profiles are of different devices: /device:TPU:31 before, /device:TPU:1 now
where the time goes in v2:
time: 96.6 us; the launch traced here: 96 us
  starting transfers between devices  50.1 us (52%)
  waiting for transfers between devices  19.7 us (20%)
  Pallas kernels  15.9 us (16%)
  local copies, waits for them, and re-layouts  6.32 us (7%)
  other arithmetic  2.41 us (2%)
  between operations  1.57 us (2%)
    all_to_all x3, starting transfers between devices, swap(): return lax.all_to_all(value, axes, 0, 0, tiled=True)  31.4 us
    ppermute x14, starting transfers between devices, exchanged(): return lax.ppermute(value, axis, pairs + [(j, i) for i, j in pairs])  18.6 us
    pallas_call x5, Pallas kernels, call(): pl.pallas_call(body, out_shape=[jax.ShapeDtypeStruct(o, jnp.float32) for...  15.9 us
    all_to_all x3, waiting for transfers between devices, swap(): return lax.all_to_all(value, axes, 0, 0, tiled=True)  13.6 us
    ppermute x14, waiting for transfers between devices, exchanged(): return lax.ppermute(value, axis, pairs + [(j, i) for i, j in pairs])  6.06 us
    unnamed x28, local copies, waits for them, and re-layouts  3.96 us
  transfers between devices with their start and end apart: 17, of which 6 were waited for; matrix products, arithmetic and copies ran while one was open for 3% of the time, Pallas kernels for 3%

profile of v2, /device:TPU:1, one launch (start us, length us, event | category | flops | bytes accessed | tf_op | source)
XLA Modules:
  0.0 96.0 jit_solution(14744737852143550856)
XLA Ops:
  1.3 0.7 pad_add_fusion.facts
  2.0 0.0 copy-start
  2.0 1.2 %copy-done = f32[2,2,256,256]{3,2,1,0:T(8,128)S(1)} copy-done((f32[2,2,256,256]{3,2,1,0:T(8,128)S(1)}, f32[2,2,256,256]{3,2,1,0:T(8,128)}, u32[]{:S(2)}) %copy-start) | copy-done | bytes 1048600
  3.3 0.8 pack_sides.1
  4.0 3.3 %collective-permute-start = (f32[2,2,64,256]{3,2,1,0:T(8,128)S(1)}, f32[2,2,64,256]{3,2,1,0:T(8,128)S(1)}, u32[]{:S(2)}, u32[]{:S(2)}) collective-permute-start(f32[2,2,64,256]{3,2,1,0:T(8,128)S(1)} %get-tuple-element.30), channel_id=1, source_target_pairs={{0,16},{32,48},{64,80},{96,112},{128,144},{160,176},{192,208},{224... | collective-permute-start | bytes 786440 | tf_op jit(solution)/shard_map/ppermute | solution.py:275
  7.3 1.0 %dynamic-slice_bitcast_fusion = f32[256,256]{1,0:T(8,128)S(1)} fusion(f32[1,1,2,256,256]{4,3,2,1,0:T(8,128)} %param.9, s32[]{:T(128)S(6)} %select_n.28), kind=kLoop, calls=%fused_computation.5 | loop fusion | bytes 524292 | tf_op jit(solution)/shard_map/jit(dynamic_index_in_dim)/squeeze | solution.py:289
  8.3 0.2 collective-permute-done.row_a
  8.5 0.4 collective-permute-start.5
  8.9 1.9 %collective-permute-start.1 = (f32[2,2,64,256]{3,2,1,0:T(8,128)S(1)}, f32[2,2,64,256]{3,2,1,0:T(8,128)S(1)}, u32[]{:S(2)}, u32[]{:S(2)}) collective-permute-start(f32[2,2,64,256]{3,2,1,0:T(8,128)S(1)} %get-tuple-element.31), channel_id=1, source_target_pairs={{16,32},{48,64},{80,96},{112,128},{144,160},{176,192},{208,224},{3... | collective-permute-start | bytes 786440 | tf_op jit(solution)/shard_map/ppermute | solution.py:275
  10.8 0.9 collective-permute-start.2
  11.7 0.7 collective-permute-start.3
  12.3 0.0 collective-permute-done.5
  12.3 0.0 copy-done.9
  12.4 0.7 bitcast_add_fusion
  13.1 13.5 %all-to-all-start = ((f32[16,16,256]{2,1,0:T(8,128)}), f32[16,16,256]{2,1,0:T(8,128)S(1)}, u32[]{:S(2)}, u32[]{:S(2)}) async-start(f32[16,16,256]{2,1,0:T(8,128)} %bitcast.6), calls=%async_computation | async-start | bytes 524288 | tf_op jit(solution)/shard_map/all_to_all | solution.py:279
  26.6 0.0 collective-permute-done.1.row_b
  26.6 0.0 copy-start.2
  26.6 0.7 pack_corners.1
  27.3 0.0 copy-done.5
  27.3 1.4 %collective-permute-start.4 = (f32[2,128,128]{2,1,0:T(8,128)S(1)}, f32[2,128,128]{2,1,0:T(8,128)S(1)}, u32[]{:S(2)}, u32[]{:S(2)}) collective-permute-start(f32[2,128,128]{2,1,0:T(8,128)S(1)} %get-tuple-element.34), channel_id=1, source_target_pairs={{0,1},{2,3},{4,5},{6,7},{8,9},{10,11},{12,13},{14,15},{1,0},{3,2},... | collective-permute-start | bytes 393224 | tf_op jit(solution)/shard_map/ppermute | solution.py:275
  28.7 0.7 collective-permute-start.6
  29.4 2.5 %collective-permute-done.4.corners_a = f32[2,128,128]{2,1,0:T(8,128)S(1)} collective-permute-done((f32[2,128,128]{2,1,0:T(8,128)S(1)}, f32[2,128,128]{2,1,0:T(8,128)S(1)}, u32[]{:S(2)}, u32[]{:S(2)}) %collective-permute-start.4) | collective-permute-done | bytes 131104 | tf_op jit(solution)/shard_map/ppermute | solution.py:275
  31.9 2.2 %all-to-all-done = f32[16,16,256]{2,1,0:T(8,128)S(1)} async-done(((f32[16,16,256]{2,1,0:T(8,128)}), f32[16,16,256]{2,1,0:T(8,128)S(1)}, u32[]{:S(2)}, u32[]{:S(2)}) %all-to-all-start) | async-done | bytes 262176 | tf_op jit(solution)/shard_map/all_to_all | solution.py:279
  34.1 0.0 collective-permute-done.2.col_a
  34.1 0.0 collective-permute-done.3.col_b
  34.1 0.0 copy-start.11
  34.1 0.0 collective-permute-done.6.corners_b
  34.1 0.0 copy-start.13
  34.2 0.0 copy-done.1
  34.2 0.0 copy-done.2
  34.2 0.0 copy-done.12
  34.2 0.6 copy-done.10
  34.8 0.1 copy-done.11
  34.9 0.0 copy-done.13
  35.0 12.0 %gradient.1 = (f32[2,2,256,256]{3,2,1,0:T(8,128)}, f32[2,2,64,256]{3,2,1,0:T(8,128)}, f32[2,2,64,256]{3,2,1,0:T(8,128)}, f32[2,256,128]{2,1,0:T(8,128)}, f32[2,2...) custom-call(s32[5]{0:T(128)} %copy-done.5, ...), custom_call_target="tpu_custom_call" | custom-call | flops 3221225472 | bytes 5767168 | tf_op jit(solution)/shard_map/gradient/pallas_call | solution.py:261
  47.0 0.7 broadcast_in_dim.9
  47.7 4.9 %all-to-all-start.1 = ((f32[8,16,256]{2,1,0:T(8,128)}), f32[8,16,256]{2,1,0:T(8,128)S(1)}, u32[]{:S(2)}, u32[]{:S(2)}) async-start(f32[8,16,256]{2,1,0:T(8,128)} %broadcast_in_dim.9), calls=%async_computation.1 | async-start | bytes 262144 | tf_op jit(solution)/shard_map/all_to_all | solution.py:279
  52.6 0.0 collective-permute-start.7
  52.6 0.7 collective-permute-start.8
  53.3 3.3 %collective-permute-done.7.corners_a = f32[2,128,128]{2,1,0:T(8,128)S(1)} collective-permute-done((f32[2,128,128]{2,1,0:T(8,128)}, f32[2,128,128]{2,1,0:T(8,128)S(1)}, u32[]{:S(2)}, u32[]{:S(2)}) %collective-permute-start.7) | collective-permute-done | bytes 131104 | tf_op jit(solution)/shard_map/ppermute | solution.py:275
  56.6 0.0 collective-permute-done.8.corners_b
  56.7 3.9 %all-to-all-done.1 = f32[8,16,256]{2,1,0:T(8,128)S(1)} async-done(((f32[8,16,256]{2,1,0:T(8,128)}), f32[8,16,256]{2,1,0:T(8,128)S(1)}, u32[]{:S(2)}, u32[]{:S(2)}) %all-to-all-start.1) | async-done | bytes 131104 | tf_op jit(solution)/shard_map/all_to_all | solution.py:279
  60.5 0.0 copy-done.6
  60.6 0.9 copy-done.3
  61.5 0.9 copy-done.4
  62.5 0.7 margins.1
  63.1 6.0 %collective-permute-start.11 = (f32[2,2,64,256]{3,2,1,0:T(8,128)S(1)}, f32[2,2,64,256]{3,2,1,0:T(8,128)S(1)}, u32[]{:S(2)}, u32[]{:S(2)}) collective-permute-start(f32[2,2,64,256]{3,2,1,0:T(8,128)S(1)} %get-tuple-element.52), channel_id=1, source_target_pairs={{0,16},{32,48},{64,80},{96,112},{128,144},{160,176},{192,208},{224... | collective-permute-start | bytes 786440 | tf_op jit(solution)/shard_map/ppermute | solution.py:275
  69.2 1.9 %collective-permute-start.12 = (f32[2,2,64,256]{3,2,1,0:T(8,128)S(1)}, f32[2,2,64,256]{3,2,1,0:T(8,128)S(1)}, u32[]{:S(2)}, u32[]{:S(2)}) collective-permute-start(f32[2,2,64,256]{3,2,1,0:T(8,128)S(1)} %get-tuple-element.53), channel_id=1, source_target_pairs={{16,32},{48,64},{80,96},{112,128},{144,160},{176,192},{208,224},{3... | collective-permute-start | bytes 786440 | tf_op jit(solution)/shard_map/ppermute | solution.py:275
  71.1 0.1 collective-permute-start.9
  71.2 0.7 collective-permute-start.10
  71.9 0.0 collective-permute-done.11.row_a
  71.9 0.7 broadcast_in_dim.10
  72.7 13.0 %all-to-all-start.2 = ((f32[16,16,256]{2,1,0:T(8,128)}), f32[16,16,256]{2,1,0:T(8,128)S(1)}, u32[]{:S(2)}, u32[]{:S(2)}) async-start(f32[16,16,256]{2,1,0:T(8,128)} %broadcast_in_dim.10), calls=%async_computation.2 | async-start | bytes 524288 | tf_op jit(solution)/shard_map/all_to_all | solution.py:279
  85.7 0.0 collective-permute-done.12.row_b
  85.7 7.5 %all-to-all-done.2 = f32[16,16,256]{2,1,0:T(8,128)S(1)} async-done(((f32[16,16,256]{2,1,0:T(8,128)}), f32[16,16,256]{2,1,0:T(8,128)S(1)}, u32[]{:S(2)}, u32[]{:S(2)}) %all-to-all-start.2) | async-done | bytes 262176 | tf_op jit(solution)/shard_map/all_to_all | solution.py:279
  93.2 0.0 collective-permute-start.13
  93.2 0.0 collective-permute-done.9.col_a
  93.3 0.0 collective-permute-done.10.col_b
  93.3 0.0 copy-done.7
  93.3 0.0 copy-start.8
  93.3 1.8 %finish.1 = f32[2,2,256,256]{3,2,1,0:T(8,128)} custom-call(s32[5]{0:T(128)S(1)} %copy-done.6, f32[2,2,256,256]{3,2,1,0:T(8,128)S(1)} %copy-done.7, f32[2,256,128]{2,1,0:T(8,128)S(1)} %collective-permute-done.9.col_a, f32[2,256,128]{2,1,0:T(8,128)S(1)} %collective-permute-done.10.col_b, f32[2,2,64,256]{3,2,1,0:T(8,128)S(1)} %collective-permute-done.11.row_a, ...), custom_call_target="tpu_custom_call" | custom-call | flops 10000000000 | bytes 2097152 | tf_op jit(solution)/shard_map/finish/pallas_call | solution.py:261
  95.0 0.0 collective-permute-done.13
  95.1 0.0 copy-done.8
  95.1 0.9 fusion
  (12 shorter events, 0.1 us)
Async XLA Ops:
  2.0 1.2 %copy-start = (f32[2,2,256,256]{3,2,1,0:T(8,128)S(1)}, f32[2,2,256,256]{3,2,1,0:T(8,128)}, u32[]{:S(2)}) copy-start(f32[2,2,256,256]{3,2,1,0:T(8,128)} %objects.3) | copy-start | bytes 3145732
  3.2 24.0 %copy-start.5 = (s32[5]{0:T(128)}, s32[5]{0:T(128)S(1)}, u32[]{:S(2)}) copy-start(s32[5]{0:T(128)S(1)} %pad_add_fusion.facts) | copy-start | bytes 64
  3.2 9.1 %copy-start.9 = (f32[1,1,2,256,256]{4,3,2,1,0:T(8,128)S(1)}, f32[1,1,2,256,256]{4,3,2,1,0:T(8,128)}, u32[]{:S(2)}) copy-start(f32[1,1,2,256,256]{4,3,2,1,0:T(8,128)} %param.9) | copy-start | bytes 1572868
  4.0 4.5 %collective-permute-start = (f32[2,2,64,256]{3,2,1,0:T(8,128)S(1)}, f32[2,2,64,256]{3,2,1,0:T(8,128)S(1)}, u32[]{:S(2)}, u32[]{:S(2)}) collective-permute-start(f32[2,2,64,256]{3,2,1,0:T(8,128)S(1)} %get-tuple-element.30), channel_id=1, source_target_pairs={{0,16},{32,48},{64,80},{96,112},{128,144},{160,176},{192,208},{224... | collective-permute-start | bytes 786440 | tf_op jit(solution)/shard_map/ppermute | solution.py:275
  8.5 25.7 %copy-start.1 = (f32[2,2,64,256]{3,2,1,0:T(8,128)}, f32[2,2,64,256]{3,2,1,0:T(8,128)S(1)}, u32[]{:S(2)}) copy-start(f32[2,2,64,256]{3,2,1,0:T(8,128)S(1)} %collective-permute-done.row_a) | copy-start | bytes 786436
  8.5 3.8 %collective-permute-start.5 = (f32[256,256]{1,0:T(8,128)S(1)}, f32[256,256]{1,0:T(8,128)S(1)}, u32[]{:S(2)}, u32[]{:S(2)}) collective-permute-start(f32[256,256]{1,0:T(8,128)S(1)} %dynamic-slice_bitcast_fusion), channel_id=1, source_target_pairs={{0,16},{16,0},{1,17},{17,1},{2,18},{18,2},{3,19},{19,3},{4,20},{20... | collective-permute-start | bytes 786440 | tf_op jit(solution)/shard_map/ppermute | solution.py:275
  8.9 17.7 %collective-permute-start.1 = (f32[2,2,64,256]{3,2,1,0:T(8,128)S(1)}, f32[2,2,64,256]{3,2,1,0:T(8,128)S(1)}, u32[]{:S(2)}, u32[]{:S(2)}) collective-permute-start(f32[2,2,64,256]{3,2,1,0:T(8,128)S(1)} %get-tuple-element.31), channel_id=1, source_target_pairs={{16,32},{48,64},{80,96},{112,128},{144,160},{176,192},{208,224},{3... | collective-permute-start | bytes 786440 | tf_op jit(solution)/shard_map/ppermute | solution.py:275
  10.8 23.3 %collective-permute-start.2 = (f32[2,256,128]{2,1,0:T(8,128)S(1)}, f32[2,256,128]{2,1,0:T(8,128)S(1)}, u32[]{:S(2)}, u32[]{:S(2)}) collective-permute-start(f32[2,256,128]{2,1,0:T(8,128)S(1)} %get-tuple-element.32), channel_id=1, source_target_pairs={{0,1},{2,3},{4,5},{6,7},{8,9},{10,11},{12,13},{14,15},{1,0},{3,2},... | collective-permute-start | bytes 786440 | tf_op jit(solution)/shard_map/ppermute | solution.py:275
  11.7 22.5 %collective-permute-start.3 = (f32[2,256,128]{2,1,0:T(8,128)S(1)}, f32[2,256,128]{2,1,0:T(8,128)S(1)}, u32[]{:S(2)}, u32[]{:S(2)}) collective-permute-start(f32[2,256,128]{2,1,0:T(8,128)S(1)} %get-tuple-element.33), channel_id=1, source_target_pairs={{1,2},{3,4},{5,6},{7,8},{9,10},{11,12},{13,14},{2,1},{4,3},{6,5},{... | collective-permute-start | bytes 786440 | tf_op jit(solution)/shard_map/ppermute | solution.py:275
  13.1 21.0 %all-to-all-start = ((f32[16,16,256]{2,1,0:T(8,128)}), f32[16,16,256]{2,1,0:T(8,128)S(1)}, u32[]{:S(2)}, u32[]{:S(2)}) async-start(f32[16,16,256]{2,1,0:T(8,128)} %bitcast.6), calls=%async_computation | async-start | bytes 524288 | tf_op jit(solution)/shard_map/all_to_all | solution.py:279
  26.6 7.6 %copy-start.2 = (f32[2,2,64,256]{3,2,1,0:T(8,128)}, f32[2,2,64,256]{3,2,1,0:T(8,128)S(1)}, u32[]{:S(2)}) copy-start(f32[2,2,64,256]{3,2,1,0:T(8,128)S(1)} %collective-permute-done.1.row_b) | copy-start | bytes 786436
  27.3 4.6 %collective-permute-start.4 = (f32[2,128,128]{2,1,0:T(8,128)S(1)}, f32[2,128,128]{2,1,0:T(8,128)S(1)}, u32[]{:S(2)}, u32[]{:S(2)}) collective-permute-start(f32[2,128,128]{2,1,0:T(8,128)S(1)} %get-tuple-element.34), channel_id=1, source_target_pairs={{0,1},{2,3},{4,5},{6,7},{8,9},{10,11},{12,13},{14,15},{1,0},{3,2},... | collective-permute-start | bytes 393224 | tf_op jit(solution)/shard_map/ppermute | solution.py:275
  28.7 5.4 %collective-permute-start.6 = (f32[2,128,128]{2,1,0:T(8,128)S(1)}, f32[2,128,128]{2,1,0:T(8,128)S(1)}, u32[]{:S(2)}, u32[]{:S(2)}) collective-permute-start(f32[2,128,128]{2,1,0:T(8,128)S(1)} %get-tuple-element.37), channel_id=1, source_target_pairs={{1,2},{3,4},{5,6},{7,8},{9,10},{11,12},{13,14},{2,1},{4,3},{6,5},{... | collective-permute-start | bytes 393224 | tf_op jit(solution)/shard_map/ppermute | solution.py:275
  31.9 2.3 %copy-start.12 = (f32[2,128,128]{2,1,0:T(8,128)}, f32[2,128,128]{2,1,0:T(8,128)S(1)}, u32[]{:S(2)}) copy-start(f32[2,128,128]{2,1,0:T(8,128)S(1)} %collective-permute-done.4.corners_a) | copy-start | bytes 393220
  34.1 0.7 copy-start.10
  34.1 0.8 copy-start.11
  34.1 0.8 copy-start.13
  35.0 25.6 %copy-start.6 = (s32[5]{0:T(128)S(1)}, s32[5]{0:T(128)}, u32[]{:S(2)}) copy-start(s32[5]{0:T(128)} %copy-done.5) | copy-start | bytes 64
  47.7 12.9 %all-to-all-start.1 = ((f32[8,16,256]{2,1,0:T(8,128)}), f32[8,16,256]{2,1,0:T(8,128)S(1)}, u32[]{:S(2)}, u32[]{:S(2)}) async-start(f32[8,16,256]{2,1,0:T(8,128)} %broadcast_in_dim.9), calls=%async_computation.1 | async-start | bytes 262144 | tf_op jit(solution)/shard_map/all_to_all | solution.py:279
  52.6 4.0 %collective-permute-start.7 = (f32[2,128,128]{2,1,0:T(8,128)}, f32[2,128,128]{2,1,0:T(8,128)S(1)}, u32[]{:S(2)}, u32[]{:S(2)}) collective-permute-start(f32[2,128,128]{2,1,0:T(8,128)} %get-tuple-element.39), channel_id=1, source_target_pairs={{0,1},{2,3},{4,5},{6,7},{8,9},{10,11},{12,13},{14,15},{1,0},{3,2},... | collective-permute-start | bytes 393224 | tf_op jit(solution)/shard_map/ppermute | solution.py:275
  52.6 4.0 %collective-permute-start.8 = (f32[2,128,128]{2,1,0:T(8,128)}, f32[2,128,128]{2,1,0:T(8,128)S(1)}, u32[]{:S(2)}, u32[]{:S(2)}) collective-permute-start(f32[2,128,128]{2,1,0:T(8,128)} %get-tuple-element.40), channel_id=1, source_target_pairs={{1,2},{3,4},{5,6},{7,8},{9,10},{11,12},{13,14},{2,1},{4,3},{6,5},{... | collective-permute-start | bytes 393224 | tf_op jit(solution)/shard_map/ppermute | solution.py:275
  60.6 1.0 copy-start.3
  61.5 0.9 copy-start.4
  62.5 30.8 %copy-start.7 = (f32[2,2,256,256]{3,2,1,0:T(8,128)S(1)}, f32[2,2,256,256]{3,2,1,0:T(8,128)}, u32[]{:S(2)}) copy-start(f32[2,2,256,256]{3,2,1,0:T(8,128)} %get-tuple-element.38.center) | copy-start | bytes 3145732
  63.1 8.7 %collective-permute-start.11 = (f32[2,2,64,256]{3,2,1,0:T(8,128)S(1)}, f32[2,2,64,256]{3,2,1,0:T(8,128)S(1)}, u32[]{:S(2)}, u32[]{:S(2)}) collective-permute-start(f32[2,2,64,256]{3,2,1,0:T(8,128)S(1)} %get-tuple-element.52), channel_id=1, source_target_pairs={{0,16},{32,48},{64,80},{96,112},{128,144},{160,176},{192,208},{224... | collective-permute-start | bytes 786440 | tf_op jit(solution)/shard_map/ppermute | solution.py:275
  69.2 16.5 %collective-permute-start.12 = (f32[2,2,64,256]{3,2,1,0:T(8,128)S(1)}, f32[2,2,64,256]{3,2,1,0:T(8,128)S(1)}, u32[]{:S(2)}, u32[]{:S(2)}) collective-permute-start(f32[2,2,64,256]{3,2,1,0:T(8,128)S(1)} %get-tuple-element.53), channel_id=1, source_target_pairs={{16,32},{48,64},{80,96},{112,128},{144,160},{176,192},{208,224},{3... | collective-permute-start | bytes 786440 | tf_op jit(solution)/shard_map/ppermute | solution.py:275
  71.1 22.1 %collective-permute-start.9 = (f32[2,256,128]{2,1,0:T(8,128)}, f32[2,256,128]{2,1,0:T(8,128)S(1)}, u32[]{:S(2)}, u32[]{:S(2)}) collective-permute-start(f32[2,256,128]{2,1,0:T(8,128)} %get-tuple-element.46), channel_id=1, source_target_pairs={{0,1},{2,3},{4,5},{6,7},{8,9},{10,11},{12,13},{14,15},{1,0},{3,2},... | collective-permute-start | bytes 786440 | tf_op jit(solution)/shard_map/ppermute | solution.py:275
  71.2 22.0 %collective-permute-start.10 = (f32[2,256,128]{2,1,0:T(8,128)}, f32[2,256,128]{2,1,0:T(8,128)S(1)}, u32[]{:S(2)}, u32[]{:S(2)}) collective-permute-start(f32[2,256,128]{2,1,0:T(8,128)} %get-tuple-element.47), channel_id=1, source_target_pairs={{1,2},{3,4},{5,6},{7,8},{9,10},{11,12},{13,14},{2,1},{4,3},{6,5},{... | collective-permute-start | bytes 786440 | tf_op jit(solution)/shard_map/ppermute | solution.py:275
  72.7 20.6 %all-to-all-start.2 = ((f32[16,16,256]{2,1,0:T(8,128)}), f32[16,16,256]{2,1,0:T(8,128)S(1)}, u32[]{:S(2)}, u32[]{:S(2)}) async-start(f32[16,16,256]{2,1,0:T(8,128)} %broadcast_in_dim.10), calls=%async_computation.2 | async-start | bytes 524288 | tf_op jit(solution)/shard_map/all_to_all | solution.py:279
  93.2 1.8 %collective-permute-start.13 = (f32[256,256]{1,0:T(8,128)S(1)}, f32[256,256]{1,0:T(8,128)S(1)}, u32[]{:S(2)}, u32[]{:S(2)}) collective-permute-start(f32[256,256]{1,0:T(8,128)S(1)} %bitcast.17), channel_id=1, source_target_pairs={{0,16},{16,0},{1,17},{17,1},{2,18},{18,2},{3,19},{19,3},{4,20},{20... | collective-permute-start | bytes 786440 | tf_op jit(solution)/shard_map/ppermute | solution.py:275
  93.3 1.8 %copy-start.8 = (f32[2,256,256]{2,1,0:T(8,128)S(1)}, f32[2,256,256]{2,1,0:T(8,128)}, u32[]{:S(2)}) copy-start(f32[2,256,256]{2,1,0:T(8,128)} %probe.1) | copy-start | bytes 1572868

commit v3 on v2

--- a/solution.py
+++ b/solution.py
@@ -283,11 +283,11 @@
     return lax.optimization_barrier((value, *others))[0]
 
 
-def scatter_sum(partial, mark):
+def scatter_sum(partial):
     plane = lax.axis_size(PLANE)
     core = lax.axis_index(PAIR)
     own, other = (lax.dynamic_index_in_dim(partial, k, 0, False) for k in (core, 1 - core))
-    part = own + exchanged(after(other, mark), PAIR, 0)
+    part = own + exchanged(other, PAIR, 0)
     return swap(part.reshape(plane, WIN // plane, WIN), PLANE)
 
 
@@ -296,8 +296,8 @@
     return swap(jnp.broadcast_to(part, (lax.axis_size(DEPTH),) + part.shape), DEPTH)
 
 
-def gather_sum(parts, mark, last):
-    part = jnp.sum(after(parts, mark), axis=0)
+def gather_sum(parts, last):
+    part = jnp.sum(parts, axis=0)
     core = lax.axis_index(PAIR)
     own = swap(jnp.broadcast_to(part, (lax.axis_size(PLANE),) + part.shape), PLANE).reshape(WIN, WIN)
     own = after(own, last)
@@ -315,10 +315,11 @@
     row_a, row_b, col_a, col_b = call(pack_sides, [strip] * 2 + [column] * 2, facts, objects, name="pack_sides")
     row_b, row_a = exchanged(row_b, ROW, 1), exchanged(row_a, ROW, 0)
     col_b, col_a = exchanged(col_b, COL, 1), exchanged(col_a, COL, 0)
-    scattered = scatter_sum(prev_partial[0, 0], row_a)
+    scattered = scatter_sum(prev_partial[0, 0])
     sent_a, sent_b = call(pack_corners, [corners] * 2, facts, row_a, row_b, name="pack_corners")
     corners_b, corners_a = exchanged(sent_b, COL, 1), exchanged(sent_a, COL, 0)
-    corners_a, scattered = lax.optimization_barrier((corners_a, scattered))
+    deep = depth_sum(scattered, col_a)
+    corners_a, deep = lax.optimization_barrier((corners_a, deep))
     center, north, south, col_a_part, col_b_part, corners_a_part, corners_b_part, partial = call(
         gradient,
         [tile, strip, strip, column, column, corners, corners, (2, WIN, WIN)],
@@ -335,16 +336,15 @@
         name="gradient",
     )
     corners_b, corners_a = exchanged(corners_b_part, COL, 1), exchanged(corners_a_part, COL, 0)
-    deep = depth_sum(scattered, partial)
-    corners_a, corners_b, col_a_part, col_b_part, deep = lax.optimization_barrier(
-        (corners_a, corners_b, col_a_part, col_b_part, deep)
+    corners_a, corners_b, col_a_part, col_b_part = lax.optimization_barrier(
+        (corners_a, corners_b, col_a_part, col_b_part)
     )
     row_a, row_b = call(add_margins, [strip] * 2, facts, north, south, corners_a, corners_b, name="margins")
     row_b, row_a = exchanged(row_b, ROW, 1), exchanged(row_a, ROW, 0)
     col_b, col_a = exchanged(col_b_part, COL, 1), exchanged(col_a_part, COL, 0)
-    (new_objects,) = call(finish, [tile], facts, center, col_a, col_b, row_a, row_b, flops=10**10, name="finish")
+    (new_objects,) = call(finish, [tile], facts, center, col_a, col_b, row_a, row_b, name="finish")
     rate = PROBE_RATE / math.sqrt(lax.axis_size(ROW) * lax.axis_size(COL))
-    total = gather_sum(deep, row_a, row_b)
+    total = gather_sum(deep, partial)
     new_probe = probe - rate * total
     return (new_objects, new_probe, partial[None, None])
 

time: 96.6 us -> 96.5 us (level)
  the two profiles are of different devices: /device:TPU:1 before, /device:TPU:31 now
where the time goes in v3:
time: 96.5 us; the launch traced here: 95.8 us
  starting transfers between devices  49.8 us (52%)
  waiting for transfers between devices  18.6 us (19%)
  Pallas kernels  15.9 us (16%)
  local copies, waits for them, and re-layouts  7.5 us (8%)
  other arithmetic  2.41 us (2%)
  between operations  1.6 us (2%)
    ppermute x14, starting transfers between devices, exchanged(): return lax.ppermute(value, axis, pairs + [(j, i) for i, j in pairs])  33.1 us
    all_to_all x3, starting transfers between devices, swap(): return lax.all_to_all(value, axes, 0, 0, tiled=True)  16.7 us
    pallas_call x5, Pallas kernels, call(): pl.pallas_call(body, out_shape=[jax.ShapeDtypeStruct(o, jnp.float32) for...  15.9 us
    ppermute x14, waiting for transfers between devices, exchanged(): return lax.ppermute(value, axis, pairs + [(j, i) for i, j in pairs])  15.5 us
    unnamed x28, local copies, waits for them, and re-layouts  5.06 us
    all_to_all x3, waiting for transfers between devices, swap(): return lax.all_to_all(value, axes, 0, 0, tiled=True)  3.14 us
  transfers between devices with their start and end apart: 17, of which 5 were waited for; matrix products, arithmetic and copies ran while one was open for 3% of the time, Pallas kernels for 17%

profile of v3, /device:TPU:31, one launch (start us, length us, event | category | flops | bytes accessed | tf_op | source)
XLA Modules:
  0.0 95.8 jit_solution(17368093271475259833)
XLA Ops:
  0.6 0.0 copy-start.9
  0.6 1.0 %dynamic-slice_bitcast_fusion = f32[256,256]{1,0:T(8,128)S(1)} fusion(f32[1,1,2,256,256]{4,3,2,1,0:T(8,128)} %param.9, s32[]{:T(128)S(6)} %select_n.28), kind=kLoop, calls=%fused_computation.5 | loop fusion | bytes 524292 | tf_op jit(solution)/shard_map/jit(dynamic_index_in_dim)/squeeze | solution.py:289
  1.7 0.8 collective-permute-start.5
  3.1 0.7 pad_add_fusion.facts
  3.8 1.2 %copy-done = f32[2,2,256,256]{3,2,1,0:T(8,128)S(1)} copy-done((f32[2,2,256,256]{3,2,1,0:T(8,128)S(1)}, f32[2,2,256,256]{3,2,1,0:T(8,128)}, u32[]{:S(2)}) %copy-start) | copy-done | bytes 1048600
  5.1 0.8 pack_sides.1
  5.8 0.6 collective-permute-start.2
  6.4 0.0 collective-permute-done.5
  6.5 0.0 copy-done.9
  6.5 0.7 bitcast_add_fusion
  7.2 6.9 %all-to-all-start = ((f32[16,16,256]{2,1,0:T(8,128)}), f32[16,16,256]{2,1,0:T(8,128)S(1)}, u32[]{:S(2)}, u32[]{:S(2)}) async-start(f32[16,16,256]{2,1,0:T(8,128)} %bitcast.6), calls=%async_computation | async-start | bytes 524288 | tf_op jit(solution)/shard_map/all_to_all | solution.py:279
  14.1 0.9 collective-permute-start
  14.9 8.7 %collective-permute-start.1 = (f32[2,2,64,256]{3,2,1,0:T(8,128)S(1)}, f32[2,2,64,256]{3,2,1,0:T(8,128)S(1)}, u32[]{:S(2)}, u32[]{:S(2)}) collective-permute-start(f32[2,2,64,256]{3,2,1,0:T(8,128)S(1)} %get-tuple-element.28), channel_id=1, source_target_pairs={{16,32},{48,64},{80,96},{112,128},{144,160},{176,192},{208,224},{3... | collective-permute-start | bytes 786440 | tf_op jit(solution)/shard_map/ppermute | solution.py:275
  23.7 2.3 %collective-permute-start.3 = (f32[2,256,128]{2,1,0:T(8,128)S(1)}, f32[2,256,128]{2,1,0:T(8,128)S(1)}, u32[]{:S(2)}, u32[]{:S(2)}) collective-permute-start(f32[2,256,128]{2,1,0:T(8,128)S(1)} %get-tuple-element.30), channel_id=1, source_target_pairs={{1,2},{3,4},{5,6},{7,8},{9,10},{11,12},{13,14},{2,1},{4,3},{6,5},{... | collective-permute-start | bytes 786440 | tf_op jit(solution)/shard_map/ppermute | solution.py:275
  25.9 0.0 collective-permute-done.2.col_a
  26.0 0.0 copy-start.10
  26.0 0.0 all-to-all-done
  26.0 0.7 broadcast_in_dim.9
  26.7 3.4 %all-to-all-start.1 = ((f32[8,16,256]{2,1,0:T(8,128)}), f32[8,16,256]{2,1,0:T(8,128)S(1)}, u32[]{:S(2)}, u32[]{:S(2)}) async-start(f32[8,16,256]{2,1,0:T(8,128)} %broadcast_in_dim.9), calls=%async_computation.1 | async-start | bytes 262144 | tf_op jit(solution)/shard_map/all_to_all | solution.py:279
  30.1 0.0 collective-permute-done.row_a
  30.1 0.0 copy-start.2
  30.1 0.0 collective-permute-done.1.row_b
  30.1 0.0 copy-start.3
  30.1 0.7 pack_corners.1
  30.8 0.0 copy-done.6
  30.8 0.6 collective-permute-start.4
  31.4 4.9 %collective-permute-start.6 = (f32[2,128,128]{2,1,0:T(8,128)S(1)}, f32[2,128,128]{2,1,0:T(8,128)S(1)}, u32[]{:S(2)}, u32[]{:S(2)}) collective-permute-start(f32[2,128,128]{2,1,0:T(8,128)S(1)} %get-tuple-element.34), channel_id=1, source_target_pairs={{1,2},{3,4},{5,6},{7,8},{9,10},{11,12},{13,14},{2,1},{4,3},{6,5},{... | collective-permute-start | bytes 393224 | tf_op jit(solution)/shard_map/ppermute | solution.py:275
  36.3 0.0 collective-permute-done.4.corners_a
  36.3 0.0 copy-start.12
  36.3 3.1 %all-to-all-done.1 = f32[8,16,256]{2,1,0:T(8,128)S(1)} async-done(((f32[8,16,256]{2,1,0:T(8,128)}), f32[8,16,256]{2,1,0:T(8,128)S(1)}, u32[]{:S(2)}, u32[]{:S(2)}) %all-to-all-start.1) | async-done | bytes 131104 | tf_op jit(solution)/shard_map/all_to_all | solution.py:279
  39.5 0.7 broadcast_in_dim.10
  40.2 6.4 %all-to-all-start.2 = ((f32[16,16,256]{2,1,0:T(8,128)}), f32[16,16,256]{2,1,0:T(8,128)S(1)}, u32[]{:S(2)}, u32[]{:S(2)}) async-start(f32[16,16,256]{2,1,0:T(8,128)} %broadcast_in_dim.10), calls=%async_computation.2 | async-start | bytes 524288 | tf_op jit(solution)/shard_map/all_to_all | solution.py:279
  46.6 0.0 collective-permute-done.3.col_b
  46.6 0.0 copy-start.11
  46.6 0.0 collective-permute-done.6.corners_b
  46.6 0.0 copy-start.13
  46.6 0.0 copy-done.10
  46.6 0.0 copy-done.2
  46.7 0.0 copy-done.3
  46.7 0.0 copy-done.12
  46.7 0.6 copy-done.11
  47.3 0.0 copy-done.13
  47.3 12.0 %gradient.1 = (f32[2,2,256,256]{3,2,1,0:T(8,128)}, f32[2,2,64,256]{3,2,1,0:T(8,128)}, f32[2,2,64,256]{3,2,1,0:T(8,128)}, f32[2,256,128]{2,1,0:T(8,128)}, f32[2,2...) custom-call(s32[5]{0:T(128)} %copy-done.6, ...), custom_call_target="tpu_custom_call" | custom-call | flops 3221225472 | bytes 5767168 | tf_op jit(solution)/shard_map/gradient/pallas_call | solution.py:261
  59.4 0.7 collective-permute-start.7
  60.0 2.6 %collective-permute-start.8 = (f32[2,128,128]{2,1,0:T(8,128)}, f32[2,128,128]{2,1,0:T(8,128)S(1)}, u32[]{:S(2)}, u32[]{:S(2)}) collective-permute-start(f32[2,128,128]{2,1,0:T(8,128)} %get-tuple-element.37), channel_id=1, source_target_pairs={{1,2},{3,4},{5,6},{7,8},{9,10},{11,12},{13,14},{2,1},{4,3},{6,5},{... | collective-permute-start | bytes 393224 | tf_op jit(solution)/shard_map/ppermute | solution.py:275
  62.6 0.9 collective-permute-done.7.corners_a
  63.5 4.6 %collective-permute-done.8.corners_b = f32[2,128,128]{2,1,0:T(8,128)S(1)} collective-permute-done((f32[2,128,128]{2,1,0:T(8,128)}, f32[2,128,128]{2,1,0:T(8,128)S(1)}, u32[]{:S(2)}, u32[]{:S(2)}) %collective-permute-start.8) | collective-permute-done | bytes 131104 | tf_op jit(solution)/shard_map/ppermute | solution.py:275
  68.1 0.9 copy-done.4
  69.0 0.9 copy-done.5
  70.0 0.7 margins.1
  70.6 2.5 %collective-permute-start.11 = (f32[2,2,64,256]{3,2,1,0:T(8,128)S(1)}, f32[2,2,64,256]{3,2,1,0:T(8,128)S(1)}, u32[]{:S(2)}, u32[]{:S(2)}) collective-permute-start(f32[2,2,64,256]{3,2,1,0:T(8,128)S(1)} %get-tuple-element.46), channel_id=1, source_target_pairs={{0,16},{32,48},{64,80},{96,112},{128,144},{160,176},{192,208},{224... | collective-permute-start | bytes 786440 | tf_op jit(solution)/shard_map/ppermute | solution.py:275
  73.2 4.4 %collective-permute-start.12 = (f32[2,2,64,256]{3,2,1,0:T(8,128)S(1)}, f32[2,2,64,256]{3,2,1,0:T(8,128)S(1)}, u32[]{:S(2)}, u32[]{:S(2)}) collective-permute-start(f32[2,2,64,256]{3,2,1,0:T(8,128)S(1)} %get-tuple-element.47), channel_id=1, source_target_pairs={{16,32},{48,64},{80,96},{112,128},{144,160},{176,192},{208,224},{3... | collective-permute-start | bytes 786440 | tf_op jit(solution)/shard_map/ppermute | solution.py:275
  77.6 4.1 %collective-permute-start.10 = (f32[2,256,128]{2,1,0:T(8,128)}, f32[2,256,128]{2,1,0:T(8,128)S(1)}, u32[]{:S(2)}, u32[]{:S(2)}) collective-permute-start(f32[2,256,128]{2,1,0:T(8,128)} %get-tuple-element.41), channel_id=1, source_target_pairs={{1,2},{3,4},{5,6},{7,8},{9,10},{11,12},{13,14},{2,1},{4,3},{6,5},{... | collective-permute-start | bytes 786440 | tf_op jit(solution)/shard_map/ppermute | solution.py:275
  81.6 0.1 collective-permute-start.9
  81.7 0.0 all-to-all-done.2
  81.8 0.1 collective-permute-start.13
  81.9 0.0 collective-permute-done.11.row_a
  81.9 7.8 %collective-permute-done.12.row_b = f32[2,2,64,256]{3,2,1,0:T(8,128)S(1)} collective-permute-done((f32[2,2,64,256]{3,2,1,0:T(8,128)S(1)}, f32[2,2,64,256]{3,2,1,0:T(8,128)S(1)}, u32[]{:S(2)}, u32[]{:S(2)}) %collective-permute-start.12) | collective-permute-done | bytes 262176 | tf_op jit(solution)/shard_map/ppermute | solution.py:275
  89.7 2.2 %collective-permute-done.10.col_b = f32[2,256,128]{2,1,0:T(8,128)S(1)} collective-permute-done((f32[2,256,128]{2,1,0:T(8,128)}, f32[2,256,128]{2,1,0:T(8,128)S(1)}, u32[]{:S(2)}, u32[]{:S(2)}) %collective-permute-start.10) | collective-permute-done | bytes 262176 | tf_op jit(solution)/shard_map/ppermute | solution.py:275
  91.9 0.0 collective-permute-done.9.col_a
  91.9 1.2 %copy-done.1 = f32[2,2,256,256]{3,2,1,0:T(8,128)S(1)} copy-done((f32[2,2,256,256]{3,2,1,0:T(8,128)S(1)}, f32[2,2,256,256]{3,2,1,0:T(8,128)}, u32[]{:S(2)}) %copy-start.1) | copy-done | bytes 1048600
  93.1 1.8 %finish.1 = f32[2,2,256,256]{3,2,1,0:T(8,128)} custom-call(s32[5]{0:T(128)S(1)} %copy-done.7, f32[2,2,256,256]{3,2,1,0:T(8,128)S(1)} %copy-done.1, f32[2,256,128]{2,1,0:T(8,128)S(1)} %collective-permute-done.9.col_a, f32[2,256,128]{2,1,0:T(8,128)S(1)} %collective-permute-done.10.col_b, f32[2,2,64,256]{3,2,1,0:T(8,128)S(1)} %collective-permute-done.11.row_a, ...), custom_call_target="tpu_custom_call" | custom-call | bytes 2097152 | tf_op jit(solution)/shard_map/finish/pallas_call | solution.py:261
  94.9 0.0 collective-permute-done.13
  94.9 0.9 fusion
  (12 shorter events, 0.1 us)
Async XLA Ops:
  0.6 5.8 %copy-start.9 = (f32[1,1,2,256,256]{4,3,2,1,0:T(8,128)S(1)}, f32[1,1,2,256,256]{4,3,2,1,0:T(8,128)}, u32[]{:S(2)}) copy-start(f32[1,1,2,256,256]{4,3,2,1,0:T(8,128)} %param.9) | copy-start | bytes 1572868
  1.7 4.8 %collective-permute-start.5 = (f32[256,256]{1,0:T(8,128)S(1)}, f32[256,256]{1,0:T(8,128)S(1)}, u32[]{:S(2)}, u32[]{:S(2)}) collective-permute-start(f32[256,256]{1,0:T(8,128)S(1)} %dynamic-slice_bitcast_fusion), channel_id=1, source_target_pairs={{0,16},{16,0},{1,17},{17,1},{2,18},{18,2},{3,19},{19,3},{4,20},{20... | collective-permute-start | bytes 786440 | tf_op jit(solution)/shard_map/ppermute | solution.py:275
  3.8 1.2 %copy-start = (f32[2,2,256,256]{3,2,1,0:T(8,128)S(1)}, f32[2,2,256,256]{3,2,1,0:T(8,128)}, u32[]{:S(2)}) copy-start(f32[2,2,256,256]{3,2,1,0:T(8,128)} %objects.3) | copy-start | bytes 3145732
  5.1 25.7 %copy-start.6 = (s32[5]{0:T(128)}, s32[5]{0:T(128)S(1)}, u32[]{:S(2)}) copy-start(s32[5]{0:T(128)S(1)} %pad_add_fusion.facts) | copy-start | bytes 64
  5.8 20.1 %collective-permute-start.2 = (f32[2,256,128]{2,1,0:T(8,128)S(1)}, f32[2,256,128]{2,1,0:T(8,128)S(1)}, u32[]{:S(2)}, u32[]{:S(2)}) collective-permute-start(f32[2,256,128]{2,1,0:T(8,128)S(1)} %get-tuple-element.29), channel_id=1, source_target_pairs={{0,1},{2,3},{4,5},{6,7},{8,9},{10,11},{12,13},{14,15},{1,0},{3,2},... | collective-permute-start | bytes 786440 | tf_op jit(solution)/shard_map/ppermute | solution.py:275
  7.2 18.8 %all-to-all-start = ((f32[16,16,256]{2,1,0:T(8,128)}), f32[16,16,256]{2,1,0:T(8,128)S(1)}, u32[]{:S(2)}, u32[]{:S(2)}) async-start(f32[16,16,256]{2,1,0:T(8,128)} %bitcast.6), calls=%async_computation | async-start | bytes 524288 | tf_op jit(solution)/shard_map/all_to_all | solution.py:279
  14.1 16.0 %collective-permute-start = (f32[2,2,64,256]{3,2,1,0:T(8,128)S(1)}, f32[2,2,64,256]{3,2,1,0:T(8,128)S(1)}, u32[]{:S(2)}, u32[]{:S(2)}) collective-permute-start(f32[2,2,64,256]{3,2,1,0:T(8,128)S(1)} %get-tuple-element.27), channel_id=1, source_target_pairs={{0,16},{32,48},{64,80},{96,112},{128,144},{160,176},{192,208},{224... | collective-permute-start | bytes 786440 | tf_op jit(solution)/shard_map/ppermute | solution.py:275
  14.9 15.2 %collective-permute-start.1 = (f32[2,2,64,256]{3,2,1,0:T(8,128)S(1)}, f32[2,2,64,256]{3,2,1,0:T(8,128)S(1)}, u32[]{:S(2)}, u32[]{:S(2)}) collective-permute-start(f32[2,2,64,256]{3,2,1,0:T(8,128)S(1)} %get-tuple-element.28), channel_id=1, source_target_pairs={{16,32},{48,64},{80,96},{112,128},{144,160},{176,192},{208,224},{3... | collective-permute-start | bytes 786440 | tf_op jit(solution)/shard_map/ppermute | solution.py:275
  23.7 22.9 %collective-permute-start.3 = (f32[2,256,128]{2,1,0:T(8,128)S(1)}, f32[2,256,128]{2,1,0:T(8,128)S(1)}, u32[]{:S(2)}, u32[]{:S(2)}) collective-permute-start(f32[2,256,128]{2,1,0:T(8,128)S(1)} %get-tuple-element.30), channel_id=1, source_target_pairs={{1,2},{3,4},{5,6},{7,8},{9,10},{11,12},{13,14},{2,1},{4,3},{6,5},{... | collective-permute-start | bytes 786440 | tf_op jit(solution)/shard_map/ppermute | solution.py:275
  26.0 20.7 %copy-start.10 = (f32[2,256,128]{2,1,0:T(8,128)}, f32[2,256,128]{2,1,0:T(8,128)S(1)}, u32[]{:S(2)}) copy-start(f32[2,256,128]{2,1,0:T(8,128)S(1)} %collective-permute-done.2.col_a) | copy-start | bytes 786436
  26.7 12.8 %all-to-all-start.1 = ((f32[8,16,256]{2,1,0:T(8,128)}), f32[8,16,256]{2,1,0:T(8,128)S(1)}, u32[]{:S(2)}, u32[]{:S(2)}) async-start(f32[8,16,256]{2,1,0:T(8,128)} %broadcast_in_dim.9), calls=%async_computation.1 | async-start | bytes 262144 | tf_op jit(solution)/shard_map/all_to_all | solution.py:279
  30.1 16.6 %copy-start.2 = (f32[2,2,64,256]{3,2,1,0:T(8,128)}, f32[2,2,64,256]{3,2,1,0:T(8,128)S(1)}, u32[]{:S(2)}) copy-start(f32[2,2,64,256]{3,2,1,0:T(8,128)S(1)} %collective-permute-done.row_a) | copy-start | bytes 786436
  30.1 16.5 %copy-start.3 = (f32[2,2,64,256]{3,2,1,0:T(8,128)}, f32[2,2,64,256]{3,2,1,0:T(8,128)S(1)}, u32[]{:S(2)}) copy-start(f32[2,2,64,256]{3,2,1,0:T(8,128)S(1)} %collective-permute-done.1.row_b) | copy-start | bytes 786436
  30.8 5.5 %collective-permute-start.4 = (f32[2,128,128]{2,1,0:T(8,128)S(1)}, f32[2,128,128]{2,1,0:T(8,128)S(1)}, u32[]{:S(2)}, u32[]{:S(2)}) collective-permute-start(f32[2,128,128]{2,1,0:T(8,128)S(1)} %get-tuple-element.31), channel_id=1, source_target_pairs={{0,1},{2,3},{4,5},{6,7},{8,9},{10,11},{12,13},{14,15},{1,0},{3,2},... | collective-permute-start | bytes 393224 | tf_op jit(solution)/shard_map/ppermute | solution.py:275
  31.4 15.2 %collective-permute-start.6 = (f32[2,128,128]{2,1,0:T(8,128)S(1)}, f32[2,128,128]{2,1,0:T(8,128)S(1)}, u32[]{:S(2)}, u32[]{:S(2)}) collective-permute-start(f32[2,128,128]{2,1,0:T(8,128)S(1)} %get-tuple-element.34), channel_id=1, source_target_pairs={{1,2},{3,4},{5,6},{7,8},{9,10},{11,12},{13,14},{2,1},{4,3},{6,5},{... | collective-permute-start | bytes 393224 | tf_op jit(solution)/shard_map/ppermute | solution.py:275
  36.3 10.4 %copy-start.12 = (f32[2,128,128]{2,1,0:T(8,128)}, f32[2,128,128]{2,1,0:T(8,128)S(1)}, u32[]{:S(2)}) copy-start(f32[2,128,128]{2,1,0:T(8,128)S(1)} %collective-permute-done.4.corners_a) | copy-start | bytes 393220
  40.2 41.6 %all-to-all-start.2 = ((f32[16,16,256]{2,1,0:T(8,128)}), f32[16,16,256]{2,1,0:T(8,128)S(1)}, u32[]{:S(2)}, u32[]{:S(2)}) async-start(f32[16,16,256]{2,1,0:T(8,128)} %broadcast_in_dim.10), calls=%async_computation.2 | async-start | bytes 524288 | tf_op jit(solution)/shard_map/all_to_all | solution.py:279
  46.6 0.7 copy-start.11
  46.6 0.7 copy-start.13
  47.3 20.7 %copy-start.7 = (s32[5]{0:T(128)S(1)}, s32[5]{0:T(128)}, u32[]{:S(2)}) copy-start(s32[5]{0:T(128)} %copy-done.6) | copy-start | bytes 64
  59.4 4.1 %collective-permute-start.7 = (f32[2,128,128]{2,1,0:T(8,128)}, f32[2,128,128]{2,1,0:T(8,128)S(1)}, u32[]{:S(2)}, u32[]{:S(2)}) collective-permute-start(f32[2,128,128]{2,1,0:T(8,128)} %get-tuple-element.36), channel_id=1, source_target_pairs={{0,1},{2,3},{4,5},{6,7},{8,9},{10,11},{12,13},{14,15},{1,0},{3,2},... | collective-permute-start | bytes 393224 | tf_op jit(solution)/shard_map/ppermute | solution.py:275
  60.0 8.0 %collective-permute-start.8 = (f32[2,128,128]{2,1,0:T(8,128)}, f32[2,128,128]{2,1,0:T(8,128)S(1)}, u32[]{:S(2)}, u32[]{:S(2)}) collective-permute-start(f32[2,128,128]{2,1,0:T(8,128)} %get-tuple-element.37), channel_id=1, source_target_pairs={{1,2},{3,4},{5,6},{7,8},{9,10},{11,12},{13,14},{2,1},{4,3},{6,5},{... | collective-permute-start | bytes 393224 | tf_op jit(solution)/shard_map/ppermute | solution.py:275
  68.1 1.0 copy-start.4
  69.0 0.9 copy-start.5
  70.6 11.2 %collective-permute-start.11 = (f32[2,2,64,256]{3,2,1,0:T(8,128)S(1)}, f32[2,2,64,256]{3,2,1,0:T(8,128)S(1)}, u32[]{:S(2)}, u32[]{:S(2)}) collective-permute-start(f32[2,2,64,256]{3,2,1,0:T(8,128)S(1)} %get-tuple-element.46), channel_id=1, source_target_pairs={{0,16},{32,48},{64,80},{96,112},{128,144},{160,176},{192,208},{224... | collective-permute-start | bytes 786440 | tf_op jit(solution)/shard_map/ppermute | solution.py:275
  73.2 16.6 %collective-permute-start.12 = (f32[2,2,64,256]{3,2,1,0:T(8,128)S(1)}, f32[2,2,64,256]{3,2,1,0:T(8,128)S(1)}, u32[]{:S(2)}, u32[]{:S(2)}) collective-permute-start(f32[2,2,64,256]{3,2,1,0:T(8,128)S(1)} %get-tuple-element.47), channel_id=1, source_target_pairs={{16,32},{48,64},{80,96},{112,128},{144,160},{176,192},{208,224},{3... | collective-permute-start | bytes 786440 | tf_op jit(solution)/shard_map/ppermute | solution.py:275
  77.6 14.3 %collective-permute-start.10 = (f32[2,256,128]{2,1,0:T(8,128)}, f32[2,256,128]{2,1,0:T(8,128)S(1)}, u32[]{:S(2)}, u32[]{:S(2)}) collective-permute-start(f32[2,256,128]{2,1,0:T(8,128)} %get-tuple-element.41), channel_id=1, source_target_pairs={{1,2},{3,4},{5,6},{7,8},{9,10},{11,12},{13,14},{2,1},{4,3},{6,5},{... | collective-permute-start | bytes 786440 | tf_op jit(solution)/shard_map/ppermute | solution.py:275
  81.6 10.3 %collective-permute-start.9 = (f32[2,256,128]{2,1,0:T(8,128)}, f32[2,256,128]{2,1,0:T(8,128)S(1)}, u32[]{:S(2)}, u32[]{:S(2)}) collective-permute-start(f32[2,256,128]{2,1,0:T(8,128)} %get-tuple-element.40), channel_id=1, source_target_pairs={{0,1},{2,3},{4,5},{6,7},{8,9},{10,11},{12,13},{14,15},{1,0},{3,2},... | collective-permute-start | bytes 786440 | tf_op jit(solution)/shard_map/ppermute | solution.py:275
  81.8 13.1 %collective-permute-start.13 = (f32[256,256]{1,0:T(8,128)S(1)}, f32[256,256]{1,0:T(8,128)S(1)}, u32[]{:S(2)}, u32[]{:S(2)}) collective-permute-start(f32[256,256]{1,0:T(8,128)S(1)} %bitcast.17), channel_id=1, source_target_pairs={{0,16},{16,0},{1,17},{17,1},{2,18},{18,2},{3,19},{19,3},{4,20},{20... | collective-permute-start | bytes 786440 | tf_op jit(solution)/shard_map/ppermute | solution.py:275
  91.9 1.2 %copy-start.1 = (f32[2,2,256,256]{3,2,1,0:T(8,128)S(1)}, f32[2,2,256,256]{3,2,1,0:T(8,128)}, u32[]{:S(2)}) copy-start(f32[2,2,256,256]{3,2,1,0:T(8,128)} %get-tuple-element.35.center) | copy-start | bytes 3145732
  93.1 1.8 %copy-start.8 = (f32[2,256,256]{2,1,0:T(8,128)S(1)}, f32[2,256,256]{2,1,0:T(8,128)}, u32[]{:S(2)}) copy-start(f32[2,256,256]{2,1,0:T(8,128)} %probe.1) | copy-start | bytes 1572868

commit v4 on v3

--- a/solution.py
+++ b/solution.py
@@ -118,7 +118,7 @@
 
 def gradient(
     facts, objects, row_a, row_b, col_a, col_b, corners_a, corners_b, probe, amp, mats,
-    center_out, north_out, south_out, col_a_out, col_b_out, corners_a_out, corners_b_out, probe_out,
+    center_out, row_a_out, row_b_out, col_a_out, col_b_out, corners_a_out, corners_b_out, probe_out,
     ext, grad, sides, sides_out, probe_in, amp_in, mats_in, probe_grad, arrive, leave,
 ):
     row_odd, col_odd = facts[3], facts[4]
@@ -149,8 +149,8 @@
             incoming.insert(3, (src, sides.at[side, :, rows]))
             outgoing.append((sides_out.at[side, :, rows], dst))
     outgoing += [
-        (grad.at[:, :, upper, across], north_out),
-        (grad.at[:, :, lower, across], south_out),
+        (grad.at[:, :, beyond(row_odd), across], row_a_out),
+        (grad.at[:, :, beyond(1 - row_odd), across], row_b_out),
         (ext.at[:, :, middle, across], center_out),
     ]
     coming = [pltpu.make_async_copy(*pair, arrive.at[i]) for i, pair in enumerate(incoming)]
@@ -221,7 +221,7 @@
 
 def edge_columns(col_odd, col_a, col_b, s, start, size):
     keep = first_half((size, 2 * HALO))
-    a, b = col_a[s, pl.ds(start, size)], col_b[s, pl.ds(start, size)]
+    a, b = (x[s] if x.shape[1] == size else x[s, pl.ds(start, size)] for x in (col_a, col_b))
     w, e = either(col_odd, b, a), either(col_odd, a, b)
     zero = jnp.zeros_like(w)
     wr, er = pltpu.roll(w, HALO, 1), pltpu.roll(e, HALO, 1)
@@ -231,29 +231,38 @@
     )
 
 
-def add_margins(facts, north, south, corners_a, corners_b, row_a, row_b):
-    row_odd, col_odd = facts[3], facts[4]
-    for s in range(2):
-        upper = edge_columns(col_odd, corners_a, corners_b, s, 0, HALO)
-        lower = edge_columns(col_odd, corners_a, corners_b, s, HALO, HALO)
+def relay(facts, corners_a, corners_b, row_a, row_b):
+    row_odd = facts[3]
+    for side, src in ((0, corners_a), (1, corners_b)):
+        for s in range(2):
+            upper, lower = src[s, :HALO], src[s, HALO:]
+            row_a[side, s] = either(row_odd, lower, upper)
+            row_b[side, s] = either(row_odd, upper, lower)
+
+
+def add_sides(facts, center, col_a, col_b, row_a, row_b, tile):
+    row_odd, col_odd = facts[3], facts[4]
+    for s in range(2):
+        edges = edge_columns(col_odd, col_a, col_b, s, 0, TILE)
         for k in range(2):
             for half, cols in enumerate((slice(0, 128), slice(128, 256))):
-                up = north[s, k, :, cols] + upper[k][half]
-                down = south[s, k, :, cols] + lower[k][half]
-                row_a[s, k, :, cols] = either(row_odd, down, up)
-                row_b[s, k, :, cols] = either(row_odd, up, down)
-
-
-def finish(facts, center, col_a, col_b, row_a, row_b, new_objects):
-    row_odd, col_odd = facts[3], facts[4]
-    for s in range(2):
-        for k, edges in enumerate(edge_columns(col_odd, col_a, col_b, s, 0, TILE)):
-            for cols, edge in zip((slice(0, 128), slice(128, 256)), edges):
-                value = center[s, k, :, cols] + edge
+                value = center[s, k, :, cols] + edges[k][half]
                 a, b = row_a[s, k, :, cols], row_b[s, k, :, cols]
-                new_objects[s, k, :HALO, cols] = value[:HALO] + either(row_odd, b, a)
-                new_objects[s, k, HALO : TILE - HALO, cols] = value[HALO : TILE - HALO]
-                new_objects[s, k, TILE - HALO :, cols] = value[TILE - HALO :] + either(row_odd, a, b)
+                tile[s, k, :HALO, cols] = value[:HALO] + either(row_odd, b, a)
+                tile[s, k, HALO : TILE - HALO, cols] = value[HALO : TILE - HALO]
+                tile[s, k, TILE - HALO :, cols] = value[TILE - HALO :] + either(row_odd, a, b)
+
+
+def add_corners(facts, tile, relayed_a, relayed_b, new_objects):
+    row_odd, col_odd = facts[3], facts[4]
+    for s in range(2):
+        a, b = (edge_columns(col_odd, x[0], x[1], s, 0, HALO) for x in (relayed_a, relayed_b))
+        for k in range(2):
+            for half, cols in enumerate((slice(0, 128), slice(128, 256))):
+                first, last = a[k][half], b[k][half]
+                new_objects[s, k, :HALO, cols] = tile[s, k, :HALO, cols] + either(row_odd, last, first)
+                new_objects[s, k, HALO : TILE - HALO, cols] = tile[s, k, HALO : TILE - HALO, cols]
+                new_objects[s, k, TILE - HALO :, cols] = tile[s, k, TILE - HALO :, cols] + either(row_odd, first, last)
 
 
 def call(body, outs, *args, specs=None, scratch=(), flops=0, limit=2, name=None):
@@ -307,7 +316,7 @@
 
 def shards(objects, probe, prev_partial, offsets, counts, amplitudes):
     strip, column, corners = (2, 2, HALO, TILE), (2, TILE, 2 * HALO), (2, 2 * HALO, 2 * HALO)
-    tile = (2, 2, TILE, TILE)
+    tile, strip_corners = (2, 2, TILE, TILE), (2, 2, HALO, 2 * HALO)
     facts = jnp.concatenate([
         offsets.reshape(2), counts.reshape(1),
         jnp.stack([lax.axis_index("row_2"), lax.axis_index("col_1") % 2]).astype(jnp.int32),
@@ -320,7 +329,7 @@
     corners_b, corners_a = exchanged(sent_b, COL, 1), exchanged(sent_a, COL, 0)
     deep = depth_sum(scattered, col_a)
     corners_a, deep = lax.optimization_barrier((corners_a, deep))
-    center, north, south, col_a_part, col_b_part, corners_a_part, corners_b_part, partial = call(
+    center, row_a_part, row_b_part, col_a_part, col_b_part, corners_a_part, corners_b_part, partial = call(
         gradient,
         [tile, strip, strip, column, column, corners, corners, (2, WIN, WIN)],
         facts, objects, row_a, row_b, col_a, col_b, corners_a, corners_b, probe,
@@ -336,13 +345,12 @@
         name="gradient",
     )
     corners_b, corners_a = exchanged(corners_b_part, COL, 1), exchanged(corners_a_part, COL, 0)
-    corners_a, corners_b, col_a_part, col_b_part = lax.optimization_barrier(
-        (corners_a, corners_b, col_a_part, col_b_part)
-    )
-    row_a, row_b = call(add_margins, [strip] * 2, facts, north, south, corners_a, corners_b, name="margins")
-    row_b, row_a = exchanged(row_b, ROW, 1), exchanged(row_a, ROW, 0)
+    row_b, row_a = exchanged(row_b_part, ROW, 1), exchanged(row_a_part, ROW, 0)
+    sent_a, sent_b = call(relay, [strip_corners] * 2, facts, corners_a, corners_b, name="relay")
+    relayed_b, relayed_a = exchanged(sent_b, ROW, 1), exchanged(sent_a, ROW, 0)
     col_b, col_a = exchanged(col_b_part, COL, 1), exchanged(col_a_part, COL, 0)
-    (new_objects,) = call(finish, [tile], facts, center, col_a, col_b, row_a, row_b, name="finish")
+    (added,) = call(add_sides, [tile], facts, center, col_a, col_b, row_a, row_b, name="add_sides")
+    (new_objects,) = call(add_corners, [tile], facts, added, relayed_a, relayed_b, name="add_corners")
     rate = PROBE_RATE / math.sqrt(lax.axis_size(ROW) * lax.axis_size(COL))
     total = gather_sum(deep, partial)
     new_probe = probe - rate * total

time: 96.5 us -> 93.4 us (0.968)
  waiting for transfers between devices: 18.6 us -> 7.41 us
  starting transfers between devices: 49.8 us -> 58.7 us
  local copies, waits for them, and re-layouts: 7.5 us -> 5.61 us
    ppermute x14 -> x16, waiting for transfers between devices: 15.5 us -> 4.27 us  [exchanged(): return lax.ppermute(value, axis, pairs + [(j, i) for i, j in pairs])]
    ppermute x14 -> x16, starting transfers between devices: 33.1 us -> 42.1 us  [exchanged(): return lax.ppermute(value, axis, pairs + [(j, i) for i, j in pairs])]
    unnamed x28 -> x24, local copies, waits for them, and re-layouts: 5.06 us -> 3.18 us
    pallas_call x5 -> x6, Pallas kernels: 15.9 us -> 16.4 us  [call(): pl.pallas_call(body, out_shape=[jax.ShapeDtypeStruct(o, jnp.float32) for...]
  transfers between devices with their start and end apart: 17 -> 19, of which waited for: 5 -> 3; matrix products, arithmetic and copies ran while one was open for 3% -> 3% of each run, Pallas kernels for 17% -> 18%
where the time goes in v4:
time: 93.4 us; the launch traced here: 92.3 us
  starting transfers between devices  58.7 us (63%)
  Pallas kernels  16.4 us (18%)
  waiting for transfers between devices  7.41 us (8%)
  local copies, waits for them, and re-layouts  5.61 us (6%)
  other arithmetic  2.41 us (3%)
  between operations  1.64 us (2%)
    ppermute x16, starting transfers between devices, exchanged(): return lax.ppermute(value, axis, pairs + [(j, i) for i, j in pairs])  42.1 us
    all_to_all x3, starting transfers between devices, swap(): return lax.all_to_all(value, axes, 0, 0, tiled=True)  16.7 us
    pallas_call x6, Pallas kernels, call(): pl.pallas_call(body, out_shape=[jax.ShapeDtypeStruct(o, jnp.float32) for...  16.4 us
    ppermute x16, waiting for transfers between devices, exchanged(): return lax.ppermute(value, axis, pairs + [(j, i) for i, j in pairs])  4.27 us
    unnamed x24, local copies, waits for them, and re-layouts  3.18 us
    all_to_all x3, waiting for transfers between devices, swap(): return lax.all_to_all(value, axes, 0, 0, tiled=True)  3.14 us
  transfers between devices with their start and end apart: 19, of which 3 were waited for; matrix products, arithmetic and copies ran while one was open for 3% of the time, Pallas kernels for 18%

profile of v4, /device:TPU:31, one launch (start us, length us, event | category | flops | bytes accessed | tf_op | source)
XLA Modules:
  0.0 92.3 jit_solution(13121001526008918719)
XLA Ops:
  0.6 0.0 copy-start.7
  0.6 1.0 %dynamic-slice_bitcast_fusion = f32[256,256]{1,0:T(8,128)S(1)} fusion(f32[1,1,2,256,256]{4,3,2,1,0:T(8,128)} %param.9, s32[]{:T(128)S(6)} %select_n.28), kind=kLoop, calls=%fused_computation.5 | loop fusion | bytes 524292 | tf_op jit(solution)/shard_map/jit(dynamic_index_in_dim)/squeeze | solution.py:298
  1.7 0.8 collective-permute-start.5
  3.1 0.7 pad_add_fusion.facts
  3.8 1.2 %copy-done = f32[2,2,256,256]{3,2,1,0:T(8,128)S(1)} copy-done((f32[2,2,256,256]{3,2,1,0:T(8,128)S(1)}, f32[2,2,256,256]{3,2,1,0:T(8,128)}, u32[]{:S(2)}) %copy-start) | copy-done | bytes 1048600
  5.1 0.8 pack_sides.1
  5.8 0.6 collective-permute-start.2
  6.4 0.0 collective-permute-done.5
  6.5 0.0 copy-done.7
  6.5 0.7 bitcast_add_fusion
  7.2 6.9 %all-to-all-start = ((f32[16,16,256]{2,1,0:T(8,128)}), f32[16,16,256]{2,1,0:T(8,128)S(1)}, u32[]{:S(2)}, u32[]{:S(2)}) async-start(f32[16,16,256]{2,1,0:T(8,128)} %bitcast.6), calls=%async_computation | async-start | bytes 524288 | tf_op jit(solution)/shard_map/all_to_all | solution.py:288
  14.1 0.9 collective-permute-start
  14.9 8.7 %collective-permute-start.1 = (f32[2,2,64,256]{3,2,1,0:T(8,128)S(1)}, f32[2,2,64,256]{3,2,1,0:T(8,128)S(1)}, u32[]{:S(2)}, u32[]{:S(2)}) collective-permute-start(f32[2,2,64,256]{3,2,1,0:T(8,128)S(1)} %get-tuple-element.24), channel_id=1, source_target_pairs={{16,32},{48,64},{80,96},{112,128},{144,160},{176,192},{208,224},{3... | collective-permute-start | bytes 786440 | tf_op jit(solution)/shard_map/ppermute | solution.py:284
  23.7 2.3 %collective-permute-start.3 = (f32[2,256,128]{2,1,0:T(8,128)S(1)}, f32[2,256,128]{2,1,0:T(8,128)S(1)}, u32[]{:S(2)}, u32[]{:S(2)}) collective-permute-start(f32[2,256,128]{2,1,0:T(8,128)S(1)} %get-tuple-element.26), channel_id=1, source_target_pairs={{1,2},{3,4},{5,6},{7,8},{9,10},{11,12},{13,14},{2,1},{4,3},{6,5},{... | collective-permute-start | bytes 786440 | tf_op jit(solution)/shard_map/ppermute | solution.py:284
  25.9 0.0 collective-permute-done.2.col_a
  26.0 0.0 copy-start.8
  26.0 0.0 all-to-all-done
  26.0 0.7 broadcast_in_dim.9
  26.7 3.4 %all-to-all-start.1 = ((f32[8,16,256]{2,1,0:T(8,128)}), f32[8,16,256]{2,1,0:T(8,128)S(1)}, u32[]{:S(2)}, u32[]{:S(2)}) async-start(f32[8,16,256]{2,1,0:T(8,128)} %broadcast_in_dim.9), calls=%async_computation.1 | async-start | bytes 262144 | tf_op jit(solution)/shard_map/all_to_all | solution.py:288
  30.1 0.0 collective-permute-done.row_a
  30.1 0.0 copy-start.2
  30.1 0.0 collective-permute-done.1.row_b
  30.1 0.0 copy-start.3
  30.1 0.7 pack_corners.1
  30.8 0.0 copy-done.4
  30.8 0.6 collective-permute-start.4
  31.4 4.9 %collective-permute-start.6 = (f32[2,128,128]{2,1,0:T(8,128)S(1)}, f32[2,128,128]{2,1,0:T(8,128)S(1)}, u32[]{:S(2)}, u32[]{:S(2)}) collective-permute-start(f32[2,128,128]{2,1,0:T(8,128)S(1)} %get-tuple-element.30), channel_id=1, source_target_pairs={{1,2},{3,4},{5,6},{7,8},{9,10},{11,12},{13,14},{2,1},{4,3},{6,5},{... | collective-permute-start | bytes 393224 | tf_op jit(solution)/shard_map/ppermute | solution.py:284
  36.3 0.0 collective-permute-done.4.corners_a
  36.3 0.0 copy-start.10
  36.3 3.1 %all-to-all-done.1 = f32[8,16,256]{2,1,0:T(8,128)S(1)} async-done(((f32[8,16,256]{2,1,0:T(8,128)}), f32[8,16,256]{2,1,0:T(8,128)S(1)}, u32[]{:S(2)}, u32[]{:S(2)}) %all-to-all-start.1) | async-done | bytes 131104 | tf_op jit(solution)/shard_map/all_to_all | solution.py:288
  39.5 0.7 broadcast_in_dim.10
  40.2 6.4 %all-to-all-start.2 = ((f32[16,16,256]{2,1,0:T(8,128)}), f32[16,16,256]{2,1,0:T(8,128)S(1)}, u32[]{:S(2)}, u32[]{:S(2)}) async-start(f32[16,16,256]{2,1,0:T(8,128)} %broadcast_in_dim.10), calls=%async_computation.2 | async-start | bytes 524288 | tf_op jit(solution)/shard_map/all_to_all | solution.py:288
  46.6 0.0 collective-permute-done.3.col_b
  46.6 0.0 copy-start.9
  46.6 0.0 collective-permute-done.6.corners_b
  46.6 0.0 copy-start.11
  46.7 0.6 copy-done.9
  47.3 0.0 copy-done.11
  47.4 12.0 %gradient.1 = (f32[2,2,256,256]{3,2,1,0:T(8,128)}, f32[2,2,64,256]{3,2,1,0:T(8,128)}, f32[2,2,64,256]{3,2,1,0:T(8,128)}, f32[2,256,128]{2,1,0:T(8,128)}, f32[2,2...) custom-call(s32[5]{0:T(128)} %copy-done.4, ...), custom_call_target="tpu_custom_call" | custom-call | flops 3221225472 | bytes 5767168 | tf_op jit(solution)/shard_map/gradient/pallas_call | solution.py:270
  59.4 0.7 collective-permute-start.11
  60.0 0.9 collective-permute-start.7
  60.9 2.0 %collective-permute-start.8 = (f32[2,256,128]{2,1,0:T(8,128)}, f32[2,256,128]{2,1,0:T(8,128)S(1)}, u32[]{:S(2)}, u32[]{:S(2)}) collective-permute-start(f32[2,256,128]{2,1,0:T(8,128)} %get-tuple-element.33), channel_id=1, source_target_pairs={{1,2},{3,4},{5,6},{7,8},{9,10},{11,12},{13,14},{2,1},{4,3},{6,5},{... | collective-permute-start | bytes 786440 | tf_op jit(solution)/shard_map/ppermute | solution.py:284
  62.9 5.4 %collective-permute-start.12 = (f32[2,128,128]{2,1,0:T(8,128)}, f32[2,128,128]{2,1,0:T(8,128)S(1)}, u32[]{:S(2)}, u32[]{:S(2)}) collective-permute-start(f32[2,128,128]{2,1,0:T(8,128)} %get-tuple-element.37), channel_id=1, source_target_pairs={{1,2},{3,4},{5,6},{7,8},{9,10},{11,12},{13,14},{2,1},{4,3},{6,5},{... | collective-permute-start | bytes 393224 | tf_op jit(solution)/shard_map/ppermute | solution.py:284
  68.3 2.2 %collective-permute-start.9 = (f32[2,2,64,256]{3,2,1,0:T(8,128)}, f32[2,2,64,256]{3,2,1,0:T(8,128)S(1)}, u32[]{:S(2)}, u32[]{:S(2)}) collective-permute-start(f32[2,2,64,256]{3,2,1,0:T(8,128)} %get-tuple-element.34), channel_id=1, source_target_pairs={{0,16},{32,48},{64,80},{96,112},{128,144},{160,176},{192,208},{224... | collective-permute-start | bytes 786440 | tf_op jit(solution)/shard_map/ppermute | solution.py:284
  70.5 0.0 collective-permute-done.11.corners_a
  70.5 3.9 %collective-permute-start.10 = (f32[2,2,64,256]{3,2,1,0:T(8,128)}, f32[2,2,64,256]{3,2,1,0:T(8,128)S(1)}, u32[]{:S(2)}, u32[]{:S(2)}) collective-permute-start(f32[2,2,64,256]{3,2,1,0:T(8,128)} %get-tuple-element.35), channel_id=1, source_target_pairs={{16,32},{48,64},{80,96},{112,128},{144,160},{176,192},{208,224},{3... | collective-permute-start | bytes 786440 | tf_op jit(solution)/shard_map/ppermute | solution.py:284
  74.5 0.0 all-to-all-done.2
  74.5 0.0 collective-permute-done.12.corners_b
  74.5 2.2 %collective-permute-start.15 = (f32[256,256]{1,0:T(8,128)S(1)}, f32[256,256]{1,0:T(8,128)S(1)}, u32[]{:S(2)}, u32[]{:S(2)}) collective-permute-start(f32[256,256]{1,0:T(8,128)S(1)} %bitcast.17), channel_id=1, source_target_pairs={{0,16},{16,0},{1,17},{17,1},{2,18},{18,2},{3,19},{19,3},{4,20},{20... | collective-permute-start | bytes 786440 | tf_op jit(solution)/shard_map/ppermute | solution.py:284
  76.7 0.6 relay.1
  77.3 0.0 collective-permute-done.7.col_a
  77.3 0.1 collective-permute-start.13
  77.4 0.0 collective-permute-done.8.col_b
  77.4 6.0 %collective-permute-start.14 = (f32[2,2,64,128]{3,2,1,0:T(8,128)S(1)}, f32[2,2,64,128]{3,2,1,0:T(8,128)S(1)}, u32[]{:S(2)}, u32[]{:S(2)}) collective-permute-start(f32[2,2,64,128]{3,2,1,0:T(8,128)S(1)} %get-tuple-element.39), channel_id=1, source_target_pairs={{16,32},{48,64},{80,96},{112,128},{144,160},{176,192},{208,224},{3... | collective-permute-start | bytes 393224 | tf_op jit(solution)/shard_map/ppermute | solution.py:284
  83.4 0.0 collective-permute-done.9.row_a
  83.4 1.1 %collective-permute-done.10.row_b = f32[2,2,64,256]{3,2,1,0:T(8,128)S(1)} collective-permute-done((f32[2,2,64,256]{3,2,1,0:T(8,128)}, f32[2,2,64,256]{3,2,1,0:T(8,128)S(1)}, u32[]{:S(2)}, u32[]{:S(2)}) %collective-permute-start.10) | collective-permute-done | bytes 262176 | tf_op jit(solution)/shard_map/ppermute | solution.py:284
  84.5 1.2 %copy-done.1 = f32[2,2,256,256]{3,2,1,0:T(8,128)S(1)} copy-done((f32[2,2,256,256]{3,2,1,0:T(8,128)S(1)}, f32[2,2,256,256]{3,2,1,0:T(8,128)}, u32[]{:S(2)}) %copy-start.1) | copy-done | bytes 1048600
  85.8 0.8 add_sides.1.tile
  86.5 0.0 copy-start.6
  86.6 0.0 collective-permute-done.13.relayed_a
  86.6 3.1 %collective-permute-done.14.relayed_b = f32[2,2,64,128]{3,2,1,0:T(8,128)S(1)} collective-permute-done((f32[2,2,64,128]{3,2,1,0:T(8,128)S(1)}, f32[2,2,64,128]{3,2,1,0:T(8,128)S(1)}, u32[]{:S(2)}, u32[]{:S(2)}) %collective-permute-start.14) | collective-permute-done | bytes 131104 | tf_op jit(solution)/shard_map/ppermute | solution.py:284
  89.7 1.7 %add_corners.1 = f32[2,2,256,256]{3,2,1,0:T(8,128)} custom-call(s32[5]{0:T(128)S(1)} %copy-done.5, f32[2,2,256,256]{3,2,1,0:T(8,128)S(1)} %add_sides.1.tile, f32[2,2,64,128]{3,2,1,0:T(8,128)S(1)} %collective-permute-done.13.relayed_a, f32[2,2,64,128]{3,2,1,0:T(8,128)S(1)} %collective-permute-done.14.relayed_b), custom_call_target="tpu_custom_call" | custom-call | bytes 2097152 | tf_op jit(solution)/shard_map/add_corners/pallas_call | solution.py:270
  91.3 0.0 collective-permute-done.15
  91.4 0.9 fusion
  (13 shorter events, 0.1 us)
Async XLA Ops:
  0.6 5.8 %copy-start.7 = (f32[1,1,2,256,256]{4,3,2,1,0:T(8,128)S(1)}, f32[1,1,2,256,256]{4,3,2,1,0:T(8,128)}, u32[]{:S(2)}) copy-start(f32[1,1,2,256,256]{4,3,2,1,0:T(8,128)} %param.9) | copy-start | bytes 1572868
  1.7 4.8 %collective-permute-start.5 = (f32[256,256]{1,0:T(8,128)S(1)}, f32[256,256]{1,0:T(8,128)S(1)}, u32[]{:S(2)}, u32[]{:S(2)}) collective-permute-start(f32[256,256]{1,0:T(8,128)S(1)} %dynamic-slice_bitcast_fusion), channel_id=1, source_target_pairs={{0,16},{16,0},{1,17},{17,1},{2,18},{18,2},{3,19},{19,3},{4,20},{20... | collective-permute-start | bytes 786440 | tf_op jit(solution)/shard_map/ppermute | solution.py:284
  3.8 1.2 %copy-start = (f32[2,2,256,256]{3,2,1,0:T(8,128)S(1)}, f32[2,2,256,256]{3,2,1,0:T(8,128)}, u32[]{:S(2)}) copy-start(f32[2,2,256,256]{3,2,1,0:T(8,128)} %objects.3) | copy-start | bytes 3145732
  5.1 25.7 %copy-start.4 = (s32[5]{0:T(128)}, s32[5]{0:T(128)S(1)}, u32[]{:S(2)}) copy-start(s32[5]{0:T(128)S(1)} %pad_add_fusion.facts) | copy-start | bytes 64
  5.8 20.1 %collective-permute-start.2 = (f32[2,256,128]{2,1,0:T(8,128)S(1)}, f32[2,256,128]{2,1,0:T(8,128)S(1)}, u32[]{:S(2)}, u32[]{:S(2)}) collective-permute-start(f32[2,256,128]{2,1,0:T(8,128)S(1)} %get-tuple-element.25), channel_id=1, source_target_pairs={{0,1},{2,3},{4,5},{6,7},{8,9},{10,11},{12,13},{14,15},{1,0},{3,2},... | collective-permute-start | bytes 786440 | tf_op jit(solution)/shard_map/ppermute | solution.py:284
  7.2 18.8 %all-to-all-start = ((f32[16,16,256]{2,1,0:T(8,128)}), f32[16,16,256]{2,1,0:T(8,128)S(1)}, u32[]{:S(2)}, u32[]{:S(2)}) async-start(f32[16,16,256]{2,1,0:T(8,128)} %bitcast.6), calls=%async_computation | async-start | bytes 524288 | tf_op jit(solution)/shard_map/all_to_all | solution.py:288
  14.1 16.0 %collective-permute-start = (f32[2,2,64,256]{3,2,1,0:T(8,128)S(1)}, f32[2,2,64,256]{3,2,1,0:T(8,128)S(1)}, u32[]{:S(2)}, u32[]{:S(2)}) collective-permute-start(f32[2,2,64,256]{3,2,1,0:T(8,128)S(1)} %get-tuple-element.23), channel_id=1, source_target_pairs={{0,16},{32,48},{64,80},{96,112},{128,144},{160,176},{192,208},{224... | collective-permute-start | bytes 786440 | tf_op jit(solution)/shard_map/ppermute | solution.py:284
  14.9 15.2 %collective-permute-start.1 = (f32[2,2,64,256]{3,2,1,0:T(8,128)S(1)}, f32[2,2,64,256]{3,2,1,0:T(8,128)S(1)}, u32[]{:S(2)}, u32[]{:S(2)}) collective-permute-start(f32[2,2,64,256]{3,2,1,0:T(8,128)S(1)} %get-tuple-element.24), channel_id=1, source_target_pairs={{16,32},{48,64},{80,96},{112,128},{144,160},{176,192},{208,224},{3... | collective-permute-start | bytes 786440 | tf_op jit(solution)/shard_map/ppermute | solution.py:284
  23.7 22.9 %collective-permute-start.3 = (f32[2,256,128]{2,1,0:T(8,128)S(1)}, f32[2,256,128]{2,1,0:T(8,128)S(1)}, u32[]{:S(2)}, u32[]{:S(2)}) collective-permute-start(f32[2,256,128]{2,1,0:T(8,128)S(1)} %get-tuple-element.26), channel_id=1, source_target_pairs={{1,2},{3,4},{5,6},{7,8},{9,10},{11,12},{13,14},{2,1},{4,3},{6,5},{... | collective-permute-start | bytes 786440 | tf_op jit(solution)/shard_map/ppermute | solution.py:284
  26.0 20.7 %copy-start.8 = (f32[2,256,128]{2,1,0:T(8,128)}, f32[2,256,128]{2,1,0:T(8,128)S(1)}, u32[]{:S(2)}) copy-start(f32[2,256,128]{2,1,0:T(8,128)S(1)} %collective-permute-done.2.col_a) | copy-start | bytes 786436
  26.7 12.8 %all-to-all-start.1 = ((f32[8,16,256]{2,1,0:T(8,128)}), f32[8,16,256]{2,1,0:T(8,128)S(1)}, u32[]{:S(2)}, u32[]{:S(2)}) async-start(f32[8,16,256]{2,1,0:T(8,128)} %broadcast_in_dim.9), calls=%async_computation.1 | async-start | bytes 262144 | tf_op jit(solution)/shard_map/all_to_all | solution.py:288
  30.1 16.6 %copy-start.2 = (f32[2,2,64,256]{3,2,1,0:T(8,128)}, f32[2,2,64,256]{3,2,1,0:T(8,128)S(1)}, u32[]{:S(2)}) copy-start(f32[2,2,64,256]{3,2,1,0:T(8,128)S(1)} %collective-permute-done.row_a) | copy-start | bytes 786436
  30.1 16.5 %copy-start.3 = (f32[2,2,64,256]{3,2,1,0:T(8,128)}, f32[2,2,64,256]{3,2,1,0:T(8,128)S(1)}, u32[]{:S(2)}) copy-start(f32[2,2,64,256]{3,2,1,0:T(8,128)S(1)} %collective-permute-done.1.row_b) | copy-start | bytes 786436
  30.8 5.5 %collective-permute-start.4 = (f32[2,128,128]{2,1,0:T(8,128)S(1)}, f32[2,128,128]{2,1,0:T(8,128)S(1)}, u32[]{:S(2)}, u32[]{:S(2)}) collective-permute-start(f32[2,128,128]{2,1,0:T(8,128)S(1)} %get-tuple-element.27), channel_id=1, source_target_pairs={{0,1},{2,3},{4,5},{6,7},{8,9},{10,11},{12,13},{14,15},{1,0},{3,2},... | collective-permute-start | bytes 393224 | tf_op jit(solution)/shard_map/ppermute | solution.py:284
  31.4 15.2 %collective-permute-start.6 = (f32[2,128,128]{2,1,0:T(8,128)S(1)}, f32[2,128,128]{2,1,0:T(8,128)S(1)}, u32[]{:S(2)}, u32[]{:S(2)}) collective-permute-start(f32[2,128,128]{2,1,0:T(8,128)S(1)} %get-tuple-element.30), channel_id=1, source_target_pairs={{1,2},{3,4},{5,6},{7,8},{9,10},{11,12},{13,14},{2,1},{4,3},{6,5},{... | collective-permute-start | bytes 393224 | tf_op jit(solution)/shard_map/ppermute | solution.py:284
  36.3 10.4 %copy-start.10 = (f32[2,128,128]{2,1,0:T(8,128)}, f32[2,128,128]{2,1,0:T(8,128)S(1)}, u32[]{:S(2)}) copy-start(f32[2,128,128]{2,1,0:T(8,128)S(1)} %collective-permute-done.4.corners_a) | copy-start | bytes 393220
  40.2 34.3 %all-to-all-start.2 = ((f32[16,16,256]{2,1,0:T(8,128)}), f32[16,16,256]{2,1,0:T(8,128)S(1)}, u32[]{:S(2)}, u32[]{:S(2)}) async-start(f32[16,16,256]{2,1,0:T(8,128)} %broadcast_in_dim.10), calls=%async_computation.2 | async-start | bytes 524288 | tf_op jit(solution)/shard_map/all_to_all | solution.py:288
  46.6 0.7 copy-start.9
  46.6 0.7 copy-start.11
  47.4 29.3 %copy-start.5 = (s32[5]{0:T(128)S(1)}, s32[5]{0:T(128)}, u32[]{:S(2)}) copy-start(s32[5]{0:T(128)} %copy-done.4) | copy-start | bytes 64
  59.4 11.2 %collective-permute-start.11 = (f32[2,128,128]{2,1,0:T(8,128)}, f32[2,128,128]{2,1,0:T(8,128)S(1)}, u32[]{:S(2)}, u32[]{:S(2)}) collective-permute-start(f32[2,128,128]{2,1,0:T(8,128)} %get-tuple-element.36), channel_id=1, source_target_pairs={{0,1},{2,3},{4,5},{6,7},{8,9},{10,11},{12,13},{14,15},{1,0},{3,2},... | collective-permute-start | bytes 393224 | tf_op jit(solution)/shard_map/ppermute | solution.py:284
  60.0 17.2 %collective-permute-start.7 = (f32[2,256,128]{2,1,0:T(8,128)}, f32[2,256,128]{2,1,0:T(8,128)S(1)}, u32[]{:S(2)}, u32[]{:S(2)}) collective-permute-start(f32[2,256,128]{2,1,0:T(8,128)} %get-tuple-element.32), channel_id=1, source_target_pairs={{0,1},{2,3},{4,5},{6,7},{8,9},{10,11},{12,13},{14,15},{1,0},{3,2},... | collective-permute-start | bytes 786440 | tf_op jit(solution)/shard_map/ppermute | solution.py:284
  60.9 16.4 %collective-permute-start.8 = (f32[2,256,128]{2,1,0:T(8,128)}, f32[2,256,128]{2,1,0:T(8,128)S(1)}, u32[]{:S(2)}, u32[]{:S(2)}) collective-permute-start(f32[2,256,128]{2,1,0:T(8,128)} %get-tuple-element.33), channel_id=1, source_target_pairs={{1,2},{3,4},{5,6},{7,8},{9,10},{11,12},{13,14},{2,1},{4,3},{6,5},{... | collective-permute-start | bytes 786440 | tf_op jit(solution)/shard_map/ppermute | solution.py:284
  62.9 11.6 %collective-permute-start.12 = (f32[2,128,128]{2,1,0:T(8,128)}, f32[2,128,128]{2,1,0:T(8,128)S(1)}, u32[]{:S(2)}, u32[]{:S(2)}) collective-permute-start(f32[2,128,128]{2,1,0:T(8,128)} %get-tuple-element.37), channel_id=1, source_target_pairs={{1,2},{3,4},{5,6},{7,8},{9,10},{11,12},{13,14},{2,1},{4,3},{6,5},{... | collective-permute-start | bytes 393224 | tf_op jit(solution)/shard_map/ppermute | solution.py:284
  68.3 15.1 %collective-permute-start.9 = (f32[2,2,64,256]{3,2,1,0:T(8,128)}, f32[2,2,64,256]{3,2,1,0:T(8,128)S(1)}, u32[]{:S(2)}, u32[]{:S(2)}) collective-permute-start(f32[2,2,64,256]{3,2,1,0:T(8,128)} %get-tuple-element.34), channel_id=1, source_target_pairs={{0,16},{32,48},{64,80},{96,112},{128,144},{160,176},{192,208},{224... | collective-permute-start | bytes 786440 | tf_op jit(solution)/shard_map/ppermute | solution.py:284
  70.5 14.0 %collective-permute-start.10 = (f32[2,2,64,256]{3,2,1,0:T(8,128)}, f32[2,2,64,256]{3,2,1,0:T(8,128)S(1)}, u32[]{:S(2)}, u32[]{:S(2)}) collective-permute-start(f32[2,2,64,256]{3,2,1,0:T(8,128)} %get-tuple-element.35), channel_id=1, source_target_pairs={{16,32},{48,64},{80,96},{112,128},{144,160},{176,192},{208,224},{3... | collective-permute-start | bytes 786440 | tf_op jit(solution)/shard_map/ppermute | solution.py:284
  74.5 16.9 %collective-permute-start.15 = (f32[256,256]{1,0:T(8,128)S(1)}, f32[256,256]{1,0:T(8,128)S(1)}, u32[]{:S(2)}, u32[]{:S(2)}) collective-permute-start(f32[256,256]{1,0:T(8,128)S(1)} %bitcast.17), channel_id=1, source_target_pairs={{0,16},{16,0},{1,17},{17,1},{2,18},{18,2},{3,19},{19,3},{4,20},{20... | collective-permute-start | bytes 786440 | tf_op jit(solution)/shard_map/ppermute | solution.py:284
  77.3 9.3 %collective-permute-start.13 = (f32[2,2,64,128]{3,2,1,0:T(8,128)S(1)}, f32[2,2,64,128]{3,2,1,0:T(8,128)S(1)}, u32[]{:S(2)}, u32[]{:S(2)}) collective-permute-start(f32[2,2,64,128]{3,2,1,0:T(8,128)S(1)} %get-tuple-element.38), channel_id=1, source_target_pairs={{0,16},{32,48},{64,80},{96,112},{128,144},{160,176},{192,208},{224... | collective-permute-start | bytes 393224 | tf_op jit(solution)/shard_map/ppermute | solution.py:284
  77.4 12.3 %collective-permute-start.14 = (f32[2,2,64,128]{3,2,1,0:T(8,128)S(1)}, f32[2,2,64,128]{3,2,1,0:T(8,128)S(1)}, u32[]{:S(2)}, u32[]{:S(2)}) collective-permute-start(f32[2,2,64,128]{3,2,1,0:T(8,128)S(1)} %get-tuple-element.39), channel_id=1, source_target_pairs={{16,32},{48,64},{80,96},{112,128},{144,160},{176,192},{208,224},{3... | collective-permute-start | bytes 393224 | tf_op jit(solution)/shard_map/ppermute | solution.py:284
  84.5 1.2 %copy-start.1 = (f32[2,2,256,256]{3,2,1,0:T(8,128)S(1)}, f32[2,2,256,256]{3,2,1,0:T(8,128)}, u32[]{:S(2)}) copy-start(f32[2,2,256,256]{3,2,1,0:T(8,128)} %get-tuple-element.31.center) | copy-start | bytes 3145732
  86.5 4.8 %copy-start.6 = (f32[2,256,256]{2,1,0:T(8,128)S(1)}, f32[2,256,256]{2,1,0:T(8,128)}, u32[]{:S(2)}) copy-start(f32[2,256,256]{2,1,0:T(8,128)} %probe.1) | copy-start | bytes 1572868

commit v5 on v4

--- a/solution.py
+++ b/solution.py
@@ -118,7 +118,7 @@
 
 def gradient(
     facts, objects, row_a, row_b, col_a, col_b, corners_a, corners_b, probe, amp, mats,
-    center_out, row_a_out, row_b_out, col_a_out, col_b_out, corners_a_out, corners_b_out, probe_out,
+    center_out, row_a_out, row_b_out, col_a_out, col_b_out, probe_out,
     ext, grad, sides, sides_out, probe_in, amp_in, mats_in, probe_grad, arrive, leave,
 ):
     row_odd, col_odd = facts[3], facts[4]
@@ -136,19 +136,17 @@
         (mats, mats_in),
         (amp, amp_in),
     ]
-    outgoing = [(probe_grad, probe_out)]
-    for side, col, corner, col_out, corner_out in (
-        (1 - col_odd, col_a, corners_a, col_a_out, corners_a_out),
-        (col_odd, col_b, corners_b, col_b_out, corners_b_out),
-    ):
-        for rows, src, dst in (
-            (upper, corner.at[:, upper], corner_out.at[:, upper]),
-            (middle, col, col_out),
-            (lower, corner.at[:, pl.ds(HALO, HALO)], corner_out.at[:, pl.ds(HALO, HALO)]),
+    for side, col, corner in ((1 - col_odd, col_a, corners_a), (col_odd, col_b, corners_b)):
+        for rows, src in (
+            (upper, corner.at[:, upper]),
+            (middle, col),
+            (lower, corner.at[:, pl.ds(HALO, HALO)]),
         ):
             incoming.insert(3, (src, sides.at[side, :, rows]))
-            outgoing.append((sides_out.at[side, :, rows], dst))
-    outgoing += [
+    outgoing = [
+        (probe_grad, probe_out),
+        (sides_out.at[1 - col_odd], col_a_out),
+        (sides_out.at[col_odd], col_b_out),
         (grad.at[:, :, beyond(row_odd), across], row_a_out),
         (grad.at[:, :, beyond(1 - row_odd), across], row_b_out),
         (ext.at[:, :, middle, across], center_out),
@@ -231,11 +229,11 @@
     )
 
 
-def relay(facts, corners_a, corners_b, row_a, row_b):
+def relay(facts, col_a, col_b, row_a, row_b):
     row_odd = facts[3]
-    for side, src in ((0, corners_a), (1, corners_b)):
+    for side, src in ((0, col_a), (1, col_b)):
         for s in range(2):
-            upper, lower = src[s, :HALO], src[s, HALO:]
+            upper, lower = src[s, :HALO], src[s, HALO + TILE :]
             row_a[side, s] = either(row_odd, lower, upper)
             row_b[side, s] = either(row_odd, upper, lower)
 
@@ -243,7 +241,7 @@
 def add_sides(facts, center, col_a, col_b, row_a, row_b, tile):
     row_odd, col_odd = facts[3], facts[4]
     for s in range(2):
-        edges = edge_columns(col_odd, col_a, col_b, s, 0, TILE)
+        edges = edge_columns(col_odd, col_a, col_b, s, HALO, TILE)
         for k in range(2):
             for half, cols in enumerate((slice(0, 128), slice(128, 256))):
                 value = center[s, k, :, cols] + edges[k][half]
@@ -317,6 +315,7 @@
 def shards(objects, probe, prev_partial, offsets, counts, amplitudes):
     strip, column, corners = (2, 2, HALO, TILE), (2, TILE, 2 * HALO), (2, 2 * HALO, 2 * HALO)
     tile, strip_corners = (2, 2, TILE, TILE), (2, 2, HALO, 2 * HALO)
+    whole_column = (2, SIDE, 2 * HALO)
     facts = jnp.concatenate([
         offsets.reshape(2), counts.reshape(1),
         jnp.stack([lax.axis_index("row_2"), lax.axis_index("col_1") % 2]).astype(jnp.int32),
@@ -329,9 +328,9 @@
     corners_b, corners_a = exchanged(sent_b, COL, 1), exchanged(sent_a, COL, 0)
     deep = depth_sum(scattered, col_a)
     corners_a, deep = lax.optimization_barrier((corners_a, deep))
-    center, row_a_part, row_b_part, col_a_part, col_b_part, corners_a_part, corners_b_part, partial = call(
+    center, row_a_part, row_b_part, col_a_part, col_b_part, partial = call(
         gradient,
-        [tile, strip, strip, column, column, corners, corners, (2, WIN, WIN)],
+        [tile, strip, strip, whole_column, whole_column, (2, WIN, WIN)],
         facts, objects, row_a, row_b, col_a, col_b, corners_a, corners_b, probe,
         amplitudes.reshape(WIN, WIN), jnp.asarray(operator_parts()),
         specs=[ANY] * 3 + [HBM] * 7,
@@ -339,16 +338,15 @@
         + [pltpu.VMEM((2, 2, SIDE, 2 * HALO), jnp.float32)] * 2
         + [pltpu.VMEM((2, WIN, WIN), jnp.float32), pltpu.VMEM((WIN, WIN), jnp.float32)]
         + [pltpu.VMEM((12, WIN, WIN), jnp.bfloat16), pltpu.VMEM((2, WIN, WIN), jnp.float32)]
-        + [pltpu.SemaphoreType.DMA((12,)), pltpu.SemaphoreType.DMA((10,))],
+        + [pltpu.SemaphoreType.DMA((12,)), pltpu.SemaphoreType.DMA((6,))],
         flops=96 * 2 * WIN**3,
         limit=60,
         name="gradient",
     )
-    corners_b, corners_a = exchanged(corners_b_part, COL, 1), exchanged(corners_a_part, COL, 0)
+    col_b, col_a = exchanged(col_b_part, COL, 1), exchanged(col_a_part, COL, 0)
     row_b, row_a = exchanged(row_b_part, ROW, 1), exchanged(row_a_part, ROW, 0)
-    sent_a, sent_b = call(relay, [strip_corners] * 2, facts, corners_a, corners_b, name="relay")
+    sent_a, sent_b = call(relay, [strip_corners] * 2, facts, col_a, col_b, name="relay")
     relayed_b, relayed_a = exchanged(sent_b, ROW, 1), exchanged(sent_a, ROW, 0)
-    col_b, col_a = exchanged(col_b_part, COL, 1), exchanged(col_a_part, COL, 0)
     (added,) = call(add_sides, [tile], facts, center, col_a, col_b, row_a, row_b, name="add_sides")
     (new_objects,) = call(add_corners, [tile], facts, added, relayed_a, relayed_b, name="add_corners")
     rate = PROBE_RATE / math.sqrt(lax.axis_size(ROW) * lax.axis_size(COL))

time: 93.4 us -> 92.9 us (level)
  starting transfers between devices: 58.7 us -> 53.3 us
  waiting for transfers between devices: 7.41 us -> 12.6 us
    ppermute x16 -> x14, starting transfers between devices: 42.1 us -> 36.6 us  [exchanged(): return lax.ppermute(value, axis, pairs + [(j, i) for i, j in pairs])]
    ppermute x16 -> x14, waiting for transfers between devices: 4.27 us -> 9.49 us  [exchanged(): return lax.ppermute(value, axis, pairs + [(j, i) for i, j in pairs])]
  transfers between devices with their start and end apart: 19 -> 17, of which waited for: 3 -> 3; matrix products, arithmetic and copies ran while one was open for 3% -> 4% of each run, Pallas kernels for 18% -> 16%
where the time goes in v5:
time: 92.9 us; the launch traced here: 92.1 us
  starting transfers between devices  53.3 us (57%)
  Pallas kernels  16.4 us (18%)
  waiting for transfers between devices  12.6 us (14%)
  local copies, waits for them, and re-layouts  5.79 us (6%)
  other arithmetic  2.41 us (3%)
  between operations  1.62 us (2%)
    ppermute x14, starting transfers between devices, exchanged(): return lax.ppermute(value, axis, pairs + [(j, i) for i, j in pairs])  36.6 us
    all_to_all x3, starting transfers between devices, swap(): return lax.all_to_all(value, axes, 0, 0, tiled=True)  16.7 us
    pallas_call x6, Pallas kernels, call(): pl.pallas_call(body, out_shape=[jax.ShapeDtypeStruct(o, jnp.float32) for...  16.4 us
    ppermute x14, waiting for transfers between devices, exchanged(): return lax.ppermute(value, axis, pairs + [(j, i) for i, j in pairs])  9.49 us
    unnamed x24, local copies, waits for them, and re-layouts  3.35 us
    all_to_all x3, waiting for transfers between devices, swap(): return lax.all_to_all(value, axes, 0, 0, tiled=True)  3.14 us
  transfers between devices with their start and end apart: 17, of which 3 were waited for; matrix products, arithmetic and copies ran while one was open for 4% of the time, Pallas kernels for 16%

profile of v5, /device:TPU:31, one launch (start us, length us, event | category | flops | bytes accessed | tf_op | source)
XLA Modules:
  0.0 92.1 jit_solution(8801942464812801220)
XLA Ops:
  0.6 0.0 copy-start.7
  0.6 1.0 %dynamic-slice_bitcast_fusion = f32[256,256]{1,0:T(8,128)S(1)} fusion(f32[1,1,2,256,256]{4,3,2,1,0:T(8,128)} %param.9, s32[]{:T(128)S(6)} %select_n.28), kind=kLoop, calls=%fused_computation.5 | loop fusion | bytes 524292 | tf_op jit(solution)/shard_map/jit(dynamic_index_in_dim)/squeeze | solution.py:296
  1.7 0.8 collective-permute-start.5
  3.1 0.7 pad_add_fusion.facts
  3.8 1.2 %copy-done = f32[2,2,256,256]{3,2,1,0:T(8,128)S(1)} copy-done((f32[2,2,256,256]{3,2,1,0:T(8,128)S(1)}, f32[2,2,256,256]{3,2,1,0:T(8,128)}, u32[]{:S(2)}) %copy-start) | copy-done | bytes 1048600
  5.1 0.8 pack_sides.1
  5.8 0.6 collective-permute-start.2
  6.4 0.0 collective-permute-done.5
  6.5 0.0 copy-done.7
  6.5 0.7 bitcast_add_fusion
  7.2 6.9 %all-to-all-start = ((f32[16,16,256]{2,1,0:T(8,128)}), f32[16,16,256]{2,1,0:T(8,128)S(1)}, u32[]{:S(2)}, u32[]{:S(2)}) async-start(f32[16,16,256]{2,1,0:T(8,128)} %bitcast.6), calls=%async_computation | async-start | bytes 524288 | tf_op jit(solution)/shard_map/all_to_all | solution.py:286
  14.1 0.9 collective-permute-start
  14.9 8.7 %collective-permute-start.1 = (f32[2,2,64,256]{3,2,1,0:T(8,128)S(1)}, f32[2,2,64,256]{3,2,1,0:T(8,128)S(1)}, u32[]{:S(2)}, u32[]{:S(2)}) collective-permute-start(f32[2,2,64,256]{3,2,1,0:T(8,128)S(1)} %get-tuple-element.22), channel_id=1, source_target_pairs={{16,32},{48,64},{80,96},{112,128},{144,160},{176,192},{208,224},{3... | collective-permute-start | bytes 786440 | tf_op jit(solution)/shard_map/ppermute | solution.py:282
  23.7 2.3 %collective-permute-start.3 = (f32[2,256,128]{2,1,0:T(8,128)S(1)}, f32[2,256,128]{2,1,0:T(8,128)S(1)}, u32[]{:S(2)}, u32[]{:S(2)}) collective-permute-start(f32[2,256,128]{2,1,0:T(8,128)S(1)} %get-tuple-element.24), channel_id=1, source_target_pairs={{1,2},{3,4},{5,6},{7,8},{9,10},{11,12},{13,14},{2,1},{4,3},{6,5},{... | collective-permute-start | bytes 786440 | tf_op jit(solution)/shard_map/ppermute | solution.py:282
  25.9 0.0 collective-permute-done.2.col_a
  26.0 0.0 copy-start.8
  26.0 0.0 all-to-all-done
  26.0 0.7 broadcast_in_dim.9
  26.7 3.4 %all-to-all-start.1 = ((f32[8,16,256]{2,1,0:T(8,128)}), f32[8,16,256]{2,1,0:T(8,128)S(1)}, u32[]{:S(2)}, u32[]{:S(2)}) async-start(f32[8,16,256]{2,1,0:T(8,128)} %broadcast_in_dim.9), calls=%async_computation.1 | async-start | bytes 262144 | tf_op jit(solution)/shard_map/all_to_all | solution.py:286
  30.1 0.0 collective-permute-done.row_a
  30.1 0.0 copy-start.2
  30.1 0.0 collective-permute-done.1.row_b
  30.1 0.0 copy-start.3
  30.1 0.7 pack_corners.1
  30.8 0.0 copy-done.4
  30.8 0.6 collective-permute-start.4
  31.4 4.9 %collective-permute-start.6 = (f32[2,128,128]{2,1,0:T(8,128)S(1)}, f32[2,128,128]{2,1,0:T(8,128)S(1)}, u32[]{:S(2)}, u32[]{:S(2)}) collective-permute-start(f32[2,128,128]{2,1,0:T(8,128)S(1)} %get-tuple-element.28), channel_id=1, source_target_pairs={{1,2},{3,4},{5,6},{7,8},{9,10},{11,12},{13,14},{2,1},{4,3},{6,5},{... | collective-permute-start | bytes 393224 | tf_op jit(solution)/shard_map/ppermute | solution.py:282
  36.3 0.0 collective-permute-done.4.corners_a
  36.3 0.0 copy-start.10
  36.3 3.1 %all-to-all-done.1 = f32[8,16,256]{2,1,0:T(8,128)S(1)} async-done(((f32[8,16,256]{2,1,0:T(8,128)}), f32[8,16,256]{2,1,0:T(8,128)S(1)}, u32[]{:S(2)}, u32[]{:S(2)}) %all-to-all-start.1) | async-done | bytes 131104 | tf_op jit(solution)/shard_map/all_to_all | solution.py:286
  39.5 0.7 broadcast_in_dim.10
  40.2 6.4 %all-to-all-start.2 = ((f32[16,16,256]{2,1,0:T(8,128)}), f32[16,16,256]{2,1,0:T(8,128)S(1)}, u32[]{:S(2)}, u32[]{:S(2)}) async-start(f32[16,16,256]{2,1,0:T(8,128)} %broadcast_in_dim.10), calls=%async_computation.2 | async-start | bytes 524288 | tf_op jit(solution)/shard_map/all_to_all | solution.py:286
  46.6 0.0 collective-permute-done.3.col_b
  46.6 0.0 copy-start.9
  46.6 0.0 collective-permute-done.6.corners_b
  46.6 0.0 copy-start.11
  46.6 0.0 copy-done.8
  46.6 0.0 copy-done.2
  46.7 0.0 copy-done.3
  46.7 0.6 copy-done.9
  47.3 0.0 copy-done.11
  47.4 12.0 %gradient.1 = (f32[2,2,256,256]{3,2,1,0:T(8,128)}, f32[2,2,64,256]{3,2,1,0:T(8,128)}, f32[2,2,64,256]{3,2,1,0:T(8,128)}, f32[2,384,128]{2,1,0:T(8,128)}, f32[2,384,128]{2,1,0:T(8,128)}, /*index=5*/f32[2,256,256]{2,1,0:T(8,128)}) custom-call(s32[5]{0:T(128)} %copy-done.4, f32[2,2,256,256]{3,2,1,0:T(8,128)} %objects.3, f32[2,2,64,256]{3,2,1,0:T(8,128)} %copy-done.2, ...), custom_call_target="tpu_custom_call" | custom-call | flops 3221225472 | bytes 5767168 | tf_op jit(solution)/shard_map/gradient/pallas_call | solution.py:268
  59.3 0.6 collective-permute-start.7
  60.0 2.6 %collective-permute-start.8 = (f32[2,384,128]{2,1,0:T(8,128)}, f32[2,384,128]{2,1,0:T(8,128)S(1)}, u32[]{:S(2)}, u32[]{:S(2)}) collective-permute-start(f32[2,384,128]{2,1,0:T(8,128)} %get-tuple-element.31), channel_id=1, source_target_pairs={{1,2},{3,4},{5,6},{7,8},{9,10},{11,12},{13,14},{2,1},{4,3},{6,5},{... | collective-permute-start | bytes 1179656 | tf_op jit(solution)/shard_map/ppermute | solution.py:282
  62.6 1.8 %collective-permute-start.9 = (f32[2,2,64,256]{3,2,1,0:T(8,128)}, f32[2,2,64,256]{3,2,1,0:T(8,128)S(1)}, u32[]{:S(2)}, u32[]{:S(2)}) collective-permute-start(f32[2,2,64,256]{3,2,1,0:T(8,128)} %get-tuple-element.32), channel_id=1, source_target_pairs={{0,16},{32,48},{64,80},{96,112},{128,144},{160,176},{192,208},{224... | collective-permute-start | bytes 786440 | tf_op jit(solution)/shard_map/ppermute | solution.py:282
  64.4 5.6 %collective-permute-start.10 = (f32[2,2,64,256]{3,2,1,0:T(8,128)}, f32[2,2,64,256]{3,2,1,0:T(8,128)S(1)}, u32[]{:S(2)}, u32[]{:S(2)}) collective-permute-start(f32[2,2,64,256]{3,2,1,0:T(8,128)} %get-tuple-element.33), channel_id=1, source_target_pairs={{16,32},{48,64},{80,96},{112,128},{144,160},{176,192},{208,224},{3... | collective-permute-start | bytes 786440 | tf_op jit(solution)/shard_map/ppermute | solution.py:282
  70.1 0.0 all-to-all-done.2
  70.1 0.1 collective-permute-start.13
  70.2 0.0 collective-permute-done.7.col_a
  70.2 3.3 %collective-permute-done.8.col_b = f32[2,384,128]{2,1,0:T(8,128)S(1)} collective-permute-done((f32[2,384,128]{2,1,0:T(8,128)}, f32[2,384,128]{2,1,0:T(8,128)S(1)}, u32[]{:S(2)}, u32[]{:S(2)}) %collective-permute-start.8) | collective-permute-done | bytes 393248 | tf_op jit(solution)/shard_map/ppermute | solution.py:282
  73.5 0.6 relay.1
  74.1 4.1 %collective-permute-start.11 = (f32[2,2,64,128]{3,2,1,0:T(8,128)S(1)}, f32[2,2,64,128]{3,2,1,0:T(8,128)S(1)}, u32[]{:S(2)}, u32[]{:S(2)}) collective-permute-start(f32[2,2,64,128]{3,2,1,0:T(8,128)S(1)} %get-tuple-element.34), channel_id=1, source_target_pairs={{0,16},{32,48},{64,80},{96,112},{128,144},{160,176},{192,208},{224... | collective-permute-start | bytes 393224 | tf_op jit(solution)/shard_map/ppermute | solution.py:282
  78.2 3.0 %collective-permute-start.12 = (f32[2,2,64,128]{3,2,1,0:T(8,128)S(1)}, f32[2,2,64,128]{3,2,1,0:T(8,128)S(1)}, u32[]{:S(2)}, u32[]{:S(2)}) collective-permute-start(f32[2,2,64,128]{3,2,1,0:T(8,128)S(1)} %get-tuple-element.35), channel_id=1, source_target_pairs={{16,32},{48,64},{80,96},{112,128},{144,160},{176,192},{208,224},{3... | collective-permute-start | bytes 393224 | tf_op jit(solution)/shard_map/ppermute | solution.py:282
  81.1 0.0 collective-permute-done.9.row_a
  81.2 0.0 collective-permute-done.10.row_b
  81.2 0.0 copy-start.1
  81.2 1.2 %copy-done.1 = f32[2,2,256,256]{3,2,1,0:T(8,128)S(1)} copy-done((f32[2,2,256,256]{3,2,1,0:T(8,128)S(1)}, f32[2,2,256,256]{3,2,1,0:T(8,128)}, u32[]{:S(2)}) %copy-start.1) | copy-done | bytes 1048600
  82.4 0.8 add_sides.1.tile
  83.2 0.0 collective-permute-done.13
  83.2 0.2 copy-done.6
  83.4 0.9 fusion
  84.3 0.0 collective-permute-done.11.relayed_a
  84.3 6.2 %collective-permute-done.12.relayed_b = f32[2,2,64,128]{3,2,1,0:T(8,128)S(1)} collective-permute-done((f32[2,2,64,128]{3,2,1,0:T(8,128)S(1)}, f32[2,2,64,128]{3,2,1,0:T(8,128)S(1)}, u32[]{:S(2)}, u32[]{:S(2)}) %collective-permute-start.12) | collective-permute-done | bytes 131104 | tf_op jit(solution)/shard_map/ppermute | solution.py:282
  90.5 1.7 %add_corners.1 = f32[2,2,256,256]{3,2,1,0:T(8,128)} custom-call(s32[5]{0:T(128)S(1)} %copy-done.5, f32[2,2,256,256]{3,2,1,0:T(8,128)S(1)} %add_sides.1.tile, f32[2,2,64,128]{3,2,1,0:T(8,128)S(1)} %collective-permute-done.11.relayed_a, f32[2,2,64,128]{3,2,1,0:T(8,128)S(1)} %collective-permute-done.12.relayed_b), custom_call_target="tpu_custom_call" | custom-call | bytes 2097152 | tf_op jit(solution)/shard_map/add_corners/pallas_call | solution.py:268
  (9 shorter events, 0.1 us)
Async XLA Ops:
  0.6 5.8 %copy-start.7 = (f32[1,1,2,256,256]{4,3,2,1,0:T(8,128)S(1)}, f32[1,1,2,256,256]{4,3,2,1,0:T(8,128)}, u32[]{:S(2)}) copy-start(f32[1,1,2,256,256]{4,3,2,1,0:T(8,128)} %param.9) | copy-start | bytes 1572868
  1.7 4.8 %collective-permute-start.5 = (f32[256,256]{1,0:T(8,128)S(1)}, f32[256,256]{1,0:T(8,128)S(1)}, u32[]{:S(2)}, u32[]{:S(2)}) collective-permute-start(f32[256,256]{1,0:T(8,128)S(1)} %dynamic-slice_bitcast_fusion), channel_id=1, source_target_pairs={{0,16},{16,0},{1,17},{17,1},{2,18},{18,2},{3,19},{19,3},{4,20},{20... | collective-permute-start | bytes 786440 | tf_op jit(solution)/shard_map/ppermute | solution.py:282
  3.8 1.2 %copy-start = (f32[2,2,256,256]{3,2,1,0:T(8,128)S(1)}, f32[2,2,256,256]{3,2,1,0:T(8,128)}, u32[]{:S(2)}) copy-start(f32[2,2,256,256]{3,2,1,0:T(8,128)} %objects.3) | copy-start | bytes 3145732
  5.1 25.7 %copy-start.4 = (s32[5]{0:T(128)}, s32[5]{0:T(128)S(1)}, u32[]{:S(2)}) copy-start(s32[5]{0:T(128)S(1)} %pad_add_fusion.facts) | copy-start | bytes 64
  5.8 20.1 %collective-permute-start.2 = (f32[2,256,128]{2,1,0:T(8,128)S(1)}, f32[2,256,128]{2,1,0:T(8,128)S(1)}, u32[]{:S(2)}, u32[]{:S(2)}) collective-permute-start(f32[2,256,128]{2,1,0:T(8,128)S(1)} %get-tuple-element.23), channel_id=1, source_target_pairs={{0,1},{2,3},{4,5},{6,7},{8,9},{10,11},{12,13},{14,15},{1,0},{3,2},... | collective-permute-start | bytes 786440 | tf_op jit(solution)/shard_map/ppermute | solution.py:282
  7.2 18.8 %all-to-all-start = ((f32[16,16,256]{2,1,0:T(8,128)}), f32[16,16,256]{2,1,0:T(8,128)S(1)}, u32[]{:S(2)}, u32[]{:S(2)}) async-start(f32[16,16,256]{2,1,0:T(8,128)} %bitcast.6), calls=%async_computation | async-start | bytes 524288 | tf_op jit(solution)/shard_map/all_to_all | solution.py:286
  14.1 16.0 %collective-permute-start = (f32[2,2,64,256]{3,2,1,0:T(8,128)S(1)}, f32[2,2,64,256]{3,2,1,0:T(8,128)S(1)}, u32[]{:S(2)}, u32[]{:S(2)}) collective-permute-start(f32[2,2,64,256]{3,2,1,0:T(8,128)S(1)} %get-tuple-element.21), channel_id=1, source_target_pairs={{0,16},{32,48},{64,80},{96,112},{128,144},{160,176},{192,208},{224... | collective-permute-start | bytes 786440 | tf_op jit(solution)/shard_map/ppermute | solution.py:282
  14.9 15.2 %collective-permute-start.1 = (f32[2,2,64,256]{3,2,1,0:T(8,128)S(1)}, f32[2,2,64,256]{3,2,1,0:T(8,128)S(1)}, u32[]{:S(2)}, u32[]{:S(2)}) collective-permute-start(f32[2,2,64,256]{3,2,1,0:T(8,128)S(1)} %get-tuple-element.22), channel_id=1, source_target_pairs={{16,32},{48,64},{80,96},{112,128},{144,160},{176,192},{208,224},{3... | collective-permute-start | bytes 786440 | tf_op jit(solution)/shard_map/ppermute | solution.py:282
  23.7 22.9 %collective-permute-start.3 = (f32[2,256,128]{2,1,0:T(8,128)S(1)}, f32[2,256,128]{2,1,0:T(8,128)S(1)}, u32[]{:S(2)}, u32[]{:S(2)}) collective-permute-start(f32[2,256,128]{2,1,0:T(8,128)S(1)} %get-tuple-element.24), channel_id=1, source_target_pairs={{1,2},{3,4},{5,6},{7,8},{9,10},{11,12},{13,14},{2,1},{4,3},{6,5},{... | collective-permute-start | bytes 786440 | tf_op jit(solution)/shard_map/ppermute | solution.py:282
  26.0 20.7 %copy-start.8 = (f32[2,256,128]{2,1,0:T(8,128)}, f32[2,256,128]{2,1,0:T(8,128)S(1)}, u32[]{:S(2)}) copy-start(f32[2,256,128]{2,1,0:T(8,128)S(1)} %collective-permute-done.2.col_a) | copy-start | bytes 786436
  26.7 12.8 %all-to-all-start.1 = ((f32[8,16,256]{2,1,0:T(8,128)}), f32[8,16,256]{2,1,0:T(8,128)S(1)}, u32[]{:S(2)}, u32[]{:S(2)}) async-start(f32[8,16,256]{2,1,0:T(8,128)} %broadcast_in_dim.9), calls=%async_computation.1 | async-start | bytes 262144 | tf_op jit(solution)/shard_map/all_to_all | solution.py:286
  30.1 16.6 %copy-start.2 = (f32[2,2,64,256]{3,2,1,0:T(8,128)}, f32[2,2,64,256]{3,2,1,0:T(8,128)S(1)}, u32[]{:S(2)}) copy-start(f32[2,2,64,256]{3,2,1,0:T(8,128)S(1)} %collective-permute-done.row_a) | copy-start | bytes 786436
  30.1 16.6 %copy-start.3 = (f32[2,2,64,256]{3,2,1,0:T(8,128)}, f32[2,2,64,256]{3,2,1,0:T(8,128)S(1)}, u32[]{:S(2)}) copy-start(f32[2,2,64,256]{3,2,1,0:T(8,128)S(1)} %collective-permute-done.1.row_b) | copy-start | bytes 786436
  30.8 5.5 %collective-permute-start.4 = (f32[2,128,128]{2,1,0:T(8,128)S(1)}, f32[2,128,128]{2,1,0:T(8,128)S(1)}, u32[]{:S(2)}, u32[]{:S(2)}) collective-permute-start(f32[2,128,128]{2,1,0:T(8,128)S(1)} %get-tuple-element.25), channel_id=1, source_target_pairs={{0,1},{2,3},{4,5},{6,7},{8,9},{10,11},{12,13},{14,15},{1,0},{3,2},... | collective-permute-start | bytes 393224 | tf_op jit(solution)/shard_map/ppermute | solution.py:282
  31.4 15.2 %collective-permute-start.6 = (f32[2,128,128]{2,1,0:T(8,128)S(1)}, f32[2,128,128]{2,1,0:T(8,128)S(1)}, u32[]{:S(2)}, u32[]{:S(2)}) collective-permute-start(f32[2,128,128]{2,1,0:T(8,128)S(1)} %get-tuple-element.28), channel_id=1, source_target_pairs={{1,2},{3,4},{5,6},{7,8},{9,10},{11,12},{13,14},{2,1},{4,3},{6,5},{... | collective-permute-start | bytes 393224 | tf_op jit(solution)/shard_map/ppermute | solution.py:282
  36.3 10.4 %copy-start.10 = (f32[2,128,128]{2,1,0:T(8,128)}, f32[2,128,128]{2,1,0:T(8,128)S(1)}, u32[]{:S(2)}) copy-start(f32[2,128,128]{2,1,0:T(8,128)S(1)} %collective-permute-done.4.corners_a) | copy-start | bytes 393220
  40.2 29.9 %all-to-all-start.2 = ((f32[16,16,256]{2,1,0:T(8,128)}), f32[16,16,256]{2,1,0:T(8,128)S(1)}, u32[]{:S(2)}, u32[]{:S(2)}) async-start(f32[16,16,256]{2,1,0:T(8,128)} %broadcast_in_dim.10), calls=%async_computation.2 | async-start | bytes 524288 | tf_op jit(solution)/shard_map/all_to_all | solution.py:286
  46.6 0.7 copy-start.9
  46.6 0.7 copy-start.11
  47.4 26.2 %copy-start.5 = (s32[5]{0:T(128)S(1)}, s32[5]{0:T(128)}, u32[]{:S(2)}) copy-start(s32[5]{0:T(128)} %copy-done.4) | copy-start | bytes 64
  59.3 10.9 %collective-permute-start.7 = (f32[2,384,128]{2,1,0:T(8,128)}, f32[2,384,128]{2,1,0:T(8,128)S(1)}, u32[]{:S(2)}, u32[]{:S(2)}) collective-permute-start(f32[2,384,128]{2,1,0:T(8,128)} %get-tuple-element.30), channel_id=1, source_target_pairs={{0,1},{2,3},{4,5},{6,7},{8,9},{10,11},{12,13},{14,15},{1,0},{3,2},... | collective-permute-start | bytes 1179656 | tf_op jit(solution)/shard_map/ppermute | solution.py:282
  60.0 13.5 %collective-permute-start.8 = (f32[2,384,128]{2,1,0:T(8,128)}, f32[2,384,128]{2,1,0:T(8,128)S(1)}, u32[]{:S(2)}, u32[]{:S(2)}) collective-permute-start(f32[2,384,128]{2,1,0:T(8,128)} %get-tuple-element.31), channel_id=1, source_target_pairs={{1,2},{3,4},{5,6},{7,8},{9,10},{11,12},{13,14},{2,1},{4,3},{6,5},{... | collective-permute-start | bytes 1179656 | tf_op jit(solution)/shard_map/ppermute | solution.py:282
  62.6 18.5 %collective-permute-start.9 = (f32[2,2,64,256]{3,2,1,0:T(8,128)}, f32[2,2,64,256]{3,2,1,0:T(8,128)S(1)}, u32[]{:S(2)}, u32[]{:S(2)}) collective-permute-start(f32[2,2,64,256]{3,2,1,0:T(8,128)} %get-tuple-element.32), channel_id=1, source_target_pairs={{0,16},{32,48},{64,80},{96,112},{128,144},{160,176},{192,208},{224... | collective-permute-start | bytes 786440 | tf_op jit(solution)/shard_map/ppermute | solution.py:282
  64.4 16.7 %collective-permute-start.10 = (f32[2,2,64,256]{3,2,1,0:T(8,128)}, f32[2,2,64,256]{3,2,1,0:T(8,128)S(1)}, u32[]{:S(2)}, u32[]{:S(2)}) collective-permute-start(f32[2,2,64,256]{3,2,1,0:T(8,128)} %get-tuple-element.33), channel_id=1, source_target_pairs={{16,32},{48,64},{80,96},{112,128},{144,160},{176,192},{208,224},{3... | collective-permute-start | bytes 786440 | tf_op jit(solution)/shard_map/ppermute | solution.py:282
  70.1 13.1 %collective-permute-start.13 = (f32[256,256]{1,0:T(8,128)S(1)}, f32[256,256]{1,0:T(8,128)S(1)}, u32[]{:S(2)}, u32[]{:S(2)}) collective-permute-start(f32[256,256]{1,0:T(8,128)S(1)} %bitcast.17), channel_id=1, source_target_pairs={{0,16},{16,0},{1,17},{17,1},{2,18},{18,2},{3,19},{19,3},{4,20},{20... | collective-permute-start | bytes 786440 | tf_op jit(solution)/shard_map/ppermute | solution.py:282
  74.1 10.2 %collective-permute-start.11 = (f32[2,2,64,128]{3,2,1,0:T(8,128)S(1)}, f32[2,2,64,128]{3,2,1,0:T(8,128)S(1)}, u32[]{:S(2)}, u32[]{:S(2)}) collective-permute-start(f32[2,2,64,128]{3,2,1,0:T(8,128)S(1)} %get-tuple-element.34), channel_id=1, source_target_pairs={{0,16},{32,48},{64,80},{96,112},{128,144},{160,176},{192,208},{224... | collective-permute-start | bytes 393224 | tf_op jit(solution)/shard_map/ppermute | solution.py:282
  78.2 12.3 %collective-permute-start.12 = (f32[2,2,64,128]{3,2,1,0:T(8,128)S(1)}, f32[2,2,64,128]{3,2,1,0:T(8,128)S(1)}, u32[]{:S(2)}, u32[]{:S(2)}) collective-permute-start(f32[2,2,64,128]{3,2,1,0:T(8,128)S(1)} %get-tuple-element.35), channel_id=1, source_target_pairs={{16,32},{48,64},{80,96},{112,128},{144,160},{176,192},{208,224},{3... | collective-permute-start | bytes 393224 | tf_op jit(solution)/shard_map/ppermute | solution.py:282
  81.2 1.2 %copy-start.1 = (f32[2,2,256,256]{3,2,1,0:T(8,128)S(1)}, f32[2,2,256,256]{3,2,1,0:T(8,128)}, u32[]{:S(2)}) copy-start(f32[2,2,256,256]{3,2,1,0:T(8,128)} %get-tuple-element.29.center) | copy-start | bytes 3145732
  82.4 1.0 %copy-start.6 = (f32[2,256,256]{2,1,0:T(8,128)S(1)}, f32[2,256,256]{2,1,0:T(8,128)}, u32[]{:S(2)}) copy-start(f32[2,256,256]{2,1,0:T(8,128)} %probe.1) | copy-start | bytes 1572868

commit v6 on v5

--- a/solution.py
+++ b/solution.py
@@ -290,11 +290,11 @@
     return lax.optimization_barrier((value, *others))[0]
 
 
-def scatter_sum(partial):
+def scatter_sum(partial, mark):
     plane = lax.axis_size(PLANE)
     core = lax.axis_index(PAIR)
     own, other = (lax.dynamic_index_in_dim(partial, k, 0, False) for k in (core, 1 - core))
-    part = own + exchanged(other, PAIR, 0)
+    part = own + exchanged(after(other, mark), PAIR, 0)
     return swap(part.reshape(plane, WIN // plane, WIN), PLANE)
 
 
@@ -303,8 +303,8 @@
     return swap(jnp.broadcast_to(part, (lax.axis_size(DEPTH),) + part.shape), DEPTH)
 
 
-def gather_sum(parts, last):
-    part = jnp.sum(parts, axis=0)
+def gather_sum(parts, mark, last):
+    part = jnp.sum(after(parts, mark), axis=0)
     core = lax.axis_index(PAIR)
     own = swap(jnp.broadcast_to(part, (lax.axis_size(PLANE),) + part.shape), PLANE).reshape(WIN, WIN)
     own = after(own, last)
@@ -323,10 +323,10 @@
     row_a, row_b, col_a, col_b = call(pack_sides, [strip] * 2 + [column] * 2, facts, objects, name="pack_sides")
     row_b, row_a = exchanged(row_b, ROW, 1), exchanged(row_a, ROW, 0)
     col_b, col_a = exchanged(col_b, COL, 1), exchanged(col_a, COL, 0)
-    scattered = scatter_sum(prev_partial[0, 0])
+    scattered = scatter_sum(prev_partial[0, 0], row_a)
     sent_a, sent_b = call(pack_corners, [corners] * 2, facts, row_a, row_b, name="pack_corners")
     corners_b, corners_a = exchanged(sent_b, COL, 1), exchanged(sent_a, COL, 0)
-    deep = depth_sum(scattered, col_a)
+    deep = depth_sum(scattered, sent_a)
     corners_a, deep = lax.optimization_barrier((corners_a, deep))
     center, row_a_part, row_b_part, col_a_part, col_b_part, partial = call(
         gradient,
@@ -350,7 +350,7 @@
     (added,) = call(add_sides, [tile], facts, center, col_a, col_b, row_a, row_b, name="add_sides")
     (new_objects,) = call(add_corners, [tile], facts, added, relayed_a, relayed_b, name="add_corners")
     rate = PROBE_RATE / math.sqrt(lax.axis_size(ROW) * lax.axis_size(COL))
-    total = gather_sum(deep, partial)
+    total = gather_sum(deep, partial, new_objects)
     new_probe = probe - rate * total
     return (new_objects, new_probe, partial[None, None])
 

time: 92.9 us -> 93.3 us (level)
  waiting for transfers between devices: 12.6 us -> 14.2 us
  local copies, waits for them, and re-layouts: 5.79 us -> 4.23 us
    ppermute x14, waiting for transfers between devices: 9.49 us -> 14.2 us  [exchanged(): return lax.ppermute(value, axis, pairs + [(j, i) for i, j in pairs])]
    all_to_all x3, waiting for transfers between devices: 3.14 us -> 0.01 us  [swap(): return lax.all_to_all(value, axes, 0, 0, tiled=True)]
    unnamed x24, local copies, waits for them, and re-layouts: 3.35 us -> 1.88 us
  transfers between devices with their start and end apart: 17 -> 17, of which waited for: 3 -> 4; matrix products, arithmetic and copies ran while one was open for 4% -> 3% of each run, Pallas kernels for 16% -> 4%
where the time goes in v6:
time: 93.3 us; the launch traced here: 91.9 us
  starting transfers between devices  53.1 us (57%)
  Pallas kernels  16.4 us (18%)
  waiting for transfers between devices  14.2 us (15%)
  local copies, waits for them, and re-layouts  4.23 us (5%)
  other arithmetic  2.41 us (3%)
  between operations  1.62 us (2%)
    ppermute x14, starting transfers between devices, exchanged(): return lax.ppermute(value, axis, pairs + [(j, i) for i, j in pairs])  37.1 us
    pallas_call x6, Pallas kernels, call(): pl.pallas_call(body, out_shape=[jax.ShapeDtypeStruct(o, jnp.float32) for...  16.4 us
    all_to_all x3, starting transfers between devices, swap(): return lax.all_to_all(value, axes, 0, 0, tiled=True)  16 us
    ppermute x14, waiting for transfers between devices, exchanged(): return lax.ppermute(value, axis, pairs + [(j, i) for i, j in pairs])  14.2 us
    unnamed x24, local copies, waits for them, and re-layouts  1.88 us
  transfers between devices with their start and end apart: 17, of which 4 were waited for; matrix products, arithmetic and copies ran while one was open for 3% of the time, Pallas kernels for 4%

profile of v6, /device:TPU:31, one launch (start us, length us, event | category | flops | bytes accessed | tf_op | source)
XLA Modules:
  0.0 91.9 jit_solution(9029902679805201071)
XLA Ops:
  1.3 0.7 pad_add_fusion.facts
  2.0 1.2 %copy-done = f32[2,2,256,256]{3,2,1,0:T(8,128)S(1)} copy-done((f32[2,2,256,256]{3,2,1,0:T(8,128)S(1)}, f32[2,2,256,256]{3,2,1,0:T(8,128)}, u32[]{:S(2)}) %copy-start) | copy-done | bytes 1048600
  3.3 0.8 pack_sides.1
  4.0 0.8 collective-permute-start
  4.8 1.0 %dynamic-slice_bitcast_fusion = f32[256,256]{1,0:T(8,128)S(1)} fusion(f32[1,1,2,256,256]{4,3,2,1,0:T(8,128)} %param.9, s32[]{:T(128)S(6)} %select_n.28), kind=kLoop, calls=%fused_computation.5 | loop fusion | bytes 524292 | tf_op jit(solution)/shard_map/jit(dynamic_index_in_dim)/squeeze | solution.py:296
  5.7 0.2 collective-permute-done.row_a
  5.9 0.4 collective-permute-start.5
  6.3 8.5 %collective-permute-start.1 = (f32[2,2,64,256]{3,2,1,0:T(8,128)S(1)}, f32[2,2,64,256]{3,2,1,0:T(8,128)S(1)}, u32[]{:S(2)}, u32[]{:S(2)}) collective-permute-start(f32[2,2,64,256]{3,2,1,0:T(8,128)S(1)} %get-tuple-element.24), channel_id=1, source_target_pairs={{16,32},{48,64},{80,96},{112,128},{144,160},{176,192},{208,224},{3... | collective-permute-start | bytes 786440 | tf_op jit(solution)/shard_map/ppermute | solution.py:282
  14.8 0.0 collective-permute-done.5
  14.8 0.0 copy-done.7
  14.8 0.7 bitcast_add_fusion
  15.6 6.3 %all-to-all-start = ((f32[16,16,256]{2,1,0:T(8,128)}), f32[16,16,256]{2,1,0:T(8,128)S(1)}, u32[]{:S(2)}, u32[]{:S(2)}) async-start(f32[16,16,256]{2,1,0:T(8,128)} %bitcast.6), calls=%async_computation | async-start | bytes 524288 | tf_op jit(solution)/shard_map/all_to_all | solution.py:286
  21.9 0.6 collective-permute-start.2
  22.5 3.2 %collective-permute-start.3 = (f32[2,256,128]{2,1,0:T(8,128)S(1)}, f32[2,256,128]{2,1,0:T(8,128)S(1)}, u32[]{:S(2)}, u32[]{:S(2)}) collective-permute-start(f32[2,256,128]{2,1,0:T(8,128)S(1)} %get-tuple-element.26), channel_id=1, source_target_pairs={{1,2},{3,4},{5,6},{7,8},{9,10},{11,12},{13,14},{2,1},{4,3},{6,5},{... | collective-permute-start | bytes 786440 | tf_op jit(solution)/shard_map/ppermute | solution.py:282
  25.7 0.0 collective-permute-done.1.row_b
  25.7 0.0 copy-start.3
  25.8 0.7 pack_corners.1
  26.4 0.0 copy-done.4
  26.5 0.0 all-to-all-done
  26.5 0.7 broadcast_in_dim.9
  27.2 3.6 %all-to-all-start.1 = ((f32[8,16,256]{2,1,0:T(8,128)}), f32[8,16,256]{2,1,0:T(8,128)S(1)}, u32[]{:S(2)}, u32[]{:S(2)}) async-start(f32[8,16,256]{2,1,0:T(8,128)} %broadcast_in_dim.9), calls=%async_computation.1 | async-start | bytes 262144 | tf_op jit(solution)/shard_map/all_to_all | solution.py:286
  30.7 0.2 collective-permute-start.4
  31.0 8.3 %collective-permute-start.6 = (f32[2,128,128]{2,1,0:T(8,128)S(1)}, f32[2,128,128]{2,1,0:T(8,128)S(1)}, u32[]{:S(2)}, u32[]{:S(2)}) collective-permute-start(f32[2,128,128]{2,1,0:T(8,128)S(1)} %get-tuple-element.31), channel_id=1, source_target_pairs={{1,2},{3,4},{5,6},{7,8},{9,10},{11,12},{13,14},{2,1},{4,3},{6,5},{... | collective-permute-start | bytes 393224 | tf_op jit(solution)/shard_map/ppermute | solution.py:282
  39.3 0.0 collective-permute-done.4.corners_a
  39.3 0.0 copy-start.10
  39.3 0.0 all-to-all-done.1
  39.3 0.0 collective-permute-done.2.col_a
  39.3 0.0 copy-start.8
  39.3 0.0 collective-permute-done.3.col_b
  39.3 0.0 copy-start.9
  39.3 3.7 %collective-permute-done.6.corners_b = f32[2,128,128]{2,1,0:T(8,128)S(1)} collective-permute-done((f32[2,128,128]{2,1,0:T(8,128)S(1)}, f32[2,128,128]{2,1,0:T(8,128)S(1)}, u32[]{:S(2)}, u32[]{:S(2)}) %collective-permute-start.6) | collective-permute-done | bytes 131104 | tf_op jit(solution)/shard_map/ppermute | solution.py:282
  43.0 0.0 copy-done.2
  43.0 0.0 copy-done.3
  43.0 0.0 copy-done.10
  43.0 0.0 copy-done.8
  43.0 0.0 copy-done.9
  43.0 0.6 copy-done.11
  43.6 12.0 %gradient.1 = (f32[2,2,256,256]{3,2,1,0:T(8,128)}, f32[2,2,64,256]{3,2,1,0:T(8,128)}, f32[2,2,64,256]{3,2,1,0:T(8,128)}, f32[2,384,128]{2,1,0:T(8,128)}, f32[2,384,128]{2,1,0:T(8,128)}, /*index=5*/f32[2,256,256]{2,1,0:T(8,128)}) custom-call(s32[5]{0:T(128)} %copy-done.4, f32[2,2,256,256]{3,2,1,0:T(8,128)} %objects.3, f32[2,2,64,256]{3,2,1,0:T(8,128)} %copy-done.2, ...), custom_call_target="tpu_custom_call" | custom-call | flops 3221225472 | bytes 5767168 | tf_op jit(solution)/shard_map/gradient/pallas_call | solution.py:268
  55.6 0.0 copy-start.1
  55.6 0.1 collective-permute-start.7
  55.7 4.6 %collective-permute-start.8 = (f32[2,384,128]{2,1,0:T(8,128)}, f32[2,384,128]{2,1,0:T(8,128)S(1)}, u32[]{:S(2)}, u32[]{:S(2)}) collective-permute-start(f32[2,384,128]{2,1,0:T(8,128)} %get-tuple-element.34), channel_id=1, source_target_pairs={{1,2},{3,4},{5,6},{7,8},{9,10},{11,12},{13,14},{2,1},{4,3},{6,5},{... | collective-permute-start | bytes 1179656 | tf_op jit(solution)/shard_map/ppermute | solution.py:282
  60.4 0.1 collective-permute-start.9
  60.5 7.4 %collective-permute-start.10 = (f32[2,2,64,256]{3,2,1,0:T(8,128)}, f32[2,2,64,256]{3,2,1,0:T(8,128)S(1)}, u32[]{:S(2)}, u32[]{:S(2)}) collective-permute-start(f32[2,2,64,256]{3,2,1,0:T(8,128)} %get-tuple-element.36), channel_id=1, source_target_pairs={{16,32},{48,64},{80,96},{112,128},{144,160},{176,192},{208,224},{3... | collective-permute-start | bytes 786440 | tf_op jit(solution)/shard_map/ppermute | solution.py:282
  67.9 0.7 broadcast_in_dim.10
  68.6 6.1 %all-to-all-start.2 = ((f32[16,16,256]{2,1,0:T(8,128)}), f32[16,16,256]{2,1,0:T(8,128)S(1)}, u32[]{:S(2)}, u32[]{:S(2)}) async-start(f32[16,16,256]{2,1,0:T(8,128)} %broadcast_in_dim.10), calls=%async_computation.2 | async-start | bytes 524288 | tf_op jit(solution)/shard_map/all_to_all | solution.py:286
  74.7 0.0 collective-permute-done.7.col_a
  74.7 0.0 collective-permute-done.8.col_b
  74.7 0.0 copy-done.5
  74.7 0.6 relay.1
  75.3 0.1 collective-permute-start.11
  75.4 2.8 %collective-permute-start.12 = (f32[2,2,64,128]{3,2,1,0:T(8,128)S(1)}, f32[2,2,64,128]{3,2,1,0:T(8,128)S(1)}, u32[]{:S(2)}, u32[]{:S(2)}) collective-permute-start(f32[2,2,64,128]{3,2,1,0:T(8,128)S(1)} %get-tuple-element.38), channel_id=1, source_target_pairs={{16,32},{48,64},{80,96},{112,128},{144,160},{176,192},{208,224},{3... | collective-permute-start | bytes 393224 | tf_op jit(solution)/shard_map/ppermute | solution.py:282
  78.2 0.0 collective-permute-done.9.row_a
  78.2 0.0 collective-permute-done.10.row_b
  78.2 0.0 copy-done.1
  78.2 0.8 add_sides.1.tile
  79.0 0.0 copy-start.6
  79.0 0.0 collective-permute-done.11.relayed_a
  79.0 8.7 %collective-permute-done.12.relayed_b = f32[2,2,64,128]{3,2,1,0:T(8,128)S(1)} collective-permute-done((f32[2,2,64,128]{3,2,1,0:T(8,128)S(1)}, f32[2,2,64,128]{3,2,1,0:T(8,128)S(1)}, u32[]{:S(2)}, u32[]{:S(2)}) %collective-permute-start.12) | collective-permute-done | bytes 131104 | tf_op jit(solution)/shard_map/ppermute | solution.py:282
  87.8 1.7 %add_corners.1 = f32[2,2,256,256]{3,2,1,0:T(8,128)} custom-call(s32[5]{0:T(128)S(1)} %copy-done.5, f32[2,2,256,256]{3,2,1,0:T(8,128)S(1)} %add_sides.1.tile, f32[2,2,64,128]{3,2,1,0:T(8,128)S(1)} %collective-permute-done.11.relayed_a, f32[2,2,64,128]{3,2,1,0:T(8,128)S(1)} %collective-permute-done.12.relayed_b), custom_call_target="tpu_custom_call" | custom-call | bytes 2097152 | tf_op jit(solution)/shard_map/add_corners/pallas_call | solution.py:268
  89.4 0.0 all-to-all-done.2
  89.4 0.0 collective-permute-start.13
  89.4 1.5 %collective-permute-done.13 = f32[256,256]{1,0:T(8,128)S(1)} collective-permute-done((f32[256,256]{1,0:T(8,128)S(1)}, f32[256,256]{1,0:T(8,128)S(1)}, u32[]{:S(2)}, u32[]{:S(2)}) %collective-permute-start.13) | collective-permute-done | bytes 262176 | tf_op jit(solution)/shard_map/ppermute | solution.py:282
  91.0 0.0 copy-done.6
  91.0 0.9 fusion
  (9 shorter events, 0.1 us)
Async XLA Ops:
  2.0 1.2 %copy-start = (f32[2,2,256,256]{3,2,1,0:T(8,128)S(1)}, f32[2,2,256,256]{3,2,1,0:T(8,128)}, u32[]{:S(2)}) copy-start(f32[2,2,256,256]{3,2,1,0:T(8,128)} %objects.3) | copy-start | bytes 3145732
  3.2 23.2 %copy-start.4 = (s32[5]{0:T(128)}, s32[5]{0:T(128)S(1)}, u32[]{:S(2)}) copy-start(s32[5]{0:T(128)S(1)} %pad_add_fusion.facts) | copy-start | bytes 64
  3.2 11.6 %copy-start.7 = (f32[1,1,2,256,256]{4,3,2,1,0:T(8,128)S(1)}, f32[1,1,2,256,256]{4,3,2,1,0:T(8,128)}, u32[]{:S(2)}) copy-start(f32[1,1,2,256,256]{4,3,2,1,0:T(8,128)} %param.9) | copy-start | bytes 1572868
  4.0 1.9 %collective-permute-start = (f32[2,2,64,256]{3,2,1,0:T(8,128)S(1)}, f32[2,2,64,256]{3,2,1,0:T(8,128)S(1)}, u32[]{:S(2)}, u32[]{:S(2)}) collective-permute-start(f32[2,2,64,256]{3,2,1,0:T(8,128)S(1)} %get-tuple-element.23), channel_id=1, source_target_pairs={{0,16},{32,48},{64,80},{96,112},{128,144},{160,176},{192,208},{224... | collective-permute-start | bytes 786440 | tf_op jit(solution)/shard_map/ppermute | solution.py:282
  5.9 37.1 %copy-start.2 = (f32[2,2,64,256]{3,2,1,0:T(8,128)}, f32[2,2,64,256]{3,2,1,0:T(8,128)S(1)}, u32[]{:S(2)}) copy-start(f32[2,2,64,256]{3,2,1,0:T(8,128)S(1)} %collective-permute-done.row_a) | copy-start | bytes 786436
  5.9 8.9 %collective-permute-start.5 = (f32[256,256]{1,0:T(8,128)S(1)}, f32[256,256]{1,0:T(8,128)S(1)}, u32[]{:S(2)}, u32[]{:S(2)}) collective-permute-start(f32[256,256]{1,0:T(8,128)S(1)} %dynamic-slice_bitcast_fusion), channel_id=1, source_target_pairs={{0,16},{16,0},{1,17},{17,1},{2,18},{18,2},{3,19},{19,3},{4,20},{20... | collective-permute-start | bytes 786440 | tf_op jit(solution)/shard_map/ppermute | solution.py:282
  6.3 19.4 %collective-permute-start.1 = (f32[2,2,64,256]{3,2,1,0:T(8,128)S(1)}, f32[2,2,64,256]{3,2,1,0:T(8,128)S(1)}, u32[]{:S(2)}, u32[]{:S(2)}) collective-permute-start(f32[2,2,64,256]{3,2,1,0:T(8,128)S(1)} %get-tuple-element.24), channel_id=1, source_target_pairs={{16,32},{48,64},{80,96},{112,128},{144,160},{176,192},{208,224},{3... | collective-permute-start | bytes 786440 | tf_op jit(solution)/shard_map/ppermute | solution.py:282
  15.6 10.9 %all-to-all-start = ((f32[16,16,256]{2,1,0:T(8,128)}), f32[16,16,256]{2,1,0:T(8,128)S(1)}, u32[]{:S(2)}, u32[]{:S(2)}) async-start(f32[16,16,256]{2,1,0:T(8,128)} %bitcast.6), calls=%async_computation | async-start | bytes 524288 | tf_op jit(solution)/shard_map/all_to_all | solution.py:286
  21.9 17.4 %collective-permute-start.2 = (f32[2,256,128]{2,1,0:T(8,128)S(1)}, f32[2,256,128]{2,1,0:T(8,128)S(1)}, u32[]{:S(2)}, u32[]{:S(2)}) collective-permute-start(f32[2,256,128]{2,1,0:T(8,128)S(1)} %get-tuple-element.25), channel_id=1, source_target_pairs={{0,1},{2,3},{4,5},{6,7},{8,9},{10,11},{12,13},{14,15},{1,0},{3,2},... | collective-permute-start | bytes 786440 | tf_op jit(solution)/shard_map/ppermute | solution.py:282
  22.5 16.8 %collective-permute-start.3 = (f32[2,256,128]{2,1,0:T(8,128)S(1)}, f32[2,256,128]{2,1,0:T(8,128)S(1)}, u32[]{:S(2)}, u32[]{:S(2)}) collective-permute-start(f32[2,256,128]{2,1,0:T(8,128)S(1)} %get-tuple-element.26), channel_id=1, source_target_pairs={{1,2},{3,4},{5,6},{7,8},{9,10},{11,12},{13,14},{2,1},{4,3},{6,5},{... | collective-permute-start | bytes 786440 | tf_op jit(solution)/shard_map/ppermute | solution.py:282
  25.7 17.3 %copy-start.3 = (f32[2,2,64,256]{3,2,1,0:T(8,128)}, f32[2,2,64,256]{3,2,1,0:T(8,128)S(1)}, u32[]{:S(2)}) copy-start(f32[2,2,64,256]{3,2,1,0:T(8,128)S(1)} %collective-permute-done.1.row_b) | copy-start | bytes 786436
  27.2 12.1 %all-to-all-start.1 = ((f32[8,16,256]{2,1,0:T(8,128)}), f32[8,16,256]{2,1,0:T(8,128)S(1)}, u32[]{:S(2)}, u32[]{:S(2)}) async-start(f32[8,16,256]{2,1,0:T(8,128)} %broadcast_in_dim.9), calls=%async_computation.1 | async-start | bytes 262144 | tf_op jit(solution)/shard_map/all_to_all | solution.py:286
  30.7 8.5 %collective-permute-start.4 = (f32[2,128,128]{2,1,0:T(8,128)S(1)}, f32[2,128,128]{2,1,0:T(8,128)S(1)}, u32[]{:S(2)}, u32[]{:S(2)}) collective-permute-start(f32[2,128,128]{2,1,0:T(8,128)S(1)} %get-tuple-element.27), channel_id=1, source_target_pairs={{0,1},{2,3},{4,5},{6,7},{8,9},{10,11},{12,13},{14,15},{1,0},{3,2},... | collective-permute-start | bytes 393224 | tf_op jit(solution)/shard_map/ppermute | solution.py:282
  31.0 12.0 %collective-permute-start.6 = (f32[2,128,128]{2,1,0:T(8,128)S(1)}, f32[2,128,128]{2,1,0:T(8,128)S(1)}, u32[]{:S(2)}, u32[]{:S(2)}) collective-permute-start(f32[2,128,128]{2,1,0:T(8,128)S(1)} %get-tuple-element.31), channel_id=1, source_target_pairs={{1,2},{3,4},{5,6},{7,8},{9,10},{11,12},{13,14},{2,1},{4,3},{6,5},{... | collective-permute-start | bytes 393224 | tf_op jit(solution)/shard_map/ppermute | solution.py:282
  39.3 3.7 %copy-start.10 = (f32[2,128,128]{2,1,0:T(8,128)}, f32[2,128,128]{2,1,0:T(8,128)S(1)}, u32[]{:S(2)}) copy-start(f32[2,128,128]{2,1,0:T(8,128)S(1)} %collective-permute-done.4.corners_a) | copy-start | bytes 393220
  39.3 3.7 %copy-start.8 = (f32[2,256,128]{2,1,0:T(8,128)}, f32[2,256,128]{2,1,0:T(8,128)S(1)}, u32[]{:S(2)}) copy-start(f32[2,256,128]{2,1,0:T(8,128)S(1)} %collective-permute-done.2.col_a) | copy-start | bytes 786436
  39.3 3.7 %copy-start.9 = (f32[2,256,128]{2,1,0:T(8,128)}, f32[2,256,128]{2,1,0:T(8,128)S(1)}, u32[]{:S(2)}) copy-start(f32[2,256,128]{2,1,0:T(8,128)S(1)} %collective-permute-done.3.col_b) | copy-start | bytes 786436
  43.0 0.6 copy-start.11
  43.6 31.1 %copy-start.5 = (s32[5]{0:T(128)S(1)}, s32[5]{0:T(128)}, u32[]{:S(2)}) copy-start(s32[5]{0:T(128)} %copy-done.4) | copy-start | bytes 64
  55.6 22.6 %copy-start.1 = (f32[2,2,256,256]{3,2,1,0:T(8,128)S(1)}, f32[2,2,256,256]{3,2,1,0:T(8,128)}, u32[]{:S(2)}) copy-start(f32[2,2,256,256]{3,2,1,0:T(8,128)} %get-tuple-element.32.center) | copy-start | bytes 3145732
  55.6 19.1 %collective-permute-start.7 = (f32[2,384,128]{2,1,0:T(8,128)}, f32[2,384,128]{2,1,0:T(8,128)S(1)}, u32[]{:S(2)}, u32[]{:S(2)}) collective-permute-start(f32[2,384,128]{2,1,0:T(8,128)} %get-tuple-element.33), channel_id=1, source_target_pairs={{0,1},{2,3},{4,5},{6,7},{8,9},{10,11},{12,13},{14,15},{1,0},{3,2},... | collective-permute-start | bytes 1179656 | tf_op jit(solution)/shard_map/ppermute | solution.py:282
  55.7 19.0 %collective-permute-start.8 = (f32[2,384,128]{2,1,0:T(8,128)}, f32[2,384,128]{2,1,0:T(8,128)S(1)}, u32[]{:S(2)}, u32[]{:S(2)}) collective-permute-start(f32[2,384,128]{2,1,0:T(8,128)} %get-tuple-element.34), channel_id=1, source_target_pairs={{1,2},{3,4},{5,6},{7,8},{9,10},{11,12},{13,14},{2,1},{4,3},{6,5},{... | collective-permute-start | bytes 1179656 | tf_op jit(solution)/shard_map/ppermute | solution.py:282
  60.4 17.8 %collective-permute-start.9 = (f32[2,2,64,256]{3,2,1,0:T(8,128)}, f32[2,2,64,256]{3,2,1,0:T(8,128)S(1)}, u32[]{:S(2)}, u32[]{:S(2)}) collective-permute-start(f32[2,2,64,256]{3,2,1,0:T(8,128)} %get-tuple-element.35), channel_id=1, source_target_pairs={{0,16},{32,48},{64,80},{96,112},{128,144},{160,176},{192,208},{224... | collective-permute-start | bytes 786440 | tf_op jit(solution)/shard_map/ppermute | solution.py:282
  60.5 17.7 %collective-permute-start.10 = (f32[2,2,64,256]{3,2,1,0:T(8,128)}, f32[2,2,64,256]{3,2,1,0:T(8,128)S(1)}, u32[]{:S(2)}, u32[]{:S(2)}) collective-permute-start(f32[2,2,64,256]{3,2,1,0:T(8,128)} %get-tuple-element.36), channel_id=1, source_target_pairs={{16,32},{48,64},{80,96},{112,128},{144,160},{176,192},{208,224},{3... | collective-permute-start | bytes 786440 | tf_op jit(solution)/shard_map/ppermute | solution.py:282
  68.6 20.8 %all-to-all-start.2 = ((f32[16,16,256]{2,1,0:T(8,128)}), f32[16,16,256]{2,1,0:T(8,128)S(1)}, u32[]{:S(2)}, u32[]{:S(2)}) async-start(f32[16,16,256]{2,1,0:T(8,128)} %broadcast_in_dim.10), calls=%async_computation.2 | async-start | bytes 524288 | tf_op jit(solution)/shard_map/all_to_all | solution.py:286
  75.3 3.8 %collective-permute-start.11 = (f32[2,2,64,128]{3,2,1,0:T(8,128)S(1)}, f32[2,2,64,128]{3,2,1,0:T(8,128)S(1)}, u32[]{:S(2)}, u32[]{:S(2)}) collective-permute-start(f32[2,2,64,128]{3,2,1,0:T(8,128)S(1)} %get-tuple-element.37), channel_id=1, source_target_pairs={{0,16},{32,48},{64,80},{96,112},{128,144},{160,176},{192,208},{224... | collective-permute-start | bytes 393224 | tf_op jit(solution)/shard_map/ppermute | solution.py:282
  75.4 12.4 %collective-permute-start.12 = (f32[2,2,64,128]{3,2,1,0:T(8,128)S(1)}, f32[2,2,64,128]{3,2,1,0:T(8,128)S(1)}, u32[]{:S(2)}, u32[]{:S(2)}) collective-permute-start(f32[2,2,64,128]{3,2,1,0:T(8,128)S(1)} %get-tuple-element.38), channel_id=1, source_target_pairs={{16,32},{48,64},{80,96},{112,128},{144,160},{176,192},{208,224},{3... | collective-permute-start | bytes 393224 | tf_op jit(solution)/shard_map/ppermute | solution.py:282
  79.0 12.0 %copy-start.6 = (f32[2,256,256]{2,1,0:T(8,128)S(1)}, f32[2,256,256]{2,1,0:T(8,128)}, u32[]{:S(2)}) copy-start(f32[2,256,256]{2,1,0:T(8,128)} %probe.1) | copy-start | bytes 1572868
  89.4 1.5 %collective-permute-start.13 = (f32[256,256]{1,0:T(8,128)S(1)}, f32[256,256]{1,0:T(8,128)S(1)}, u32[]{:S(2)}, u32[]{:S(2)}) collective-permute-start(f32[256,256]{1,0:T(8,128)S(1)} %bitcast.17), channel_id=1, source_target_pairs={{0,16},{16,0},{1,17},{17,1},{2,18},{18,2},{3,19},{19,3},{4,20},{20... | collective-permute-start | bytes 786440 | tf_op jit(solution)/shard_map/ppermute | solution.py:282

commit v7 on v5

--- a/solution.py
+++ b/solution.py
@@ -41,7 +41,7 @@
     for matrix in (propagate, forward):
         matrix = (matrix + matrix.T) / 2
         halves = []
-        for part in (matrix.real, matrix.imag, -matrix.imag):
+        for part in (matrix.real, matrix.imag, matrix.real + matrix.imag):
             high = part.astype(np.float32).astype(ml_dtypes.bfloat16)
             low = (part - high.astype(np.float64)).astype(np.float32)
             halves.append((high, low.astype(ml_dtypes.bfloat16)))
@@ -65,17 +65,16 @@
 
 
 def sandwich(mats, which, real_part, imag_part):
-    def block(rows):
-        return jnp.concatenate(
-            [jnp.concatenate([mats[6 * which + k] for k in row], axis=1) for row in rows], axis=0
-        )
-
-    right = tuple(block(((3 * h, 3 * h + 1), (3 * h + 2, 3 * h))) for h in range(2))
-    left = tuple(block(((3 * h, 3 * h + 2), (3 * h + 1, 3 * h))) for h in range(2))
-    inner = three(halves_of(jnp.concatenate([real_part, imag_part], axis=1)), right)
-    stacked = jnp.concatenate([inner[:, :WIN], inner[:, WIN:]], axis=0)
-    outer = three(left, halves_of(stacked))
-    return outer[:WIN], outer[WIN:]
+    def halves(k):
+        return mats[6 * which + k], mats[6 * which + 3 + k]
+
+    def combine(real_real, imag_imag, both):
+        return real_real - imag_imag, both - real_real - imag_imag
+
+    parts = (real_part, imag_part, real_part + imag_part)
+    real_part, imag_part = combine(*(three(halves_of(part), halves(k)) for k, part in enumerate(parts)))
+    parts = (real_part, imag_part, real_part + imag_part)
+    return combine(*(three(halves(k), halves_of(part)) for k, part in enumerate(parts)))
 
 
 def first_half(shape):

time: 92.9 us -> 90.5 us (0.974)
  Pallas kernels: 16.4 us -> 14 us
    pallas_call x6, Pallas kernels: 16.4 us -> 14 us  [call(): pl.pallas_call(body, out_shape=[jax.ShapeDtypeStruct(o, jnp.float32) for...]
  transfers between devices with their start and end apart: 17 -> 17, of which waited for: 3 -> 3; matrix products, arithmetic and copies ran while one was open for 4% -> 4% of each run, Pallas kernels for 16% -> 14%
where the time goes in v7:
time: 90.5 us; the launch traced here: 89.7 us
  starting transfers between devices  53.3 us (59%)
  Pallas kernels  14 us (15%)
  waiting for transfers between devices  12.7 us (14%)
  local copies, waits for them, and re-layouts  5.79 us (6%)
  other arithmetic  2.41 us (3%)
  between operations  1.62 us (2%)
    ppermute x14, starting transfers between devices, exchanged(): return lax.ppermute(value, axis, pairs + [(j, i) for i, j in pairs])  36.6 us
    all_to_all x3, starting transfers between devices, swap(): return lax.all_to_all(value, axes, 0, 0, tiled=True)  16.7 us
    pallas_call x6, Pallas kernels, call(): pl.pallas_call(body, out_shape=[jax.ShapeDtypeStruct(o, jnp.float32) for...  14 us
    ppermute x14, waiting for transfers between devices, exchanged(): return lax.ppermute(value, axis, pairs + [(j, i) for i, j in pairs])  9.51 us
    unnamed x24, local copies, waits for them, and re-layouts  3.35 us
    all_to_all x3, waiting for transfers between devices, swap(): return lax.all_to_all(value, axes, 0, 0, tiled=True)  3.14 us
  transfers between devices with their start and end apart: 17, of which 3 were waited for; matrix products, arithmetic and copies ran while one was open for 4% of the time, Pallas kernels for 14%

profile of v7, /device:TPU:31, one launch (start us, length us, event | category | flops | bytes accessed | tf_op | source)
XLA Modules:
  0.0 89.7 jit_solution(14313186009257546607)
XLA Ops:
  0.6 0.0 copy-start.7
  0.6 1.0 %dynamic-slice_bitcast_fusion = f32[256,256]{1,0:T(8,128)S(1)} fusion(f32[1,1,2,256,256]{4,3,2,1,0:T(8,128)} %param.9, s32[]{:T(128)S(6)} %select_n.28), kind=kLoop, calls=%fused_computation.5 | loop fusion | bytes 524292 | tf_op jit(solution)/shard_map/jit(dynamic_index_in_dim)/squeeze | solution.py:295
  1.7 0.8 collective-permute-start.5
  3.1 0.7 pad_add_fusion.facts
  3.8 1.2 %copy-done = f32[2,2,256,256]{3,2,1,0:T(8,128)S(1)} copy-done((f32[2,2,256,256]{3,2,1,0:T(8,128)S(1)}, f32[2,2,256,256]{3,2,1,0:T(8,128)}, u32[]{:S(2)}) %copy-start) | copy-done | bytes 1048600
  5.1 0.8 pack_sides.1
  5.8 0.6 collective-permute-start.2
  6.4 0.0 collective-permute-done.5
  6.5 0.0 copy-done.7
  6.5 0.7 bitcast_add_fusion
  7.2 6.9 %all-to-all-start = ((f32[16,16,256]{2,1,0:T(8,128)}), f32[16,16,256]{2,1,0:T(8,128)S(1)}, u32[]{:S(2)}, u32[]{:S(2)}) async-start(f32[16,16,256]{2,1,0:T(8,128)} %bitcast.6), calls=%async_computation | async-start | bytes 524288 | tf_op jit(solution)/shard_map/all_to_all | solution.py:285
  14.1 0.9 collective-permute-start
  14.9 8.7 %collective-permute-start.1 = (f32[2,2,64,256]{3,2,1,0:T(8,128)S(1)}, f32[2,2,64,256]{3,2,1,0:T(8,128)S(1)}, u32[]{:S(2)}, u32[]{:S(2)}) collective-permute-start(f32[2,2,64,256]{3,2,1,0:T(8,128)S(1)} %get-tuple-element.22), channel_id=1, source_target_pairs={{16,32},{48,64},{80,96},{112,128},{144,160},{176,192},{208,224},{3... | collective-permute-start | bytes 786440 | tf_op jit(solution)/shard_map/ppermute | solution.py:281
  23.7 2.3 %collective-permute-start.3 = (f32[2,256,128]{2,1,0:T(8,128)S(1)}, f32[2,256,128]{2,1,0:T(8,128)S(1)}, u32[]{:S(2)}, u32[]{:S(2)}) collective-permute-start(f32[2,256,128]{2,1,0:T(8,128)S(1)} %get-tuple-element.24), channel_id=1, source_target_pairs={{1,2},{3,4},{5,6},{7,8},{9,10},{11,12},{13,14},{2,1},{4,3},{6,5},{... | collective-permute-start | bytes 786440 | tf_op jit(solution)/shard_map/ppermute | solution.py:281
  25.9 0.0 collective-permute-done.2.col_a
  26.0 0.0 copy-start.8
  26.0 0.0 all-to-all-done
  26.0 0.7 broadcast_in_dim.9
  26.7 3.4 %all-to-all-start.1 = ((f32[8,16,256]{2,1,0:T(8,128)}), f32[8,16,256]{2,1,0:T(8,128)S(1)}, u32[]{:S(2)}, u32[]{:S(2)}) async-start(f32[8,16,256]{2,1,0:T(8,128)} %broadcast_in_dim.9), calls=%async_computation.1 | async-start | bytes 262144 | tf_op jit(solution)/shard_map/all_to_all | solution.py:285
  30.1 0.0 collective-permute-done.row_a
  30.1 0.0 copy-start.2
  30.1 0.0 collective-permute-done.1.row_b
  30.1 0.0 copy-start.3
  30.1 0.7 pack_corners.1
  30.8 0.0 copy-done.4
  30.8 0.6 collective-permute-start.4
  31.4 4.9 %collective-permute-start.6 = (f32[2,128,128]{2,1,0:T(8,128)S(1)}, f32[2,128,128]{2,1,0:T(8,128)S(1)}, u32[]{:S(2)}, u32[]{:S(2)}) collective-permute-start(f32[2,128,128]{2,1,0:T(8,128)S(1)} %get-tuple-element.28), channel_id=1, source_target_pairs={{1,2},{3,4},{5,6},{7,8},{9,10},{11,12},{13,14},{2,1},{4,3},{6,5},{... | collective-permute-start | bytes 393224 | tf_op jit(solution)/shard_map/ppermute | solution.py:281
  36.3 0.0 collective-permute-done.4.corners_a
  36.3 0.0 copy-start.10
  36.3 3.1 %all-to-all-done.1 = f32[8,16,256]{2,1,0:T(8,128)S(1)} async-done(((f32[8,16,256]{2,1,0:T(8,128)}), f32[8,16,256]{2,1,0:T(8,128)S(1)}, u32[]{:S(2)}, u32[]{:S(2)}) %all-to-all-start.1) | async-done | bytes 131104 | tf_op jit(solution)/shard_map/all_to_all | solution.py:285
  39.5 0.7 broadcast_in_dim.10
  40.2 6.4 %all-to-all-start.2 = ((f32[16,16,256]{2,1,0:T(8,128)}), f32[16,16,256]{2,1,0:T(8,128)S(1)}, u32[]{:S(2)}, u32[]{:S(2)}) async-start(f32[16,16,256]{2,1,0:T(8,128)} %broadcast_in_dim.10), calls=%async_computation.2 | async-start | bytes 524288 | tf_op jit(solution)/shard_map/all_to_all | solution.py:285
  46.6 0.0 collective-permute-done.3.col_b
  46.6 0.0 collective-permute-done.6.corners_b
  46.6 0.0 copy-start.11
  46.6 0.0 copy-done.8
  46.6 0.0 copy-done.2
  46.7 0.0 copy-done.3
  46.7 0.0 copy-done.10
  46.7 0.6 copy-done.9
  47.3 0.0 copy-done.11
  47.4 9.6 %gradient.1 = (f32[2,2,256,256]{3,2,1,0:T(8,128)}, f32[2,2,64,256]{3,2,1,0:T(8,128)}, f32[2,2,64,256]{3,2,1,0:T(8,128)}, f32[2,384,128]{2,1,0:T(8,128)}, f32[2,384,128]{2,1,0:T(8,128)}, /*index=5*/f32[2,256,256]{2,1,0:T(8,128)}) custom-call(s32[5]{0:T(128)} %copy-done.4, f32[2,2,256,256]{3,2,1,0:T(8,128)} %objects.3, f32[2,2,64,256]{3,2,1,0:T(8,128)} %copy-done.2, ...), custom_call_target="tpu_custom_call" | custom-call | flops 3221225472 | bytes 5767168 | tf_op jit(solution)/shard_map/gradient/pallas_call | solution.py:267
  56.9 0.7 collective-permute-start.7
  57.6 2.6 %collective-permute-start.8 = (f32[2,384,128]{2,1,0:T(8,128)}, f32[2,384,128]{2,1,0:T(8,128)S(1)}, u32[]{:S(2)}, u32[]{:S(2)}) collective-permute-start(f32[2,384,128]{2,1,0:T(8,128)} %get-tuple-element.31), channel_id=1, source_target_pairs={{1,2},{3,4},{5,6},{7,8},{9,10},{11,12},{13,14},{2,1},{4,3},{6,5},{... | collective-permute-start | bytes 1179656 | tf_op jit(solution)/shard_map/ppermute | solution.py:281
  60.2 1.8 %collective-permute-start.9 = (f32[2,2,64,256]{3,2,1,0:T(8,128)}, f32[2,2,64,256]{3,2,1,0:T(8,128)S(1)}, u32[]{:S(2)}, u32[]{:S(2)}) collective-permute-start(f32[2,2,64,256]{3,2,1,0:T(8,128)} %get-tuple-element.32), channel_id=1, source_target_pairs={{0,16},{32,48},{64,80},{96,112},{128,144},{160,176},{192,208},{224... | collective-permute-start | bytes 786440 | tf_op jit(solution)/shard_map/ppermute | solution.py:281
  62.0 5.6 %collective-permute-start.10 = (f32[2,2,64,256]{3,2,1,0:T(8,128)}, f32[2,2,64,256]{3,2,1,0:T(8,128)S(1)}, u32[]{:S(2)}, u32[]{:S(2)}) collective-permute-start(f32[2,2,64,256]{3,2,1,0:T(8,128)} %get-tuple-element.33), channel_id=1, source_target_pairs={{16,32},{48,64},{80,96},{112,128},{144,160},{176,192},{208,224},{3... | collective-permute-start | bytes 786440 | tf_op jit(solution)/shard_map/ppermute | solution.py:281
  67.7 0.0 all-to-all-done.2
  67.7 0.1 collective-permute-start.13
  67.8 0.0 collective-permute-done.7.col_a
  67.8 3.3 %collective-permute-done.8.col_b = f32[2,384,128]{2,1,0:T(8,128)S(1)} collective-permute-done((f32[2,384,128]{2,1,0:T(8,128)}, f32[2,384,128]{2,1,0:T(8,128)S(1)}, u32[]{:S(2)}, u32[]{:S(2)}) %collective-permute-start.8) | collective-permute-done | bytes 393248 | tf_op jit(solution)/shard_map/ppermute | solution.py:281
  71.1 0.6 relay.1
  71.7 4.1 %collective-permute-start.11 = (f32[2,2,64,128]{3,2,1,0:T(8,128)S(1)}, f32[2,2,64,128]{3,2,1,0:T(8,128)S(1)}, u32[]{:S(2)}, u32[]{:S(2)}) collective-permute-start(f32[2,2,64,128]{3,2,1,0:T(8,128)S(1)} %get-tuple-element.34), channel_id=1, source_target_pairs={{0,16},{32,48},{64,80},{96,112},{128,144},{160,176},{192,208},{224... | collective-permute-start | bytes 393224 | tf_op jit(solution)/shard_map/ppermute | solution.py:281
  75.8 3.0 %collective-permute-start.12 = (f32[2,2,64,128]{3,2,1,0:T(8,128)S(1)}, f32[2,2,64,128]{3,2,1,0:T(8,128)S(1)}, u32[]{:S(2)}, u32[]{:S(2)}) collective-permute-start(f32[2,2,64,128]{3,2,1,0:T(8,128)S(1)} %get-tuple-element.35), channel_id=1, source_target_pairs={{16,32},{48,64},{80,96},{112,128},{144,160},{176,192},{208,224},{3... | collective-permute-start | bytes 393224 | tf_op jit(solution)/shard_map/ppermute | solution.py:281
  78.7 0.0 collective-permute-done.9.row_a
  78.7 0.0 collective-permute-done.10.row_b
  78.8 0.0 copy-start.1
  78.8 1.2 %copy-done.1 = f32[2,2,256,256]{3,2,1,0:T(8,128)S(1)} copy-done((f32[2,2,256,256]{3,2,1,0:T(8,128)S(1)}, f32[2,2,256,256]{3,2,1,0:T(8,128)}, u32[]{:S(2)}) %copy-start.1) | copy-done | bytes 1048600
  80.0 0.8 add_sides.1.tile
  80.8 0.0 collective-permute-done.13
  80.8 0.2 copy-done.6
  81.0 0.9 fusion
  81.9 0.0 collective-permute-done.11.relayed_a
  81.9 6.2 %collective-permute-done.12.relayed_b = f32[2,2,64,128]{3,2,1,0:T(8,128)S(1)} collective-permute-done((f32[2,2,64,128]{3,2,1,0:T(8,128)S(1)}, f32[2,2,64,128]{3,2,1,0:T(8,128)S(1)}, u32[]{:S(2)}, u32[]{:S(2)}) %collective-permute-start.12) | collective-permute-done | bytes 131104 | tf_op jit(solution)/shard_map/ppermute | solution.py:281
  88.1 1.7 %add_corners.1 = f32[2,2,256,256]{3,2,1,0:T(8,128)} custom-call(s32[5]{0:T(128)S(1)} %copy-done.5, f32[2,2,256,256]{3,2,1,0:T(8,128)S(1)} %add_sides.1.tile, f32[2,2,64,128]{3,2,1,0:T(8,128)S(1)} %collective-permute-done.11.relayed_a, f32[2,2,64,128]{3,2,1,0:T(8,128)S(1)} %collective-permute-done.12.relayed_b), custom_call_target="tpu_custom_call" | custom-call | bytes 2097152 | tf_op jit(solution)/shard_map/add_corners/pallas_call | solution.py:267
  (9 shorter events, 0.1 us)
Async XLA Ops:
  0.6 5.8 %copy-start.7 = (f32[1,1,2,256,256]{4,3,2,1,0:T(8,128)S(1)}, f32[1,1,2,256,256]{4,3,2,1,0:T(8,128)}, u32[]{:S(2)}) copy-start(f32[1,1,2,256,256]{4,3,2,1,0:T(8,128)} %param.9) | copy-start | bytes 1572868
  1.7 4.8 %collective-permute-start.5 = (f32[256,256]{1,0:T(8,128)S(1)}, f32[256,256]{1,0:T(8,128)S(1)}, u32[]{:S(2)}, u32[]{:S(2)}) collective-permute-start(f32[256,256]{1,0:T(8,128)S(1)} %dynamic-slice_bitcast_fusion), channel_id=1, source_target_pairs={{0,16},{16,0},{1,17},{17,1},{2,18},{18,2},{3,19},{19,3},{4,20},{20... | collective-permute-start | bytes 786440 | tf_op jit(solution)/shard_map/ppermute | solution.py:281
  3.8 1.2 %copy-start = (f32[2,2,256,256]{3,2,1,0:T(8,128)S(1)}, f32[2,2,256,256]{3,2,1,0:T(8,128)}, u32[]{:S(2)}) copy-start(f32[2,2,256,256]{3,2,1,0:T(8,128)} %objects.3) | copy-start | bytes 3145732
  5.1 25.7 %copy-start.4 = (s32[5]{0:T(128)}, s32[5]{0:T(128)S(1)}, u32[]{:S(2)}) copy-start(s32[5]{0:T(128)S(1)} %pad_add_fusion.facts) | copy-start | bytes 64
  5.8 20.1 %collective-permute-start.2 = (f32[2,256,128]{2,1,0:T(8,128)S(1)}, f32[2,256,128]{2,1,0:T(8,128)S(1)}, u32[]{:S(2)}, u32[]{:S(2)}) collective-permute-start(f32[2,256,128]{2,1,0:T(8,128)S(1)} %get-tuple-element.23), channel_id=1, source_target_pairs={{0,1},{2,3},{4,5},{6,7},{8,9},{10,11},{12,13},{14,15},{1,0},{3,2},... | collective-permute-start | bytes 786440 | tf_op jit(solution)/shard_map/ppermute | solution.py:281
  7.2 18.8 %all-to-all-start = ((f32[16,16,256]{2,1,0:T(8,128)}), f32[16,16,256]{2,1,0:T(8,128)S(1)}, u32[]{:S(2)}, u32[]{:S(2)}) async-start(f32[16,16,256]{2,1,0:T(8,128)} %bitcast.6), calls=%async_computation | async-start | bytes 524288 | tf_op jit(solution)/shard_map/all_to_all | solution.py:285
  14.1 16.0 %collective-permute-start = (f32[2,2,64,256]{3,2,1,0:T(8,128)S(1)}, f32[2,2,64,256]{3,2,1,0:T(8,128)S(1)}, u32[]{:S(2)}, u32[]{:S(2)}) collective-permute-start(f32[2,2,64,256]{3,2,1,0:T(8,128)S(1)} %get-tuple-element.21), channel_id=1, source_target_pairs={{0,16},{32,48},{64,80},{96,112},{128,144},{160,176},{192,208},{224... | collective-permute-start | bytes 786440 | tf_op jit(solution)/shard_map/ppermute | solution.py:281
  14.9 15.2 %collective-permute-start.1 = (f32[2,2,64,256]{3,2,1,0:T(8,128)S(1)}, f32[2,2,64,256]{3,2,1,0:T(8,128)S(1)}, u32[]{:S(2)}, u32[]{:S(2)}) collective-permute-start(f32[2,2,64,256]{3,2,1,0:T(8,128)S(1)} %get-tuple-element.22), channel_id=1, source_target_pairs={{16,32},{48,64},{80,96},{112,128},{144,160},{176,192},{208,224},{3... | collective-permute-start | bytes 786440 | tf_op jit(solution)/shard_map/ppermute | solution.py:281
  23.7 22.9 %collective-permute-start.3 = (f32[2,256,128]{2,1,0:T(8,128)S(1)}, f32[2,256,128]{2,1,0:T(8,128)S(1)}, u32[]{:S(2)}, u32[]{:S(2)}) collective-permute-start(f32[2,256,128]{2,1,0:T(8,128)S(1)} %get-tuple-element.24), channel_id=1, source_target_pairs={{1,2},{3,4},{5,6},{7,8},{9,10},{11,12},{13,14},{2,1},{4,3},{6,5},{... | collective-permute-start | bytes 786440 | tf_op jit(solution)/shard_map/ppermute | solution.py:281
  26.0 20.7 %copy-start.8 = (f32[2,256,128]{2,1,0:T(8,128)}, f32[2,256,128]{2,1,0:T(8,128)S(1)}, u32[]{:S(2)}) copy-start(f32[2,256,128]{2,1,0:T(8,128)S(1)} %collective-permute-done.2.col_a) | copy-start | bytes 786436
  26.7 12.8 %all-to-all-start.1 = ((f32[8,16,256]{2,1,0:T(8,128)}), f32[8,16,256]{2,1,0:T(8,128)S(1)}, u32[]{:S(2)}, u32[]{:S(2)}) async-start(f32[8,16,256]{2,1,0:T(8,128)} %broadcast_in_dim.9), calls=%async_computation.1 | async-start | bytes 262144 | tf_op jit(solution)/shard_map/all_to_all | solution.py:285
  30.1 16.6 %copy-start.2 = (f32[2,2,64,256]{3,2,1,0:T(8,128)}, f32[2,2,64,256]{3,2,1,0:T(8,128)S(1)}, u32[]{:S(2)}) copy-start(f32[2,2,64,256]{3,2,1,0:T(8,128)S(1)} %collective-permute-done.row_a) | copy-start | bytes 786436
  30.1 16.6 %copy-start.3 = (f32[2,2,64,256]{3,2,1,0:T(8,128)}, f32[2,2,64,256]{3,2,1,0:T(8,128)S(1)}, u32[]{:S(2)}) copy-start(f32[2,2,64,256]{3,2,1,0:T(8,128)S(1)} %collective-permute-done.1.row_b) | copy-start | bytes 786436
  30.8 5.5 %collective-permute-start.4 = (f32[2,128,128]{2,1,0:T(8,128)S(1)}, f32[2,128,128]{2,1,0:T(8,128)S(1)}, u32[]{:S(2)}, u32[]{:S(2)}) collective-permute-start(f32[2,128,128]{2,1,0:T(8,128)S(1)} %get-tuple-element.25), channel_id=1, source_target_pairs={{0,1},{2,3},{4,5},{6,7},{8,9},{10,11},{12,13},{14,15},{1,0},{3,2},... | collective-permute-start | bytes 393224 | tf_op jit(solution)/shard_map/ppermute | solution.py:281
  31.4 15.2 %collective-permute-start.6 = (f32[2,128,128]{2,1,0:T(8,128)S(1)}, f32[2,128,128]{2,1,0:T(8,128)S(1)}, u32[]{:S(2)}, u32[]{:S(2)}) collective-permute-start(f32[2,128,128]{2,1,0:T(8,128)S(1)} %get-tuple-element.28), channel_id=1, source_target_pairs={{1,2},{3,4},{5,6},{7,8},{9,10},{11,12},{13,14},{2,1},{4,3},{6,5},{... | collective-permute-start | bytes 393224 | tf_op jit(solution)/shard_map/ppermute | solution.py:281
  36.3 10.4 %copy-start.10 = (f32[2,128,128]{2,1,0:T(8,128)}, f32[2,128,128]{2,1,0:T(8,128)S(1)}, u32[]{:S(2)}) copy-start(f32[2,128,128]{2,1,0:T(8,128)S(1)} %collective-permute-done.4.corners_a) | copy-start | bytes 393220
  40.2 27.5 %all-to-all-start.2 = ((f32[16,16,256]{2,1,0:T(8,128)}), f32[16,16,256]{2,1,0:T(8,128)S(1)}, u32[]{:S(2)}, u32[]{:S(2)}) async-start(f32[16,16,256]{2,1,0:T(8,128)} %broadcast_in_dim.10), calls=%async_computation.2 | async-start | bytes 524288 | tf_op jit(solution)/shard_map/all_to_all | solution.py:285
  46.6 0.7 copy-start.9
  46.6 0.7 copy-start.11
  47.4 23.8 %copy-start.5 = (s32[5]{0:T(128)S(1)}, s32[5]{0:T(128)}, u32[]{:S(2)}) copy-start(s32[5]{0:T(128)} %copy-done.4) | copy-start | bytes 64
  56.9 10.9 %collective-permute-start.7 = (f32[2,384,128]{2,1,0:T(8,128)}, f32[2,384,128]{2,1,0:T(8,128)S(1)}, u32[]{:S(2)}, u32[]{:S(2)}) collective-permute-start(f32[2,384,128]{2,1,0:T(8,128)} %get-tuple-element.30), channel_id=1, source_target_pairs={{0,1},{2,3},{4,5},{6,7},{8,9},{10,11},{12,13},{14,15},{1,0},{3,2},... | collective-permute-start | bytes 1179656 | tf_op jit(solution)/shard_map/ppermute | solution.py:281
  57.6 13.5 %collective-permute-start.8 = (f32[2,384,128]{2,1,0:T(8,128)}, f32[2,384,128]{2,1,0:T(8,128)S(1)}, u32[]{:S(2)}, u32[]{:S(2)}) collective-permute-start(f32[2,384,128]{2,1,0:T(8,128)} %get-tuple-element.31), channel_id=1, source_target_pairs={{1,2},{3,4},{5,6},{7,8},{9,10},{11,12},{13,14},{2,1},{4,3},{6,5},{... | collective-permute-start | bytes 1179656 | tf_op jit(solution)/shard_map/ppermute | solution.py:281
  60.2 18.5 %collective-permute-start.9 = (f32[2,2,64,256]{3,2,1,0:T(8,128)}, f32[2,2,64,256]{3,2,1,0:T(8,128)S(1)}, u32[]{:S(2)}, u32[]{:S(2)}) collective-permute-start(f32[2,2,64,256]{3,2,1,0:T(8,128)} %get-tuple-element.32), channel_id=1, source_target_pairs={{0,16},{32,48},{64,80},{96,112},{128,144},{160,176},{192,208},{224... | collective-permute-start | bytes 786440 | tf_op jit(solution)/shard_map/ppermute | solution.py:281
  62.0 16.7 %collective-permute-start.10 = (f32[2,2,64,256]{3,2,1,0:T(8,128)}, f32[2,2,64,256]{3,2,1,0:T(8,128)S(1)}, u32[]{:S(2)}, u32[]{:S(2)}) collective-permute-start(f32[2,2,64,256]{3,2,1,0:T(8,128)} %get-tuple-element.33), channel_id=1, source_target_pairs={{16,32},{48,64},{80,96},{112,128},{144,160},{176,192},{208,224},{3... | collective-permute-start | bytes 786440 | tf_op jit(solution)/shard_map/ppermute | solution.py:281
  67.7 13.1 %collective-permute-start.13 = (f32[256,256]{1,0:T(8,128)S(1)}, f32[256,256]{1,0:T(8,128)S(1)}, u32[]{:S(2)}, u32[]{:S(2)}) collective-permute-start(f32[256,256]{1,0:T(8,128)S(1)} %bitcast.17), channel_id=1, source_target_pairs={{0,16},{16,0},{1,17},{17,1},{2,18},{18,2},{3,19},{19,3},{4,20},{20... | collective-permute-start | bytes 786440 | tf_op jit(solution)/shard_map/ppermute | solution.py:281
  71.7 10.2 %collective-permute-start.11 = (f32[2,2,64,128]{3,2,1,0:T(8,128)S(1)}, f32[2,2,64,128]{3,2,1,0:T(8,128)S(1)}, u32[]{:S(2)}, u32[]{:S(2)}) collective-permute-start(f32[2,2,64,128]{3,2,1,0:T(8,128)S(1)} %get-tuple-element.34), channel_id=1, source_target_pairs={{0,16},{32,48},{64,80},{96,112},{128,144},{160,176},{192,208},{224... | collective-permute-start | bytes 393224 | tf_op jit(solution)/shard_map/ppermute | solution.py:281
  75.8 12.3 %collective-permute-start.12 = (f32[2,2,64,128]{3,2,1,0:T(8,128)S(1)}, f32[2,2,64,128]{3,2,1,0:T(8,128)S(1)}, u32[]{:S(2)}, u32[]{:S(2)}) collective-permute-start(f32[2,2,64,128]{3,2,1,0:T(8,128)S(1)} %get-tuple-element.35), channel_id=1, source_target_pairs={{16,32},{48,64},{80,96},{112,128},{144,160},{176,192},{208,224},{3... | collective-permute-start | bytes 393224 | tf_op jit(solution)/shard_map/ppermute | solution.py:281
  78.8 1.2 %copy-start.1 = (f32[2,2,256,256]{3,2,1,0:T(8,128)S(1)}, f32[2,2,256,256]{3,2,1,0:T(8,128)}, u32[]{:S(2)}) copy-start(f32[2,2,256,256]{3,2,1,0:T(8,128)} %get-tuple-element.29.center) | copy-start | bytes 3145732
  80.0 1.0 %copy-start.6 = (f32[2,256,256]{2,1,0:T(8,128)S(1)}, f32[2,256,256]{2,1,0:T(8,128)}, u32[]{:S(2)}) copy-start(f32[2,256,256]{2,1,0:T(8,128)} %probe.1) | copy-start | bytes 1572868

commit v8 on v7

--- a/solution.py
+++ b/solution.py
@@ -289,11 +289,11 @@
     return lax.optimization_barrier((value, *others))[0]
 
 
-def scatter_sum(partial):
+def scatter_sum(partial, mark):
     plane = lax.axis_size(PLANE)
     core = lax.axis_index(PAIR)
     own, other = (lax.dynamic_index_in_dim(partial, k, 0, False) for k in (core, 1 - core))
-    part = own + exchanged(other, PAIR, 0)
+    part = own + exchanged(after(other, mark), PAIR, 0)
     return swap(part.reshape(plane, WIN // plane, WIN), PLANE)
 
 
@@ -302,8 +302,8 @@
     return swap(jnp.broadcast_to(part, (lax.axis_size(DEPTH),) + part.shape), DEPTH)
 
 
-def gather_sum(parts, last):
-    part = jnp.sum(parts, axis=0)
+def gather_sum(parts, mark, last):
+    part = jnp.sum(after(parts, mark), axis=0)
     core = lax.axis_index(PAIR)
     own = swap(jnp.broadcast_to(part, (lax.axis_size(PLANE),) + part.shape), PLANE).reshape(WIN, WIN)
     own = after(own, last)
@@ -322,10 +322,10 @@
     row_a, row_b, col_a, col_b = call(pack_sides, [strip] * 2 + [column] * 2, facts, objects, name="pack_sides")
     row_b, row_a = exchanged(row_b, ROW, 1), exchanged(row_a, ROW, 0)
     col_b, col_a = exchanged(col_b, COL, 1), exchanged(col_a, COL, 0)
-    scattered = scatter_sum(prev_partial[0, 0])
+    scattered = scatter_sum(prev_partial[0, 0], row_a)
     sent_a, sent_b = call(pack_corners, [corners] * 2, facts, row_a, row_b, name="pack_corners")
     corners_b, corners_a = exchanged(sent_b, COL, 1), exchanged(sent_a, COL, 0)
-    deep = depth_sum(scattered, col_a)
+    deep = depth_sum(scattered, sent_a)
     corners_a, deep = lax.optimization_barrier((corners_a, deep))
     center, row_a_part, row_b_part, col_a_part, col_b_part, partial = call(
         gradient,
@@ -349,7 +349,7 @@
     (added,) = call(add_sides, [tile], facts, center, col_a, col_b, row_a, row_b, name="add_sides")
     (new_objects,) = call(add_corners, [tile], facts, added, relayed_a, relayed_b, name="add_corners")
     rate = PROBE_RATE / math.sqrt(lax.axis_size(ROW) * lax.axis_size(COL))
-    total = gather_sum(deep, partial)
+    total = gather_sum(deep, partial, new_objects)
     new_probe = probe - rate * total
     return (new_objects, new_probe, partial[None, None])
 

time: 90.5 us -> 90.8 us (level)
  local copies, waits for them, and re-layouts: 5.79 us -> 4.23 us
  waiting for transfers between devices: 12.7 us -> 14.2 us
    ppermute x14, waiting for transfers between devices: 9.51 us -> 14.2 us  [exchanged(): return lax.ppermute(value, axis, pairs + [(j, i) for i, j in pairs])]
    all_to_all x3, waiting for transfers between devices: 3.14 us -> 0.01 us  [swap(): return lax.all_to_all(value, axes, 0, 0, tiled=True)]
    unnamed x24, local copies, waits for them, and re-layouts: 3.35 us -> 1.88 us
  transfers between devices with their start and end apart: 17 -> 17, of which waited for: 3 -> 4; matrix products, arithmetic and copies ran while one was open for 4% -> 3% of each run, Pallas kernels for 14% -> 4%
where the time goes in v8:
time: 90.8 us; the launch traced here: 89.5 us
  starting transfers between devices  53.1 us (58%)
  waiting for transfers between devices  14.2 us (16%)
  Pallas kernels  14 us (15%)
  local copies, waits for them, and re-layouts  4.23 us (5%)
  other arithmetic  2.41 us (3%)
  between operations  1.63 us (2%)
    ppermute x14, starting transfers between devices, exchanged(): return lax.ppermute(value, axis, pairs + [(j, i) for i, j in pairs])  37.1 us
    all_to_all x3, starting transfers between devices, swap(): return lax.all_to_all(value, axes, 0, 0, tiled=True)  16 us
    ppermute x14, waiting for transfers between devices, exchanged(): return lax.ppermute(value, axis, pairs + [(j, i) for i, j in pairs])  14.2 us
    pallas_call x6, Pallas kernels, call(): pl.pallas_call(body, out_shape=[jax.ShapeDtypeStruct(o, jnp.float32) for...  14 us
    unnamed x24, local copies, waits for them, and re-layouts  1.88 us
  transfers between devices with their start and end apart: 17, of which 4 were waited for; matrix products, arithmetic and copies ran while one was open for 3% of the time, Pallas kernels for 4%

profile of v8, /device:TPU:31, one launch (start us, length us, event | category | flops | bytes accessed | tf_op | source)
XLA Modules:
  0.0 89.5 jit_solution(3485181016481656245)
XLA Ops:
  1.3 0.7 pad_add_fusion.facts
  2.0 1.2 %copy-done = f32[2,2,256,256]{3,2,1,0:T(8,128)S(1)} copy-done((f32[2,2,256,256]{3,2,1,0:T(8,128)S(1)}, f32[2,2,256,256]{3,2,1,0:T(8,128)}, u32[]{:S(2)}) %copy-start) | copy-done | bytes 1048600
  3.3 0.8 pack_sides.1
  4.0 0.8 collective-permute-start
  4.8 1.0 %dynamic-slice_bitcast_fusion = f32[256,256]{1,0:T(8,128)S(1)} fusion(f32[1,1,2,256,256]{4,3,2,1,0:T(8,128)} %param.9, s32[]{:T(128)S(6)} %select_n.28), kind=kLoop, calls=%fused_computation.5 | loop fusion | bytes 524292 | tf_op jit(solution)/shard_map/jit(dynamic_index_in_dim)/squeeze | solution.py:295
  5.7 0.2 collective-permute-done.row_a
  5.9 0.4 collective-permute-start.5
  6.3 8.5 %collective-permute-start.1 = (f32[2,2,64,256]{3,2,1,0:T(8,128)S(1)}, f32[2,2,64,256]{3,2,1,0:T(8,128)S(1)}, u32[]{:S(2)}, u32[]{:S(2)}) collective-permute-start(f32[2,2,64,256]{3,2,1,0:T(8,128)S(1)} %get-tuple-element.24), channel_id=1, source_target_pairs={{16,32},{48,64},{80,96},{112,128},{144,160},{176,192},{208,224},{3... | collective-permute-start | bytes 786440 | tf_op jit(solution)/shard_map/ppermute | solution.py:281
  14.8 0.0 collective-permute-done.5
  14.8 0.0 copy-done.7
  14.8 0.7 bitcast_add_fusion
  15.6 6.3 %all-to-all-start = ((f32[16,16,256]{2,1,0:T(8,128)}), f32[16,16,256]{2,1,0:T(8,128)S(1)}, u32[]{:S(2)}, u32[]{:S(2)}) async-start(f32[16,16,256]{2,1,0:T(8,128)} %bitcast.6), calls=%async_computation | async-start | bytes 524288 | tf_op jit(solution)/shard_map/all_to_all | solution.py:285
  21.9 0.6 collective-permute-start.2
  22.5 3.2 %collective-permute-start.3 = (f32[2,256,128]{2,1,0:T(8,128)S(1)}, f32[2,256,128]{2,1,0:T(8,128)S(1)}, u32[]{:S(2)}, u32[]{:S(2)}) collective-permute-start(f32[2,256,128]{2,1,0:T(8,128)S(1)} %get-tuple-element.26), channel_id=1, source_target_pairs={{1,2},{3,4},{5,6},{7,8},{9,10},{11,12},{13,14},{2,1},{4,3},{6,5},{... | collective-permute-start | bytes 786440 | tf_op jit(solution)/shard_map/ppermute | solution.py:281
  25.7 0.0 collective-permute-done.1.row_b
  25.7 0.0 copy-start.3
  25.8 0.7 pack_corners.1
  26.4 0.0 copy-done.4
  26.5 0.0 all-to-all-done
  26.5 0.7 broadcast_in_dim.9
  27.2 3.6 %all-to-all-start.1 = ((f32[8,16,256]{2,1,0:T(8,128)}), f32[8,16,256]{2,1,0:T(8,128)S(1)}, u32[]{:S(2)}, u32[]{:S(2)}) async-start(f32[8,16,256]{2,1,0:T(8,128)} %broadcast_in_dim.9), calls=%async_computation.1 | async-start | bytes 262144 | tf_op jit(solution)/shard_map/all_to_all | solution.py:285
  30.7 0.2 collective-permute-start.4
  31.0 8.3 %collective-permute-start.6 = (f32[2,128,128]{2,1,0:T(8,128)S(1)}, f32[2,128,128]{2,1,0:T(8,128)S(1)}, u32[]{:S(2)}, u32[]{:S(2)}) collective-permute-start(f32[2,128,128]{2,1,0:T(8,128)S(1)} %get-tuple-element.31), channel_id=1, source_target_pairs={{1,2},{3,4},{5,6},{7,8},{9,10},{11,12},{13,14},{2,1},{4,3},{6,5},{... | collective-permute-start | bytes 393224 | tf_op jit(solution)/shard_map/ppermute | solution.py:281
  39.3 0.0 collective-permute-done.4.corners_a
  39.3 0.0 copy-start.10
  39.3 0.0 all-to-all-done.1
  39.3 0.0 collective-permute-done.2.col_a
  39.3 0.0 copy-start.8
  39.3 0.0 collective-permute-done.3.col_b
  39.3 0.0 copy-start.9
  39.3 3.7 %collective-permute-done.6.corners_b = f32[2,128,128]{2,1,0:T(8,128)S(1)} collective-permute-done((f32[2,128,128]{2,1,0:T(8,128)S(1)}, f32[2,128,128]{2,1,0:T(8,128)S(1)}, u32[]{:S(2)}, u32[]{:S(2)}) %collective-permute-start.6) | collective-permute-done | bytes 131104 | tf_op jit(solution)/shard_map/ppermute | solution.py:281
  43.0 0.0 copy-done.2
  43.0 0.0 copy-done.3
  43.0 0.0 copy-done.10
  43.0 0.0 copy-done.8
  43.0 0.0 copy-done.9
  43.0 0.6 copy-done.11
  43.6 9.6 %gradient.1 = (f32[2,2,256,256]{3,2,1,0:T(8,128)}, f32[2,2,64,256]{3,2,1,0:T(8,128)}, f32[2,2,64,256]{3,2,1,0:T(8,128)}, f32[2,384,128]{2,1,0:T(8,128)}, f32[2,384,128]{2,1,0:T(8,128)}, /*index=5*/f32[2,256,256]{2,1,0:T(8,128)}) custom-call(s32[5]{0:T(128)} %copy-done.4, f32[2,2,256,256]{3,2,1,0:T(8,128)} %objects.3, f32[2,2,64,256]{3,2,1,0:T(8,128)} %copy-done.2, ...), custom_call_target="tpu_custom_call" | custom-call | flops 3221225472 | bytes 5767168 | tf_op jit(solution)/shard_map/gradient/pallas_call | solution.py:267
  53.2 0.0 copy-start.1
  53.2 0.1 collective-permute-start.7
  53.3 4.6 %collective-permute-start.8 = (f32[2,384,128]{2,1,0:T(8,128)}, f32[2,384,128]{2,1,0:T(8,128)S(1)}, u32[]{:S(2)}, u32[]{:S(2)}) collective-permute-start(f32[2,384,128]{2,1,0:T(8,128)} %get-tuple-element.34), channel_id=1, source_target_pairs={{1,2},{3,4},{5,6},{7,8},{9,10},{11,12},{13,14},{2,1},{4,3},{6,5},{... | collective-permute-start | bytes 1179656 | tf_op jit(solution)/shard_map/ppermute | solution.py:281
  58.0 0.1 collective-permute-start.9
  58.1 7.4 %collective-permute-start.10 = (f32[2,2,64,256]{3,2,1,0:T(8,128)}, f32[2,2,64,256]{3,2,1,0:T(8,128)S(1)}, u32[]{:S(2)}, u32[]{:S(2)}) collective-permute-start(f32[2,2,64,256]{3,2,1,0:T(8,128)} %get-tuple-element.36), channel_id=1, source_target_pairs={{16,32},{48,64},{80,96},{112,128},{144,160},{176,192},{208,224},{3... | collective-permute-start | bytes 786440 | tf_op jit(solution)/shard_map/ppermute | solution.py:281
  65.5 0.7 broadcast_in_dim.10
  66.2 6.1 %all-to-all-start.2 = ((f32[16,16,256]{2,1,0:T(8,128)}), f32[16,16,256]{2,1,0:T(8,128)S(1)}, u32[]{:S(2)}, u32[]{:S(2)}) async-start(f32[16,16,256]{2,1,0:T(8,128)} %broadcast_in_dim.10), calls=%async_computation.2 | async-start | bytes 524288 | tf_op jit(solution)/shard_map/all_to_all | solution.py:285
  72.3 0.0 collective-permute-done.7.col_a
  72.3 0.0 collective-permute-done.8.col_b
  72.3 0.0 copy-done.5
  72.3 0.6 relay.1
  72.9 0.1 collective-permute-start.11
  73.0 2.8 %collective-permute-start.12 = (f32[2,2,64,128]{3,2,1,0:T(8,128)S(1)}, f32[2,2,64,128]{3,2,1,0:T(8,128)S(1)}, u32[]{:S(2)}, u32[]{:S(2)}) collective-permute-start(f32[2,2,64,128]{3,2,1,0:T(8,128)S(1)} %get-tuple-element.38), channel_id=1, source_target_pairs={{16,32},{48,64},{80,96},{112,128},{144,160},{176,192},{208,224},{3... | collective-permute-start | bytes 393224 | tf_op jit(solution)/shard_map/ppermute | solution.py:281
  75.8 0.0 collective-permute-done.9.row_a
  75.8 0.0 collective-permute-done.10.row_b
  75.8 0.0 copy-done.1
  75.8 0.8 add_sides.1.tile
  76.6 0.0 copy-start.6
  76.6 0.0 collective-permute-done.11.relayed_a
  76.6 8.8 %collective-permute-done.12.relayed_b = f32[2,2,64,128]{3,2,1,0:T(8,128)S(1)} collective-permute-done((f32[2,2,64,128]{3,2,1,0:T(8,128)S(1)}, f32[2,2,64,128]{3,2,1,0:T(8,128)S(1)}, u32[]{:S(2)}, u32[]{:S(2)}) %collective-permute-start.12) | collective-permute-done | bytes 131104 | tf_op jit(solution)/shard_map/ppermute | solution.py:281
  85.4 1.7 %add_corners.1 = f32[2,2,256,256]{3,2,1,0:T(8,128)} custom-call(s32[5]{0:T(128)S(1)} %copy-done.5, f32[2,2,256,256]{3,2,1,0:T(8,128)S(1)} %add_sides.1.tile, f32[2,2,64,128]{3,2,1,0:T(8,128)S(1)} %collective-permute-done.11.relayed_a, f32[2,2,64,128]{3,2,1,0:T(8,128)S(1)} %collective-permute-done.12.relayed_b), custom_call_target="tpu_custom_call" | custom-call | bytes 2097152 | tf_op jit(solution)/shard_map/add_corners/pallas_call | solution.py:267
  87.0 0.0 all-to-all-done.2
  87.0 0.0 collective-permute-start.13
  87.0 1.5 %collective-permute-done.13 = f32[256,256]{1,0:T(8,128)S(1)} collective-permute-done((f32[256,256]{1,0:T(8,128)S(1)}, f32[256,256]{1,0:T(8,128)S(1)}, u32[]{:S(2)}, u32[]{:S(2)}) %collective-permute-start.13) | collective-permute-done | bytes 262176 | tf_op jit(solution)/shard_map/ppermute | solution.py:281
  88.6 0.0 copy-done.6
  88.6 0.9 fusion
  (9 shorter events, 0.1 us)
Async XLA Ops:
  2.0 1.2 %copy-start = (f32[2,2,256,256]{3,2,1,0:T(8,128)S(1)}, f32[2,2,256,256]{3,2,1,0:T(8,128)}, u32[]{:S(2)}) copy-start(f32[2,2,256,256]{3,2,1,0:T(8,128)} %objects.3) | copy-start | bytes 3145732
  3.2 23.2 %copy-start.4 = (s32[5]{0:T(128)}, s32[5]{0:T(128)S(1)}, u32[]{:S(2)}) copy-start(s32[5]{0:T(128)S(1)} %pad_add_fusion.facts) | copy-start | bytes 64
  3.2 11.6 %copy-start.7 = (f32[1,1,2,256,256]{4,3,2,1,0:T(8,128)S(1)}, f32[1,1,2,256,256]{4,3,2,1,0:T(8,128)}, u32[]{:S(2)}) copy-start(f32[1,1,2,256,256]{4,3,2,1,0:T(8,128)} %param.9) | copy-start | bytes 1572868
  4.0 1.9 %collective-permute-start = (f32[2,2,64,256]{3,2,1,0:T(8,128)S(1)}, f32[2,2,64,256]{3,2,1,0:T(8,128)S(1)}, u32[]{:S(2)}, u32[]{:S(2)}) collective-permute-start(f32[2,2,64,256]{3,2,1,0:T(8,128)S(1)} %get-tuple-element.23), channel_id=1, source_target_pairs={{0,16},{32,48},{64,80},{96,112},{128,144},{160,176},{192,208},{224... | collective-permute-start | bytes 786440 | tf_op jit(solution)/shard_map/ppermute | solution.py:281
  5.9 37.1 %copy-start.2 = (f32[2,2,64,256]{3,2,1,0:T(8,128)}, f32[2,2,64,256]{3,2,1,0:T(8,128)S(1)}, u32[]{:S(2)}) copy-start(f32[2,2,64,256]{3,2,1,0:T(8,128)S(1)} %collective-permute-done.row_a) | copy-start | bytes 786436
  5.9 8.9 %collective-permute-start.5 = (f32[256,256]{1,0:T(8,128)S(1)}, f32[256,256]{1,0:T(8,128)S(1)}, u32[]{:S(2)}, u32[]{:S(2)}) collective-permute-start(f32[256,256]{1,0:T(8,128)S(1)} %dynamic-slice_bitcast_fusion), channel_id=1, source_target_pairs={{0,16},{16,0},{1,17},{17,1},{2,18},{18,2},{3,19},{19,3},{4,20},{20... | collective-permute-start | bytes 786440 | tf_op jit(solution)/shard_map/ppermute | solution.py:281
  6.3 19.4 %collective-permute-start.1 = (f32[2,2,64,256]{3,2,1,0:T(8,128)S(1)}, f32[2,2,64,256]{3,2,1,0:T(8,128)S(1)}, u32[]{:S(2)}, u32[]{:S(2)}) collective-permute-start(f32[2,2,64,256]{3,2,1,0:T(8,128)S(1)} %get-tuple-element.24), channel_id=1, source_target_pairs={{16,32},{48,64},{80,96},{112,128},{144,160},{176,192},{208,224},{3... | collective-permute-start | bytes 786440 | tf_op jit(solution)/shard_map/ppermute | solution.py:281
  15.6 10.9 %all-to-all-start = ((f32[16,16,256]{2,1,0:T(8,128)}), f32[16,16,256]{2,1,0:T(8,128)S(1)}, u32[]{:S(2)}, u32[]{:S(2)}) async-start(f32[16,16,256]{2,1,0:T(8,128)} %bitcast.6), calls=%async_computation | async-start | bytes 524288 | tf_op jit(solution)/shard_map/all_to_all | solution.py:285
  21.9 17.4 %collective-permute-start.2 = (f32[2,256,128]{2,1,0:T(8,128)S(1)}, f32[2,256,128]{2,1,0:T(8,128)S(1)}, u32[]{:S(2)}, u32[]{:S(2)}) collective-permute-start(f32[2,256,128]{2,1,0:T(8,128)S(1)} %get-tuple-element.25), channel_id=1, source_target_pairs={{0,1},{2,3},{4,5},{6,7},{8,9},{10,11},{12,13},{14,15},{1,0},{3,2},... | collective-permute-start | bytes 786440 | tf_op jit(solution)/shard_map/ppermute | solution.py:281
  22.5 16.8 %collective-permute-start.3 = (f32[2,256,128]{2,1,0:T(8,128)S(1)}, f32[2,256,128]{2,1,0:T(8,128)S(1)}, u32[]{:S(2)}, u32[]{:S(2)}) collective-permute-start(f32[2,256,128]{2,1,0:T(8,128)S(1)} %get-tuple-element.26), channel_id=1, source_target_pairs={{1,2},{3,4},{5,6},{7,8},{9,10},{11,12},{13,14},{2,1},{4,3},{6,5},{... | collective-permute-start | bytes 786440 | tf_op jit(solution)/shard_map/ppermute | solution.py:281
  25.7 17.3 %copy-start.3 = (f32[2,2,64,256]{3,2,1,0:T(8,128)}, f32[2,2,64,256]{3,2,1,0:T(8,128)S(1)}, u32[]{:S(2)}) copy-start(f32[2,2,64,256]{3,2,1,0:T(8,128)S(1)} %collective-permute-done.1.row_b) | copy-start | bytes 786436
  27.2 12.1 %all-to-all-start.1 = ((f32[8,16,256]{2,1,0:T(8,128)}), f32[8,16,256]{2,1,0:T(8,128)S(1)}, u32[]{:S(2)}, u32[]{:S(2)}) async-start(f32[8,16,256]{2,1,0:T(8,128)} %broadcast_in_dim.9), calls=%async_computation.1 | async-start | bytes 262144 | tf_op jit(solution)/shard_map/all_to_all | solution.py:285
  30.7 8.5 %collective-permute-start.4 = (f32[2,128,128]{2,1,0:T(8,128)S(1)}, f32[2,128,128]{2,1,0:T(8,128)S(1)}, u32[]{:S(2)}, u32[]{:S(2)}) collective-permute-start(f32[2,128,128]{2,1,0:T(8,128)S(1)} %get-tuple-element.27), channel_id=1, source_target_pairs={{0,1},{2,3},{4,5},{6,7},{8,9},{10,11},{12,13},{14,15},{1,0},{3,2},... | collective-permute-start | bytes 393224 | tf_op jit(solution)/shard_map/ppermute | solution.py:281
  31.0 12.0 %collective-permute-start.6 = (f32[2,128,128]{2,1,0:T(8,128)S(1)}, f32[2,128,128]{2,1,0:T(8,128)S(1)}, u32[]{:S(2)}, u32[]{:S(2)}) collective-permute-start(f32[2,128,128]{2,1,0:T(8,128)S(1)} %get-tuple-element.31), channel_id=1, source_target_pairs={{1,2},{3,4},{5,6},{7,8},{9,10},{11,12},{13,14},{2,1},{4,3},{6,5},{... | collective-permute-start | bytes 393224 | tf_op jit(solution)/shard_map/ppermute | solution.py:281
  39.3 3.7 %copy-start.10 = (f32[2,128,128]{2,1,0:T(8,128)}, f32[2,128,128]{2,1,0:T(8,128)S(1)}, u32[]{:S(2)}) copy-start(f32[2,128,128]{2,1,0:T(8,128)S(1)} %collective-permute-done.4.corners_a) | copy-start | bytes 393220
  39.3 3.7 %copy-start.8 = (f32[2,256,128]{2,1,0:T(8,128)}, f32[2,256,128]{2,1,0:T(8,128)S(1)}, u32[]{:S(2)}) copy-start(f32[2,256,128]{2,1,0:T(8,128)S(1)} %collective-permute-done.2.col_a) | copy-start | bytes 786436
  39.3 3.7 %copy-start.9 = (f32[2,256,128]{2,1,0:T(8,128)}, f32[2,256,128]{2,1,0:T(8,128)S(1)}, u32[]{:S(2)}) copy-start(f32[2,256,128]{2,1,0:T(8,128)S(1)} %collective-permute-done.3.col_b) | copy-start | bytes 786436
  43.0 0.6 copy-start.11
  43.6 28.6 %copy-start.5 = (s32[5]{0:T(128)S(1)}, s32[5]{0:T(128)}, u32[]{:S(2)}) copy-start(s32[5]{0:T(128)} %copy-done.4) | copy-start | bytes 64
  53.2 22.6 %copy-start.1 = (f32[2,2,256,256]{3,2,1,0:T(8,128)S(1)}, f32[2,2,256,256]{3,2,1,0:T(8,128)}, u32[]{:S(2)}) copy-start(f32[2,2,256,256]{3,2,1,0:T(8,128)} %get-tuple-element.32.center) | copy-start | bytes 3145732
  53.2 19.1 %collective-permute-start.7 = (f32[2,384,128]{2,1,0:T(8,128)}, f32[2,384,128]{2,1,0:T(8,128)S(1)}, u32[]{:S(2)}, u32[]{:S(2)}) collective-permute-start(f32[2,384,128]{2,1,0:T(8,128)} %get-tuple-element.33), channel_id=1, source_target_pairs={{0,1},{2,3},{4,5},{6,7},{8,9},{10,11},{12,13},{14,15},{1,0},{3,2},... | collective-permute-start | bytes 1179656 | tf_op jit(solution)/shard_map/ppermute | solution.py:281
  53.3 19.0 %collective-permute-start.8 = (f32[2,384,128]{2,1,0:T(8,128)}, f32[2,384,128]{2,1,0:T(8,128)S(1)}, u32[]{:S(2)}, u32[]{:S(2)}) collective-permute-start(f32[2,384,128]{2,1,0:T(8,128)} %get-tuple-element.34), channel_id=1, source_target_pairs={{1,2},{3,4},{5,6},{7,8},{9,10},{11,12},{13,14},{2,1},{4,3},{6,5},{... | collective-permute-start | bytes 1179656 | tf_op jit(solution)/shard_map/ppermute | solution.py:281
  58.0 17.8 %collective-permute-start.9 = (f32[2,2,64,256]{3,2,1,0:T(8,128)}, f32[2,2,64,256]{3,2,1,0:T(8,128)S(1)}, u32[]{:S(2)}, u32[]{:S(2)}) collective-permute-start(f32[2,2,64,256]{3,2,1,0:T(8,128)} %get-tuple-element.35), channel_id=1, source_target_pairs={{0,16},{32,48},{64,80},{96,112},{128,144},{160,176},{192,208},{224... | collective-permute-start | bytes 786440 | tf_op jit(solution)/shard_map/ppermute | solution.py:281
  58.1 17.7 %collective-permute-start.10 = (f32[2,2,64,256]{3,2,1,0:T(8,128)}, f32[2,2,64,256]{3,2,1,0:T(8,128)S(1)}, u32[]{:S(2)}, u32[]{:S(2)}) collective-permute-start(f32[2,2,64,256]{3,2,1,0:T(8,128)} %get-tuple-element.36), channel_id=1, source_target_pairs={{16,32},{48,64},{80,96},{112,128},{144,160},{176,192},{208,224},{3... | collective-permute-start | bytes 786440 | tf_op jit(solution)/shard_map/ppermute | solution.py:281
  66.2 20.8 %all-to-all-start.2 = ((f32[16,16,256]{2,1,0:T(8,128)}), f32[16,16,256]{2,1,0:T(8,128)S(1)}, u32[]{:S(2)}, u32[]{:S(2)}) async-start(f32[16,16,256]{2,1,0:T(8,128)} %broadcast_in_dim.10), calls=%async_computation.2 | async-start | bytes 524288 | tf_op jit(solution)/shard_map/all_to_all | solution.py:285
  72.9 3.7 %collective-permute-start.11 = (f32[2,2,64,128]{3,2,1,0:T(8,128)S(1)}, f32[2,2,64,128]{3,2,1,0:T(8,128)S(1)}, u32[]{:S(2)}, u32[]{:S(2)}) collective-permute-start(f32[2,2,64,128]{3,2,1,0:T(8,128)S(1)} %get-tuple-element.37), channel_id=1, source_target_pairs={{0,16},{32,48},{64,80},{96,112},{128,144},{160,176},{192,208},{224... | collective-permute-start | bytes 393224 | tf_op jit(solution)/shard_map/ppermute | solution.py:281
  73.0 12.4 %collective-permute-start.12 = (f32[2,2,64,128]{3,2,1,0:T(8,128)S(1)}, f32[2,2,64,128]{3,2,1,0:T(8,128)S(1)}, u32[]{:S(2)}, u32[]{:S(2)}) collective-permute-start(f32[2,2,64,128]{3,2,1,0:T(8,128)S(1)} %get-tuple-element.38), channel_id=1, source_target_pairs={{16,32},{48,64},{80,96},{112,128},{144,160},{176,192},{208,224},{3... | collective-permute-start | bytes 393224 | tf_op jit(solution)/shard_map/ppermute | solution.py:281
  76.6 12.0 %copy-start.6 = (f32[2,256,256]{2,1,0:T(8,128)S(1)}, f32[2,256,256]{2,1,0:T(8,128)}, u32[]{:S(2)}) copy-start(f32[2,256,256]{2,1,0:T(8,128)} %probe.1) | copy-start | bytes 1572868
  87.0 1.5 %collective-permute-start.13 = (f32[256,256]{1,0:T(8,128)S(1)}, f32[256,256]{1,0:T(8,128)S(1)}, u32[]{:S(2)}, u32[]{:S(2)}) collective-permute-start(f32[256,256]{1,0:T(8,128)S(1)} %bitcast.17), channel_id=1, source_target_pairs={{0,16},{16,0},{1,17},{17,1},{2,18},{18,2},{3,19},{19,3},{4,20},{20... | collective-permute-start | bytes 786440 | tf_op jit(solution)/shard_map/ppermute | solution.py:281

commit v9 on v7

--- a/solution.py
+++ b/solution.py
@@ -94,9 +94,16 @@
     return jnp.where(flag == 0, when_even, when_odd)
 
 
-def pack_sides(facts, objects, row_a, row_b, col_a, col_b):
-    row_odd, col_odd = facts[3], facts[4]
-    for s in range(2):
+def pack_sides(facts, source, row_a, row_b, col_a, col_b, objects, arrive):
+    row_odd, col_odd = facts[3], facts[4]
+    copies = [
+        pltpu.make_async_copy(source.at[s, k], objects.at[s, k], arrive.at[s, k]) for s in range(2) for k in range(2)
+    ]
+    for copy in copies:
+        copy.start()
+    for s in range(2):
+        for copy in copies[2 * s : 2 * s + 2]:
+            copy.wait()
         top, bottom = objects[s, :, :HALO], objects[s, :, TILE - HALO :]
         row_a[s] = either(row_odd, bottom, top)
         row_b[s] = either(row_odd, top, bottom)
@@ -262,12 +269,12 @@
                 new_objects[s, k, TILE - HALO :, cols] = tile[s, k, TILE - HALO :, cols] + either(row_odd, first, last)
 
 
-def call(body, outs, *args, specs=None, scratch=(), flops=0, limit=2, name=None):
+def call(body, outs, *args, specs=None, inputs=None, scratch=(), flops=0, limit=2, name=None):
     moved = sum(math.prod(o) * 4 for o in outs)
     return pl.pallas_call(
         body,
         out_shape=[jax.ShapeDtypeStruct(o, jnp.float32) for o in outs],
-        in_specs=[SMEM] + (specs or [VMEM] * (len(args) - 1)),
+        in_specs=[SMEM] + (specs or inputs or [VMEM] * (len(args) - 1)),
         out_specs=[HBM if specs else VMEM] * len(outs),
         scratch_shapes=scratch,
         compiler_params=pltpu.CompilerParams(vmem_limit_bytes=limit * MIB),
@@ -319,7 +326,15 @@
         offsets.reshape(2), counts.reshape(1),
         jnp.stack([lax.axis_index("row_2"), lax.axis_index("col_1") % 2]).astype(jnp.int32),
     ])
-    row_a, row_b, col_a, col_b = call(pack_sides, [strip] * 2 + [column] * 2, facts, objects, name="pack_sides")
+    row_a, row_b, col_a, col_b = call(
+        pack_sides,
+        [strip] * 2 + [column] * 2,
+        facts, objects,
+        inputs=[HBM],
+        scratch=[pltpu.VMEM(tile, jnp.float32), pltpu.SemaphoreType.DMA((2, 2))],
+        limit=60,
+        name="pack_sides",
+    )
     row_b, row_a = exchanged(row_b, ROW, 1), exchanged(row_a, ROW, 0)
     col_b, col_a = exchanged(col_b, COL, 1), exchanged(col_a, COL, 0)
     scattered = scatter_sum(prev_partial[0, 0])

time: 90.5 us -> 92.3 us (1.020)
  Pallas kernels: 14 us -> 16.2 us
  local copies, waits for them, and re-layouts: 5.79 us -> 4.57 us
    pallas_call x6, Pallas kernels: 14 us -> 16.2 us  [call(): pl.pallas_call(body, out_shape=[jax.ShapeDtypeStruct(o, jnp.float32) for...]
    unnamed x24 -> x22, local copies, waits for them, and re-layouts: 3.35 us -> 2.13 us
  transfers between devices with their start and end apart: 17 -> 17, of which waited for: 3 -> 3; matrix products, arithmetic and copies ran while one was open for 4% -> 5% of each run, Pallas kernels for 14% -> 16%
where the time goes in v9:
time: 92.3 us; the launch traced here: 91.3 us
  starting transfers between devices  53.7 us (58%)
  Pallas kernels  16.2 us (18%)
  waiting for transfers between devices  12.2 us (13%)
  local copies, waits for them, and re-layouts  4.57 us (5%)
  other arithmetic  2.94 us (3%)
  between operations  1.62 us (2%)
    ppermute x14, starting transfers between devices, exchanged(): return lax.ppermute(value, axis, pairs + [(j, i) for i, j in pairs])  37.1 us
    all_to_all x3, starting transfers between devices, swap(): return lax.all_to_all(value, axes, 0, 0, tiled=True)  16.6 us
    pallas_call x6, Pallas kernels, call(): pl.pallas_call(body, out_shape=[jax.ShapeDtypeStruct(o, jnp.float32) for...  16.2 us
    ppermute x14, waiting for transfers between devices, exchanged(): return lax.ppermute(value, axis, pairs + [(j, i) for i, j in pairs])  9 us
    all_to_all x3, waiting for transfers between devices, swap(): return lax.all_to_all(value, axes, 0, 0, tiled=True)  3.21 us
    unnamed x22, local copies, waits for them, and re-layouts  2.13 us
  transfers between devices with their start and end apart: 17, of which 3 were waited for; matrix products, arithmetic and copies ran while one was open for 5% of the time, Pallas kernels for 16%

profile of v9, /device:TPU:31, one launch (start us, length us, event | category | flops | bytes accessed | tf_op | source)
XLA Modules:
  0.0 91.3 jit_solution(2223578015907263936)
XLA Ops:
  0.6 0.0 copy-start.6
  0.6 1.0 %dynamic-slice_bitcast_fusion = f32[256,256]{1,0:T(8,128)S(1)} fusion(f32[1,1,2,256,256]{4,3,2,1,0:T(8,128)} %param.9, s32[]{:T(128)S(6)} %select_n.28), kind=kLoop, calls=%fused_computation.5 | loop fusion | bytes 524292 | tf_op jit(solution)/shard_map/jit(dynamic_index_in_dim)/squeeze | solution.py:302
  1.7 0.8 collective-permute-start.5
  3.1 1.3 %pad_add_fusion.facts = s32[5]{0:T(128)} fusion(s32[1]{0:T(128)} %bitcast.3, s32[1]{0:T(128)} %bitcast.2, s32[1]{0:T(128)} %bitcast.16, s32[2]{0:T(128)} %bitcast.19), kind=kLoop, calls=%fused_computation.6 | loop fusion | flops 15 | bytes 40 | tf_op jit(solution)/shard_map/concatenate | solution.py:325
  4.3 3.0 %pack_sides.1 = (f32[2,2,64,256]{3,2,1,0:T(8,128)}, f32[2,2,64,256]{3,2,1,0:T(8,128)}, f32[2,256,128]{2,1,0:T(8,128)}, f32[2,256,128]{2,1,0:T(8,128)}) custom-call(s32[5]{0:T(128)} %pad_add_fusion.facts, f32[2,2,256,256]{3,2,1,0:T(8,128)} %objects.1), custom_call_target="tpu_custom_call" | custom-call | bytes 2097152 | tf_op jit(solution)/shard_map/pack_sides/pallas_call | solution.py:274
  7.3 0.6 collective-permute-start.2
  8.0 0.0 collective-permute-done.5
  8.0 0.0 copy-done.6
  8.0 0.8 bitcast_add_fusion
  8.7 6.9 %all-to-all-start = ((f32[16,16,256]{2,1,0:T(8,128)}), f32[16,16,256]{2,1,0:T(8,128)S(1)}, u32[]{:S(2)}, u32[]{:S(2)}) async-start(f32[16,16,256]{2,1,0:T(8,128)} %bitcast.6), calls=%async_computation | async-start | bytes 524288 | tf_op jit(solution)/shard_map/all_to_all | solution.py:292
  15.6 0.9 collective-permute-start
  16.5 8.7 %collective-permute-start.1 = (f32[2,2,64,256]{3,2,1,0:T(8,128)}, f32[2,2,64,256]{3,2,1,0:T(8,128)S(1)}, u32[]{:S(2)}, u32[]{:S(2)}) collective-permute-start(f32[2,2,64,256]{3,2,1,0:T(8,128)} %get-tuple-element.22), channel_id=1, source_target_pairs={{16,32},{48,64},{80,96},{112,128},{144,160},{176,192},{208,224},{3... | collective-permute-start | bytes 786440 | tf_op jit(solution)/shard_map/ppermute | solution.py:288
  25.2 2.3 %collective-permute-start.3 = (f32[2,256,128]{2,1,0:T(8,128)}, f32[2,256,128]{2,1,0:T(8,128)S(1)}, u32[]{:S(2)}, u32[]{:S(2)}) collective-permute-start(f32[2,256,128]{2,1,0:T(8,128)} %get-tuple-element.24), channel_id=1, source_target_pairs={{1,2},{3,4},{5,6},{7,8},{9,10},{11,12},{13,14},{2,1},{4,3},{6,5},{... | collective-permute-start | bytes 786440 | tf_op jit(solution)/shard_map/ppermute | solution.py:288
  27.5 0.0 collective-permute-done.2.col_a
  27.5 0.0 copy-start.7
  27.5 0.0 all-to-all-done
  27.5 0.7 broadcast_in_dim.9
  28.2 3.4 %all-to-all-start.1 = ((f32[8,16,256]{2,1,0:T(8,128)}), f32[8,16,256]{2,1,0:T(8,128)S(1)}, u32[]{:S(2)}, u32[]{:S(2)}) async-start(f32[8,16,256]{2,1,0:T(8,128)} %broadcast_in_dim.9), calls=%async_computation.1 | async-start | bytes 262144 | tf_op jit(solution)/shard_map/all_to_all | solution.py:292
  31.6 0.0 collective-permute-done.row_a
  31.6 0.0 copy-start.1
  31.6 0.0 collective-permute-done.1.row_b
  31.6 0.0 copy-done.3
  31.7 0.0 copy-start.2
  31.7 0.7 pack_corners.1
  32.4 0.6 collective-permute-start.4
  32.9 4.9 %collective-permute-start.6 = (f32[2,128,128]{2,1,0:T(8,128)S(1)}, f32[2,128,128]{2,1,0:T(8,128)S(1)}, u32[]{:S(2)}, u32[]{:S(2)}) collective-permute-start(f32[2,128,128]{2,1,0:T(8,128)S(1)} %get-tuple-element.28), channel_id=1, source_target_pairs={{1,2},{3,4},{5,6},{7,8},{9,10},{11,12},{13,14},{2,1},{4,3},{6,5},{... | collective-permute-start | bytes 393224 | tf_op jit(solution)/shard_map/ppermute | solution.py:288
  37.8 0.0 collective-permute-done.4.corners_a
  37.8 0.0 copy-start.9
  37.9 3.2 %all-to-all-done.1 = f32[8,16,256]{2,1,0:T(8,128)S(1)} async-done(((f32[8,16,256]{2,1,0:T(8,128)}), f32[8,16,256]{2,1,0:T(8,128)S(1)}, u32[]{:S(2)}, u32[]{:S(2)}) %all-to-all-start.1) | async-done | bytes 131104 | tf_op jit(solution)/shard_map/all_to_all | solution.py:292
  41.1 0.7 broadcast_in_dim.10
  41.8 6.3 %all-to-all-start.2 = ((f32[16,16,256]{2,1,0:T(8,128)}), f32[16,16,256]{2,1,0:T(8,128)S(1)}, u32[]{:S(2)}, u32[]{:S(2)}) async-start(f32[16,16,256]{2,1,0:T(8,128)} %broadcast_in_dim.10), calls=%async_computation.2 | async-start | bytes 524288 | tf_op jit(solution)/shard_map/all_to_all | solution.py:292
  48.1 0.0 collective-permute-done.3.col_b
  48.2 0.0 copy-start.8
  48.2 0.0 collective-permute-done.6.corners_b
  48.2 0.0 copy-start.10
  48.2 0.0 copy-done.7
  48.2 0.0 copy-done.1
  48.2 0.0 copy-done.2
  48.2 0.0 copy-done.9
  48.2 0.6 copy-done.8
  48.9 0.0 copy-done.10
  48.9 9.5 %gradient.1 = (f32[2,2,256,256]{3,2,1,0:T(8,128)}, f32[2,2,64,256]{3,2,1,0:T(8,128)}, f32[2,2,64,256]{3,2,1,0:T(8,128)}, f32[2,384,128]{2,1,0:T(8,128)}, f32[2,384,128]{2,1,0:T(8,128)}, /*index=5*/f32[2,256,256]{2,1,0:T(8,128)}) custom-call(s32[5]{0:T(128)} %pad_add_fusion.facts, f32[2,2,256,256]{3,2,1,0:T(8,128)} %objects.1, f32[2,2,64,256]{3,2,1,0:T(8,128)} %copy-done.1, ...), custom_call_target="tpu_custom_call" | custom-call | flops 3221225472 | bytes 5767168 | tf_op jit(solution)/shard_map/gradient/pallas_call | solution.py:274
  58.4 0.7 collective-permute-start.7
  59.1 2.6 %collective-permute-start.8 = (f32[2,384,128]{2,1,0:T(8,128)}, f32[2,384,128]{2,1,0:T(8,128)S(1)}, u32[]{:S(2)}, u32[]{:S(2)}) collective-permute-start(f32[2,384,128]{2,1,0:T(8,128)} %get-tuple-element.31), channel_id=1, source_target_pairs={{1,2},{3,4},{5,6},{7,8},{9,10},{11,12},{13,14},{2,1},{4,3},{6,5},{... | collective-permute-start | bytes 1179656 | tf_op jit(solution)/shard_map/ppermute | solution.py:288
  61.7 1.8 %collective-permute-start.9 = (f32[2,2,64,256]{3,2,1,0:T(8,128)}, f32[2,2,64,256]{3,2,1,0:T(8,128)S(1)}, u32[]{:S(2)}, u32[]{:S(2)}) collective-permute-start(f32[2,2,64,256]{3,2,1,0:T(8,128)} %get-tuple-element.32), channel_id=1, source_target_pairs={{0,16},{32,48},{64,80},{96,112},{128,144},{160,176},{192,208},{224... | collective-permute-start | bytes 786440 | tf_op jit(solution)/shard_map/ppermute | solution.py:288
  63.6 5.9 %collective-permute-start.10 = (f32[2,2,64,256]{3,2,1,0:T(8,128)}, f32[2,2,64,256]{3,2,1,0:T(8,128)S(1)}, u32[]{:S(2)}, u32[]{:S(2)}) collective-permute-start(f32[2,2,64,256]{3,2,1,0:T(8,128)} %get-tuple-element.33), channel_id=1, source_target_pairs={{16,32},{48,64},{80,96},{112,128},{144,160},{176,192},{208,224},{3... | collective-permute-start | bytes 786440 | tf_op jit(solution)/shard_map/ppermute | solution.py:288
  69.5 0.0 all-to-all-done.2
  69.5 0.1 collective-permute-start.13
  69.6 0.0 collective-permute-done.7.col_a
  69.6 3.0 %collective-permute-done.8.col_b = f32[2,384,128]{2,1,0:T(8,128)S(1)} collective-permute-done((f32[2,384,128]{2,1,0:T(8,128)}, f32[2,384,128]{2,1,0:T(8,128)S(1)}, u32[]{:S(2)}, u32[]{:S(2)}) %collective-permute-start.8) | collective-permute-done | bytes 393248 | tf_op jit(solution)/shard_map/ppermute | solution.py:288
  72.6 0.6 relay.1
  73.2 4.2 %collective-permute-start.11 = (f32[2,2,64,128]{3,2,1,0:T(8,128)S(1)}, f32[2,2,64,128]{3,2,1,0:T(8,128)S(1)}, u32[]{:S(2)}, u32[]{:S(2)}) collective-permute-start(f32[2,2,64,128]{3,2,1,0:T(8,128)S(1)} %get-tuple-element.34), channel_id=1, source_target_pairs={{0,16},{32,48},{64,80},{96,112},{128,144},{160,176},{192,208},{224... | collective-permute-start | bytes 393224 | tf_op jit(solution)/shard_map/ppermute | solution.py:288
  77.3 3.2 %collective-permute-start.12 = (f32[2,2,64,128]{3,2,1,0:T(8,128)S(1)}, f32[2,2,64,128]{3,2,1,0:T(8,128)S(1)}, u32[]{:S(2)}, u32[]{:S(2)}) collective-permute-start(f32[2,2,64,128]{3,2,1,0:T(8,128)S(1)} %get-tuple-element.35), channel_id=1, source_target_pairs={{16,32},{48,64},{80,96},{112,128},{144,160},{176,192},{208,224},{3... | collective-permute-start | bytes 393224 | tf_op jit(solution)/shard_map/ppermute | solution.py:288
  80.5 0.0 collective-permute-done.9.row_a
  80.5 0.0 collective-permute-done.10.row_b
  80.5 0.0 copy-start
  80.5 1.2 %copy-done = f32[2,2,256,256]{3,2,1,0:T(8,128)S(1)} copy-done((f32[2,2,256,256]{3,2,1,0:T(8,128)S(1)}, f32[2,2,256,256]{3,2,1,0:T(8,128)}, u32[]{:S(2)}) %copy-start) | copy-done | bytes 1048600
  81.8 0.8 add_sides.1.tile
  82.6 0.0 collective-permute-done.13
  82.6 0.2 copy-done.5
  82.8 0.9 fusion
  83.7 0.0 collective-permute-done.11.relayed_a
  83.7 6.0 %collective-permute-done.12.relayed_b = f32[2,2,64,128]{3,2,1,0:T(8,128)S(1)} collective-permute-done((f32[2,2,64,128]{3,2,1,0:T(8,128)S(1)}, f32[2,2,64,128]{3,2,1,0:T(8,128)S(1)}, u32[]{:S(2)}, u32[]{:S(2)}) %collective-permute-start.12) | collective-permute-done | bytes 131104 | tf_op jit(solution)/shard_map/ppermute | solution.py:288
  89.6 1.7 %add_corners.1 = f32[2,2,256,256]{3,2,1,0:T(8,128)} custom-call(s32[5]{0:T(128)S(1)} %copy-done.4, f32[2,2,256,256]{3,2,1,0:T(8,128)S(1)} %add_sides.1.tile, f32[2,2,64,128]{3,2,1,0:T(8,128)S(1)} %collective-permute-done.11.relayed_a, f32[2,2,64,128]{3,2,1,0:T(8,128)S(1)} %collective-permute-done.12.relayed_b), custom_call_target="tpu_custom_call" | custom-call | bytes 2097152 | tf_op jit(solution)/shard_map/add_corners/pallas_call | solution.py:274
  (7 shorter events, 0.1 us)
Async XLA Ops:
  0.6 7.4 %copy-start.6 = (f32[1,1,2,256,256]{4,3,2,1,0:T(8,128)S(1)}, f32[1,1,2,256,256]{4,3,2,1,0:T(8,128)}, u32[]{:S(2)}) copy-start(f32[1,1,2,256,256]{4,3,2,1,0:T(8,128)} %param.9) | copy-start | bytes 1572868
  1.7 6.3 %collective-permute-start.5 = (f32[256,256]{1,0:T(8,128)S(1)}, f32[256,256]{1,0:T(8,128)S(1)}, u32[]{:S(2)}, u32[]{:S(2)}) collective-permute-start(f32[256,256]{1,0:T(8,128)S(1)} %dynamic-slice_bitcast_fusion), channel_id=1, source_target_pairs={{0,16},{16,0},{1,17},{17,1},{2,18},{18,2},{3,19},{19,3},{4,20},{20... | collective-permute-start | bytes 786440 | tf_op jit(solution)/shard_map/ppermute | solution.py:288
  4.3 27.3 %copy-start.3 = (s32[5]{0:T(128)S(1)}, s32[5]{0:T(128)}, u32[]{:S(2)}) copy-start(s32[5]{0:T(128)} %pad_add_fusion.facts) | copy-start | bytes 64
  7.3 20.1 %collective-permute-start.2 = (f32[2,256,128]{2,1,0:T(8,128)}, f32[2,256,128]{2,1,0:T(8,128)S(1)}, u32[]{:S(2)}, u32[]{:S(2)}) collective-permute-start(f32[2,256,128]{2,1,0:T(8,128)} %get-tuple-element.23), channel_id=1, source_target_pairs={{0,1},{2,3},{4,5},{6,7},{8,9},{10,11},{12,13},{14,15},{1,0},{3,2},... | collective-permute-start | bytes 786440 | tf_op jit(solution)/shard_map/ppermute | solution.py:288
  8.7 18.8 %all-to-all-start = ((f32[16,16,256]{2,1,0:T(8,128)}), f32[16,16,256]{2,1,0:T(8,128)S(1)}, u32[]{:S(2)}, u32[]{:S(2)}) async-start(f32[16,16,256]{2,1,0:T(8,128)} %bitcast.6), calls=%async_computation | async-start | bytes 524288 | tf_op jit(solution)/shard_map/all_to_all | solution.py:292
  15.6 16.0 %collective-permute-start = (f32[2,2,64,256]{3,2,1,0:T(8,128)}, f32[2,2,64,256]{3,2,1,0:T(8,128)S(1)}, u32[]{:S(2)}, u32[]{:S(2)}) collective-permute-start(f32[2,2,64,256]{3,2,1,0:T(8,128)} %get-tuple-element.21), channel_id=1, source_target_pairs={{0,16},{32,48},{64,80},{96,112},{128,144},{160,176},{192,208},{224... | collective-permute-start | bytes 786440 | tf_op jit(solution)/shard_map/ppermute | solution.py:288
  16.5 15.1 %collective-permute-start.1 = (f32[2,2,64,256]{3,2,1,0:T(8,128)}, f32[2,2,64,256]{3,2,1,0:T(8,128)S(1)}, u32[]{:S(2)}, u32[]{:S(2)}) collective-permute-start(f32[2,2,64,256]{3,2,1,0:T(8,128)} %get-tuple-element.22), channel_id=1, source_target_pairs={{16,32},{48,64},{80,96},{112,128},{144,160},{176,192},{208,224},{3... | collective-permute-start | bytes 786440 | tf_op jit(solution)/shard_map/ppermute | solution.py:288
  25.2 22.9 %collective-permute-start.3 = (f32[2,256,128]{2,1,0:T(8,128)}, f32[2,256,128]{2,1,0:T(8,128)S(1)}, u32[]{:S(2)}, u32[]{:S(2)}) collective-permute-start(f32[2,256,128]{2,1,0:T(8,128)} %get-tuple-element.24), channel_id=1, source_target_pairs={{1,2},{3,4},{5,6},{7,8},{9,10},{11,12},{13,14},{2,1},{4,3},{6,5},{... | collective-permute-start | bytes 786440 | tf_op jit(solution)/shard_map/ppermute | solution.py:288
  27.5 20.7 %copy-start.7 = (f32[2,256,128]{2,1,0:T(8,128)}, f32[2,256,128]{2,1,0:T(8,128)S(1)}, u32[]{:S(2)}) copy-start(f32[2,256,128]{2,1,0:T(8,128)S(1)} %collective-permute-done.2.col_a) | copy-start | bytes 786436
  28.2 12.8 %all-to-all-start.1 = ((f32[8,16,256]{2,1,0:T(8,128)}), f32[8,16,256]{2,1,0:T(8,128)S(1)}, u32[]{:S(2)}, u32[]{:S(2)}) async-start(f32[8,16,256]{2,1,0:T(8,128)} %broadcast_in_dim.9), calls=%async_computation.1 | async-start | bytes 262144 | tf_op jit(solution)/shard_map/all_to_all | solution.py:292
  31.6 16.6 %copy-start.1 = (f32[2,2,64,256]{3,2,1,0:T(8,128)}, f32[2,2,64,256]{3,2,1,0:T(8,128)S(1)}, u32[]{:S(2)}) copy-start(f32[2,2,64,256]{3,2,1,0:T(8,128)S(1)} %collective-permute-done.row_a) | copy-start | bytes 786436
  31.7 16.5 %copy-start.2 = (f32[2,2,64,256]{3,2,1,0:T(8,128)}, f32[2,2,64,256]{3,2,1,0:T(8,128)S(1)}, u32[]{:S(2)}) copy-start(f32[2,2,64,256]{3,2,1,0:T(8,128)S(1)} %collective-permute-done.1.row_b) | copy-start | bytes 786436
  32.4 5.5 %collective-permute-start.4 = (f32[2,128,128]{2,1,0:T(8,128)S(1)}, f32[2,128,128]{2,1,0:T(8,128)S(1)}, u32[]{:S(2)}, u32[]{:S(2)}) collective-permute-start(f32[2,128,128]{2,1,0:T(8,128)S(1)} %get-tuple-element.25), channel_id=1, source_target_pairs={{0,1},{2,3},{4,5},{6,7},{8,9},{10,11},{12,13},{14,15},{1,0},{3,2},... | collective-permute-start | bytes 393224 | tf_op jit(solution)/shard_map/ppermute | solution.py:288
  32.9 15.2 %collective-permute-start.6 = (f32[2,128,128]{2,1,0:T(8,128)S(1)}, f32[2,128,128]{2,1,0:T(8,128)S(1)}, u32[]{:S(2)}, u32[]{:S(2)}) collective-permute-start(f32[2,128,128]{2,1,0:T(8,128)S(1)} %get-tuple-element.28), channel_id=1, source_target_pairs={{1,2},{3,4},{5,6},{7,8},{9,10},{11,12},{13,14},{2,1},{4,3},{6,5},{... | collective-permute-start | bytes 393224 | tf_op jit(solution)/shard_map/ppermute | solution.py:288
  37.8 10.4 %copy-start.9 = (f32[2,128,128]{2,1,0:T(8,128)}, f32[2,128,128]{2,1,0:T(8,128)S(1)}, u32[]{:S(2)}) copy-start(f32[2,128,128]{2,1,0:T(8,128)S(1)} %collective-permute-done.4.corners_a) | copy-start | bytes 393220
  41.8 27.7 %all-to-all-start.2 = ((f32[16,16,256]{2,1,0:T(8,128)}), f32[16,16,256]{2,1,0:T(8,128)S(1)}, u32[]{:S(2)}, u32[]{:S(2)}) async-start(f32[16,16,256]{2,1,0:T(8,128)} %broadcast_in_dim.10), calls=%async_computation.2 | async-start | bytes 524288 | tf_op jit(solution)/shard_map/all_to_all | solution.py:292
  48.2 0.7 copy-start.8
  48.2 0.7 copy-start.10
  48.9 23.7 %copy-start.4 = (s32[5]{0:T(128)S(1)}, s32[5]{0:T(128)}, u32[]{:S(2)}) copy-start(s32[5]{0:T(128)} %pad_add_fusion.facts) | copy-start | bytes 64
  58.4 11.1 %collective-permute-start.7 = (f32[2,384,128]{2,1,0:T(8,128)}, f32[2,384,128]{2,1,0:T(8,128)S(1)}, u32[]{:S(2)}, u32[]{:S(2)}) collective-permute-start(f32[2,384,128]{2,1,0:T(8,128)} %get-tuple-element.30), channel_id=1, source_target_pairs={{0,1},{2,3},{4,5},{6,7},{8,9},{10,11},{12,13},{14,15},{1,0},{3,2},... | collective-permute-start | bytes 1179656 | tf_op jit(solution)/shard_map/ppermute | solution.py:288
  59.1 13.5 %collective-permute-start.8 = (f32[2,384,128]{2,1,0:T(8,128)}, f32[2,384,128]{2,1,0:T(8,128)S(1)}, u32[]{:S(2)}, u32[]{:S(2)}) collective-permute-start(f32[2,384,128]{2,1,0:T(8,128)} %get-tuple-element.31), channel_id=1, source_target_pairs={{1,2},{3,4},{5,6},{7,8},{9,10},{11,12},{13,14},{2,1},{4,3},{6,5},{... | collective-permute-start | bytes 1179656 | tf_op jit(solution)/shard_map/ppermute | solution.py:288
  61.7 18.8 %collective-permute-start.9 = (f32[2,2,64,256]{3,2,1,0:T(8,128)}, f32[2,2,64,256]{3,2,1,0:T(8,128)S(1)}, u32[]{:S(2)}, u32[]{:S(2)}) collective-permute-start(f32[2,2,64,256]{3,2,1,0:T(8,128)} %get-tuple-element.32), channel_id=1, source_target_pairs={{0,16},{32,48},{64,80},{96,112},{128,144},{160,176},{192,208},{224... | collective-permute-start | bytes 786440 | tf_op jit(solution)/shard_map/ppermute | solution.py:288
  63.6 17.0 %collective-permute-start.10 = (f32[2,2,64,256]{3,2,1,0:T(8,128)}, f32[2,2,64,256]{3,2,1,0:T(8,128)S(1)}, u32[]{:S(2)}, u32[]{:S(2)}) collective-permute-start(f32[2,2,64,256]{3,2,1,0:T(8,128)} %get-tuple-element.33), channel_id=1, source_target_pairs={{16,32},{48,64},{80,96},{112,128},{144,160},{176,192},{208,224},{3... | collective-permute-start | bytes 786440 | tf_op jit(solution)/shard_map/ppermute | solution.py:288
  69.5 13.1 %collective-permute-start.13 = (f32[256,256]{1,0:T(8,128)S(1)}, f32[256,256]{1,0:T(8,128)S(1)}, u32[]{:S(2)}, u32[]{:S(2)}) collective-permute-start(f32[256,256]{1,0:T(8,128)S(1)} %bitcast.17), channel_id=1, source_target_pairs={{0,16},{16,0},{1,17},{17,1},{2,18},{18,2},{3,19},{19,3},{4,20},{20... | collective-permute-start | bytes 786440 | tf_op jit(solution)/shard_map/ppermute | solution.py:288
  73.2 10.5 %collective-permute-start.11 = (f32[2,2,64,128]{3,2,1,0:T(8,128)S(1)}, f32[2,2,64,128]{3,2,1,0:T(8,128)S(1)}, u32[]{:S(2)}, u32[]{:S(2)}) collective-permute-start(f32[2,2,64,128]{3,2,1,0:T(8,128)S(1)} %get-tuple-element.34), channel_id=1, source_target_pairs={{0,16},{32,48},{64,80},{96,112},{128,144},{160,176},{192,208},{224... | collective-permute-start | bytes 393224 | tf_op jit(solution)/shard_map/ppermute | solution.py:288
  77.3 12.3 %collective-permute-start.12 = (f32[2,2,64,128]{3,2,1,0:T(8,128)S(1)}, f32[2,2,64,128]{3,2,1,0:T(8,128)S(1)}, u32[]{:S(2)}, u32[]{:S(2)}) collective-permute-start(f32[2,2,64,128]{3,2,1,0:T(8,128)S(1)} %get-tuple-element.35), channel_id=1, source_target_pairs={{16,32},{48,64},{80,96},{112,128},{144,160},{176,192},{208,224},{3... | collective-permute-start | bytes 393224 | tf_op jit(solution)/shard_map/ppermute | solution.py:288
  80.5 1.2 %copy-start = (f32[2,2,256,256]{3,2,1,0:T(8,128)S(1)}, f32[2,2,256,256]{3,2,1,0:T(8,128)}, u32[]{:S(2)}) copy-start(f32[2,2,256,256]{3,2,1,0:T(8,128)} %get-tuple-element.29.center) | copy-start | bytes 3145732
  81.8 1.0 %copy-start.5 = (f32[2,256,256]{2,1,0:T(8,128)S(1)}, f32[2,256,256]{2,1,0:T(8,128)}, u32[]{:S(2)}) copy-start(f32[2,256,256]{2,1,0:T(8,128)} %probe.1) | copy-start | bytes 1572868
